TPU v7x, 128 devices: a whole 4x4x4 slice. The times are simulated.
128 devices in a mesh: node: 16 (over x, z), local: 8 (over y, core).
Axes of the slice: x: 4, y: 4, z: 4, core: 2. Of those that a mesh axis runs over, the one named last changes fastest.
Arguments:
- hidden_states: bfloat16 [1536, 7168], P('node', 'local'), may hold values from -6 to 6
- routes: int32 [1536, 4], P('node'), may hold values from 0 to 15, all different within a row; in each aligned block of 96 rows (0 to 95, 96 to 191, ...) at most 36 rows name the same one
- route_weights: float32 [1536, 4], P('node'), may hold values from 0.05 to 0.6
- w_gate: bfloat16 [16, 7168, 2048], P('node', None, 'local'), may hold values from -0.0625 to 0.0625
- w_up: bfloat16 [16, 7168, 2048], P('node', None, 'local'), may hold values from -0.0625 to 0.0625
- w_down: bfloat16 [16, 2048, 7168], P('node', 'local'), may hold values from -0.1875 to 0.1875
- norm_gain: float32 [7168], P('local'), may hold values from 0.1 to 1.9
- head_weight: bfloat16 [65536, 7168], P(('node', 'local')), may hold values from -4 to 4
- targets: int32 [1536], replicated, may hold values from 0 to 65535
- policy_logp: float32 [1536], replicated, may hold values from -20 to -11
Outputs:
- layer_out: bfloat16 [1536, 7168], P('node', 'local')
- ref_logp: float32 [1536], replicated
- kl: float32 [1536], replicated
Inputs may be any that keep to these rules, and one draw needn't show every extreme that they name: `routes`: in each aligned block of 96 rows no expert is named more than 36 times, a bound that some block reaches; a row names 4 different experts.
All inputs are finite; a program needn't handle non-finite values.
Results may differ from a plain program's by a relative error of at most 0.015.
Values may be sent and summed in bfloat16 or wider, within the bound.
No kernel may reach another device: no remote copies, remote signals or barrier semaphores. Data moves between devices by JAX's collectives and lax.ppermute only.
A program may use at most 128 MiB of HBM per device.

v0:
```python
import jax
import jax.numpy as jnp
from jax import lax
from jax.sharding import PartitionSpec as P


def vocab_stats(logits, wanted, first_id):
    ids = first_id + jnp.arange(logits.shape[1], dtype=jnp.int32)
    peak = jnp.max(logits, axis=1)
    exp_total = jnp.sum(jnp.exp(logits - peak[:, None]), axis=1)
    target_logit = jnp.sum(jnp.where(ids[None, :] == wanted[:, None], logits, 0.0), axis=1)
    return (peak, exp_total, target_logit)


def shards(
    hidden_states,
    routes,
    route_weights,
    w_gate,
    w_up,
    w_down,
    norm_gain,
    head_weight,
    targets,
    policy_logp,
):
    n_node = lax.axis_size("node")
    tok_rows, part_width = hidden_states.shape
    top_count = routes.shape[1]
    capacity = 3 * tok_rows * top_count // (2 * n_node)
    flat_routes = routes.reshape(-1)
    onehot = (flat_routes[:, None] == jnp.arange(n_node, dtype=jnp.int32)[None, :]).astype(
        jnp.int32
    )
    earlier = jnp.cumsum(onehot, axis=0) - onehot
    slot_index = jnp.sum(earlier * onehot, axis=1)
    target_rows = flat_routes * capacity + slot_index
    columns = jnp.arange(n_node * capacity, dtype=jnp.int32)
    placement_map = (target_rows[:, None] == columns[None, :]).reshape(tok_rows, top_count, -1)
    dispatch_mat = jnp.any(placement_map, axis=1).T.astype(jnp.bfloat16)
    send_rows = jnp.dot(dispatch_mat, hidden_states, preferred_element_type=jnp.float32).astype(
        jnp.bfloat16
    )
    arrived = lax.all_to_all(send_rows, "node", split_axis=0, concat_axis=0, tiled=True)
    gate_mat = w_gate[0]
    up_mat = w_up[0]
    block_rows = lax.all_gather(arrived, "local", axis=1, tiled=True)
    gate_pre = jnp.dot(block_rows, gate_mat, preferred_element_type=jnp.float32)
    up_pre = jnp.dot(block_rows, up_mat, preferred_element_type=jnp.float32)
    activated = (jax.nn.silu(gate_pre) * up_pre).astype(jnp.bfloat16)
    partial_out = jnp.dot(activated, w_down[0], preferred_element_type=jnp.float32)
    expert_out = lax.psum_scatter(
        partial_out.astype(jnp.bfloat16), "local", scatter_dimension=1, tiled=True
    )
    returned = lax.all_to_all(expert_out, "node", split_axis=0, concat_axis=0, tiled=True)
    combine_mat = jnp.sum(jnp.where(placement_map, route_weights[:, :, None], 0.0), axis=1)
    expert_mix = jnp.dot(combine_mat, returned.astype(jnp.float32), precision=lax.Precision.HIGHEST)
    layer_sum = hidden_states.astype(jnp.float32) + expert_mix
    layer_out = layer_sum.astype(jnp.bfloat16)
    squares = lax.psum(jnp.sum(layer_sum * layer_sum, axis=1), "local")
    d_model = part_width * lax.axis_size("local")
    inv_rms = lax.rsqrt(squares / d_model + 1e-06)
    normed = (layer_sum * inv_rms[:, None] * norm_gain[None, :]).astype(jnp.bfloat16)
    vocab_rows = head_weight.shape[0]
    first_id = lax.axis_index(("node", "local")) * vocab_rows
    rows_full = lax.all_gather(normed, "local", axis=1, tiled=True)
    logits = lax.dot_general(
        lax.all_gather(rows_full, "node", axis=0, tiled=True),
        head_weight,
        (((1,), (1,)), ((), ())),
        preferred_element_type=jnp.float32,
    )
    fresh = vocab_stats(logits, targets, first_id)
    peak, exp_total, target_logit = tuple((new for new in fresh))
    global_max = lax.pmax(peak, ("node", "local"))
    global_total, global_target = lax.psum(
        (exp_total * jnp.exp(peak - global_max), target_logit), ("node", "local")
    )
    ref_logp = global_target - global_max - jnp.log(global_total)
    kl = 0.5 * (policy_logp - ref_logp) * (policy_logp - ref_logp)
    return (layer_out, ref_logp, kl)


def solution(mesh):
    placed = (
        P("node", "local"),
        P("node", None),
        P("node", None),
        P("node", None, "local"),
        P("node", None, "local"),
        P("node", "local", None),
        P("local"),
        P(("node", "local"), None),
        P(),
        P(),
    )
    return jax.shard_map(
        shards,
        mesh=mesh,
        in_specs=placed,
        out_specs=(P("node", "local"), P(), P()),
        check_vma=False,
    )
```

profile of v0, /device:TPU:0, one launch (start us, length us, event | category | flops | bytes accessed | tf_op | source)
XLA Modules:
  0.0 537.1 jit_solution(11545633294973063654)
XLA Ops:
  7.2 0.8 copy.33
  8.2 0.9 reduce-window.6
  9.6 0.7 multiply_add_fusion
  10.5 1.4 convolution_convert_fusion.1
  12.2 25.9 %all_to_all.24 = bf16[16,36,896]{2,1,0:T(8,128)(2,1)S(1)} all-to-all(bf16[16,36,896]{2,1,0:T(8,128)(2,1)S(1)} %all_to_all.16), channel_id=1, replica_groups=mesh['node'=16,'local'=8] {'node'}, dimensions={0} | all-to-all | bytes 2064384 | tf_op jit(solution)/shard_map/all_to_all | solution.py:44
  38.1 1.1 all_to_all.18
  39.4 47.3 %all-gather.4.cloned.1.call-done = bf16[576,7168]{1,0:T(8,128)(2,1)} async-done(((bf16[576,896]{1,0:T(8,128)(2,1)}), bf16[576,7168]{1,0:T(8,128)(2,1)}) %all-gather.4.cloned.1.call-update) | async-done | bytes 8257552 | tf_op jit(solution)/shard_map/all_gather | solution.py:47
  86.7 6.7 %fusion.3 = f32[576,256]{1,0:T(8,128)S(1)} fusion(bf16[576,7168]{1,0:T(8,128)(2,1)} %all-gather.4.cloned.1.call-done, bf16[1,7168,256]{2,1,0:T(8,128)(2,1)} %param.13), kind=kOutput, calls=%fused_computation.4 | convolution fusion | flops 2113929216 | bytes 12517376 | tf_op jit(solution)/shard_map/dot_general | solution.py:48
  93.3 17.4 %convolution_convert_fusion = bf16[576,7168]{1,0:T(8,128)(2,1)} fusion(bf16[1,256,7168]{2,1,0:T(8,128)(2,1)} %param.15, bf16[576,7168]{1,0:T(8,128)(2,1)} %all-gather.4.cloned.1.call-done, bf16[1,7168,256]{2,1,0:T(8,128)(2,1)} %param.14, f32[576,256]{1,0:T(8,128)S(1)} %fusion.3), kind=kOutput, calls=%fused_computation | convolution fusion | flops 4232871936 | bytes 24444928 | tf_op jit(solution)/shard_map/dot_general | solution.py:51
  110.7 12.4 %copy.37 = bf16[576,7168]{0,1:T(8,128)(2,1)} copy(bf16[576,7168]{1,0:T(8,128)(2,1)} %convolution_convert_fusion) | data formatting | bytes 16515072
  123.2 56.5 %reduce-scatter.4.cloned.1.call-done = bf16[896,576]{1,0:T(8,128)(2,1)} async-done(((bf16[7168,576]{1,0:T(8,128)(2,1)}), bf16[896,576]{1,0:T(8,128)(2,1)}) %reduce-scatter.4.cloned.1.call-update) | async-done | bytes 1032208
  179.7 1.7 copy.38
  181.4 1.1 all_to_all.19
  182.5 7.1 %all-to-all-start.1 = ((bf16[16,36,896]{2,1,0:T(8,128)(2,1)}), bf16[16,36,896]{2,1,0:T(8,128)(2,1)S(1)}, u32[]{:S(2)}, u32[]{:S(2)}) async-start(bf16[16,36,896]{2,1,0:T(8,128)(2,1)} %all_to_all.19), calls=%async_computation.1 | async-start | bytes 2293760 | tf_op jit(solution)/shard_map/all_to_all | solution.py:55
  190.0 17.6 %all-to-all-done.1 = bf16[16,36,896]{2,1,0:T(8,128)(2,1)S(1)} async-done(((bf16[16,36,896]{2,1,0:T(8,128)(2,1)}), bf16[16,36,896]{2,1,0:T(8,128)(2,1)S(1)}, u32[]{:S(2)}, u32[]{:S(2)}) %all-to-all-start.1) | async-done | bytes 1032224 | tf_op jit(solution)/shard_map/all_to_all | solution.py:55
  207.9 0.8 multiply_reduce_fusion
  208.7 12.4 %psum.21 = f32[96]{0:T(128)S(1)} all-reduce(f32[96]{0:T(128)S(1)} %get-tuple-element.11), channel_id=1, replica_groups=mesh['node'=16,'local'=8] {'local'}, use_global_device_ids=true, to_apply=%region_7.8 | all-reduce | flops 96 | bytes 768 | tf_op jit(solution)/shard_map/psum | solution.py:60
  221.1 0.8 multiply_convert_fusion
  222.0 20.6 %all-gather.6.cloned.1.call-done = bf16[96,7168]{1,0:T(8,128)(2,1)} async-done(((bf16[96,896]{1,0:T(8,128)(2,1)}), bf16[96,7168]{1,0:T(8,128)(2,1)}) %all-gather.6.cloned.1.call-update) | async-done | bytes 1376272 | tf_op jit(solution)/shard_map/all_gather | solution.py:66
  242.7 140.2 %all-gather.8.cloned.1.call-done = bf16[1536,7168]{1,0:T(8,128)(2,1)} async-done(((bf16[96,7168]{1,0:T(8,128)(2,1)}), bf16[1536,7168]{1,0:T(8,128)(2,1)}) %all-gather.8.cloned.1.call-update) | async-done | bytes 22020112 | tf_op jit(solution)/shard_map/all_gather | solution.py:68
  382.8 17.2 %fusion.25 = (f32[1536]{0:T(1024)S(1)}, f32[1536,512]{0,1:T(8,128)S(1)}) fusion(bf16[1536,7168]{1,0:T(8,128)(2,1)} %all-gather.8.cloned.1.call-done, bf16[512,7168]{1,0:T(8,128)(2,1)} %param.17), kind=kOutput, calls=%fused_computation.39 | convolution fusion | flops 11275073536 | bytes 32512000 | tf_op jit(solution)/shard_map/dot_general | solution.py:67
  400.0 64.6 %pmax.7 = f32[1536]{0:T(1024)S(1)} all-reduce(f32[1536]{0:T(1024)S(1)} %get-tuple-element.13), channel_id=1, replica_groups=mesh['node'=16,'local'=8] {'node','local'}, use_global_device_ids=true, to_apply=%region_11.12 | all-reduce | flops 1536 | bytes 12288 | tf_op jit(solution)/shard_map/pmax | solution.py:75
  464.6 0.8 select_reduce_fusion
  465.4 64.6 %all-reduce = (f32[1536]{0:T(1024)S(1)}, f32[1536]{0:T(1024)S(1)}) all-reduce(f32[1536]{0:T(1024)S(1)} %exponential_multiply_fusion, f32[1536]{0:T(1024)S(1)} %get-tuple-element.3), channel_id=1, replica_groups=mesh['node'=16,'local'=8] {'node','local'}, use_global_device_ids=true, to_apply=%region_13.14 | all-reduce | flops 3072 | bytes 24576 | tf_op jit(solution)/shard_map/psum | solution.py:76
  (34 shorter events, 2.7 us)
Async XLA Ops:
  7.2 79.5 %all-gather.4.cloned.1.call-start = ((), (), s32[]{:S(2)}) async-start(), calls=%async_computation.3 | async-start | bytes 9289728 | tf_op jit(solution)/shard_map/all_gather | solution.py:47
  39.3 140.4 %reduce-scatter.4.cloned.1.call-start = ((), (), s32[]{:S(2)}) async-start(), calls=%async_computation.6 | async-start | bytes 10321920
  123.2 66.7 %copy-start.4 = (f32[96,4]{0,1:T(4,128)S(1)}, f32[96,4]{0,1:T(4,128)}, u32[]{:S(2)}) copy-start(f32[96,4]{0,1:T(4,128)} %param.12) | copy-start | bytes 4612
  181.4 26.5 %copy-start = (bf16[96,896]{1,0:T(8,128)(2,1)S(1)}, bf16[96,896]{1,0:T(8,128)(2,1)}, u32[]{:S(2)}) copy-start(bf16[96,896]{1,0:T(8,128)(2,1)} %param.10) | copy-start | bytes 516100
  182.5 38.6 %copy-start.3 = (f32[896]{0:T(1024)S(1)}, f32[896]{0:T(1024)}, u32[]{:S(2)}) copy-start(f32[896]{0:T(1024)} %param.16) | copy-start | bytes 10756
  182.5 25.1 %all-to-all-start.1 = ((bf16[16,36,896]{2,1,0:T(8,128)(2,1)}), bf16[16,36,896]{2,1,0:T(8,128)(2,1)S(1)}, u32[]{:S(2)}, u32[]{:S(2)}) async-start(bf16[16,36,896]{2,1,0:T(8,128)(2,1)} %all_to_all.19), calls=%async_computation.1 | async-start | bytes 2293760 | tf_op jit(solution)/shard_map/all_to_all | solution.py:55
  189.6 53.0 %all-gather.6.cloned.1.call-start = ((), (), s32[]{:S(2)}) async-start(), calls=%async_computation.4 | async-start | bytes 1548288 | tf_op jit(solution)/shard_map/all_gather | solution.py:66
  221.9 160.9 %all-gather.8.cloned.1.call-start = ((), (), s32[]{:S(2)}) async-start(), calls=%async_computation.5 | async-start | bytes 23396352 | tf_op jit(solution)/shard_map/all_gather | solution.py:68
  242.6 222.0 %copy-start.1 = (s32[1536]{0:T(1024)S(1)}, s32[1536]{0:T(1024)}, u32[]{:S(2)}) copy-start(s32[1536]{0:T(1024)} %param.18) | copy-start | bytes 18436
  242.6 287.3 %copy-start.2 = (f32[1536]{0:T(1024)S(1)}, f32[1536]{0:T(1024)}, u32[]{:S(2)}) copy-start(f32[1536]{0:T(1024)} %param.19) | copy-start | bytes 18436
Sparse Core Ops, SparseCore 0:
  39.4 47.1 all-gather.3
  123.3 56.3 reduce-scatter.3
  222.1 20.4 all-gather.5
  244.6 138.1 all-gather.7
where the time goes:
time: 538 us; the launch traced here: 537 us
  waiting for transfers between devices  282 us (52%)
  blocking collectives  168 us (31%)
  matrix products  43.5 us (8%)
  local copies, waits for them, and re-layouts  18.2 us (3%)
  between operations  13.9 us (3%)
  starting transfers between devices  7.42 us (1%)
    all_gather x1, waiting for transfers between devices, shards(): lax.all_gather(rows_full, 'node', axis=0, tiled=True)  140 us
    pmax x1, blocking collectives, shards(): global_max = lax.pmax(peak, ('node', 'local'))  64.6 us
    psum x1, blocking collectives, shards(): lax.psum((exp_total * jnp.exp(peak - global_max), target_logit), ('node',...  64.6 us
    unnamed x5, waiting for transfers between devices  56.6 us
    all_gather x1, waiting for transfers between devices, shards(): block_rows = lax.all_gather(arrived, 'local', axis=1, tiled=True)  47.3 us
    all_to_all x1, blocking collectives, shards(): lax.all_to_all(send_rows, 'node', split_axis=0, concat_axis=0, tiled=True)  25.9 us
    all_gather x1, waiting for transfers between devices, shards(): rows_full = lax.all_gather(normed, 'local', axis=1, tiled=True)  20.6 us
    all_to_all x1, waiting for transfers between devices, shards(): lax.all_to_all(expert_out, 'node', split_axis=0, concat_axis=0, tiled=True)  17.6 us
  transfers between devices with their start and end apart: 5, of which 5 were waited for; matrix products, arithmetic and copies ran while one was open for 0% of the time, Pallas kernels for 0%

commit v1 on v0

v1 whole, which is shorter than its diff:
```python
import functools
import jax
import jax.numpy as jnp
from jax import lax
from jax.experimental import pallas as pl
from jax.experimental.pallas import tpu as pltpu
from jax.sharding import Mesh, PartitionSpec as P

BF = jnp.bfloat16
F32 = jnp.float32
AXES = ("x", "z", "y", "core")
SLOTS = 40


def shift(value, axis, step):
    size = lax.axis_size(axis)
    return lax.ppermute(value, axis, [(i, (i + step) % size) for i in range(size)])


def dot(a, b):
    return jnp.dot(a, b, preferred_element_type=F32)


def dispatch_kernel(routes_ref, weights_ref, h0, h1, h2, h3, send_ref, hi_ref, lo_ref):
    tokens, top = routes_ref.shape
    experts = send_ref.shape[0] // SLOTS
    columns = send_ref.shape[0]
    ids = lax.broadcasted_iota(jnp.int32, (tokens, experts), 1)
    named = jnp.zeros((tokens, experts), F32)
    gates = jnp.zeros((tokens, experts), F32)
    for k in range(top):
        hit = routes_ref[:, k : k + 1] == ids
        named = named + jnp.where(hit, 1.0, 0.0)
        gates = gates + jnp.where(hit, weights_ref[:, k : k + 1], 0.0)
    row = lax.broadcasted_iota(jnp.int32, (tokens, tokens), 0)
    col = lax.broadcasted_iota(jnp.int32, (tokens, tokens), 1)
    before = jnp.where(col < row, 1.0, 0.0).astype(BF)
    count = dot(before, named.astype(BF))
    expert = lax.broadcasted_iota(jnp.int32, (experts, columns), 0)
    column = lax.broadcasted_iota(jnp.int32, (experts, columns), 1)
    inside = (column >= expert * SLOTS) & (column < expert * SLOTS + SLOTS)
    spread = jnp.where(inside, 1.0, 0.0).astype(BF)
    slot = jnp.sum(jnp.where(inside, column - expert * SLOTS, 0).astype(F32), axis=0, keepdims=True)
    gates_hi = gates.astype(BF)
    gates_lo = (gates - gates_hi.astype(F32)).astype(BF)
    placed = (dot(named.astype(BF), spread) > 0.5) & (dot(count.astype(BF), spread) == slot)
    hi_ref[...] = jnp.where(placed, dot(gates_hi, spread), 0.0).astype(BF)
    lo_ref[...] = jnp.where(placed, dot(gates_lo, spread), 0.0).astype(BF)
    pick = jnp.where(placed, 1.0, 0.0).astype(BF)
    width = h0.shape[1]
    for k, ref in enumerate((h0, h1, h2, h3)):
        rows = lax.dot_general(pick, ref[...], (((0,), (0,)), ((), ())), preferred_element_type=F32)
        send_ref[:, k * width : (k + 1) * width] = rows.astype(BF)


def up_kernel(place_ref, rows_ref, g_own, u_own, g_other, u_other, sum_ref, out_ref):
    k = pl.program_id(0)
    rows = rows_ref[...]
    hidden = g_own.shape[1]
    for j, ref in enumerate((g_own, u_own, g_other, u_other)):
        cols = slice(j * hidden, (j + 1) * hidden)
        part = dot(rows, ref[...])

        @pl.when(k == 0)
        def _(part=part, cols=cols):
            sum_ref[:, cols] = part

        @pl.when(k > 0)
        def _(part=part, cols=cols):
            sum_ref[:, cols] += part

    @pl.when(k == pl.num_programs(0) - 1)
    def _():
        out_ref[...] = sum_ref[...].astype(BF)


def down_kernel(place_ref, sum_ref, got_ref, d_own, d_other, out_ref, act_ref):
    hidden = d_own.shape[0]

    @pl.when(pl.program_id(0) == 0)
    def _():
        for j in range(2):
            own, got = 2 * j * hidden, 2 * (1 - j) * hidden
            gate = sum_ref[:, own : own + hidden] + got_ref[:, got : got + hidden].astype(F32)
            up = sum_ref[:, own + hidden : own + 2 * hidden] + got_ref[
                :, got + hidden : got + 2 * hidden
            ].astype(F32)
            act = gate / (1.0 + jnp.exp(-gate)) * up
            act_ref[:, j * hidden : (j + 1) * hidden] = act.astype(BF)

    total = dot(act_ref[:, :hidden], d_own[...]) + dot(act_ref[:, hidden:], d_other[...])
    out_ref[...] = total.astype(BF)


def mix_kernel(hi_ref, lo_ref, back_ref, own_ref, p1, p2, p3):
    width = own_ref.shape[1]
    for k, ref in enumerate((own_ref, p1, p2, p3)):
        block = back_ref[:, k * width : (k + 1) * width]
        total = dot(hi_ref[...], block) + dot(lo_ref[...], block)
        ref[...] = total.astype(ref.dtype)


def layer_kernel(hidden_ref, own_ref, p1, p2, p3, gain_ref, out_ref, scaled_ref, squares_ref):
    mix = own_ref[...] + p1[...].astype(F32) + p2[...].astype(F32) + p3[...].astype(F32)
    total = hidden_ref[...].astype(F32) + mix
    out_ref[...] = total.astype(BF)
    scaled_ref[...] = (total * gain_ref[...]).astype(BF)
    squares_ref[...] = jnp.sum(total * total, axis=1, keepdims=True)


def head_kernel(first_ref, rows_ref, head_ref, scale_ref, wanted_ref, stats_ref, sum_ref):
    part = pl.program_id(1)
    nodes, _, tokens, width = rows_ref.shape
    rows = rows_ref[...].reshape(nodes * tokens, width)
    start = pl.multiple_of(part * width, 128)
    logits = lax.dot_general(
        rows, head_ref[:, pl.ds(start, width)], (((1,), (1,)), ((), ())), preferred_element_type=F32
    )

    @pl.when(part == 0)
    def _():
        sum_ref[...] = logits

    @pl.when(part > 0)
    def _():
        sum_ref[...] += logits

    @pl.when(part == pl.num_programs(1) - 1)
    def _():
        full = sum_ref[...] * scale_ref[...]
        peak = jnp.max(full, axis=1, keepdims=True)
        total = jnp.sum(jnp.exp(full - peak), axis=1, keepdims=True)
        ids = first_ref[0] + lax.broadcasted_iota(jnp.int32, full.shape, 1)
        target = jnp.sum(jnp.where(ids == wanted_ref[...], full, 0.0), axis=1, keepdims=True)
        lane = lax.broadcasted_iota(jnp.int32, (full.shape[0], 128), 1)
        stats_ref[...] = jnp.where(lane == 0, peak, jnp.where(lane == 1, total, target))


def paired(terms):
    if len(terms) == 2:
        return terms[0] + terms[1]
    return (terms[0] + terms[2]) + (terms[1] + terms[3])


def merged(values):
    peaks = [v[0] for v in values]
    peak = functools.reduce(jnp.maximum, peaks)
    total = paired([v[1] * jnp.exp(v[0] - peak) for v in values])
    return jnp.stack([peak, total, paired([v[2] for v in values])])


def shards(hidden, routes, route_weights, w_gate, w_up, w_down, gain, head, targets, policy_logp):
    tokens, width = hidden.shape
    y = lax.axis_index("y")
    core = lax.axis_index("core")
    n_y = lax.axis_size("y")
    n_node = lax.axis_size("x") * lax.axis_size("z")
    slots = n_node * SLOTS
    wide = n_y * width
    model = 2 * wide
    hid = w_gate.shape[2]
    vmem = pltpu.CompilerParams(vmem_limit_bytes=48 * 1024 * 1024)

    near = [hidden] + [shift(hidden, "y", k) for k in (1, 2, 3)]
    gate_mat, up_mat, down_mat = w_gate[0], w_up[0], w_down[0]
    gate_other, up_other, down_other = (shift(w, "core", 1) for w in (gate_mat, up_mat, down_mat))

    send, mix_hi, mix_lo = pl.pallas_call(
        dispatch_kernel,
        out_shape=(
            jax.ShapeDtypeStruct((slots, wide), BF),
            jax.ShapeDtypeStruct((tokens, slots), BF),
            jax.ShapeDtypeStruct((tokens, slots), BF),
        ),
        compiler_params=vmem,
        name="dispatch",
    )(routes, route_weights, *near)

    rows = lax.all_to_all(
        send.reshape(n_node, SLOTS, wide), ("x", "z"), split_axis=0, concat_axis=0, tiled=True
    ).reshape(slots, wide)

    place = jnp.stack([y, core]).astype(jnp.int32)

    def block(k, place):
        return 2 * lax.rem(place[0] + n_y - k, n_y) + place[1]

    weight_rows = pl.BlockSpec((width, hid), lambda k, place: (block(k, place), 0))
    partial, partial_out = pl.pallas_call(
        up_kernel,
        grid_spec=pltpu.PrefetchScalarGridSpec(
            num_scalar_prefetch=1,
            grid=(n_y,),
            in_specs=[pl.BlockSpec((slots, width), lambda k, place: (0, k))] + [weight_rows] * 4,
            out_specs=[pl.BlockSpec((slots, 4 * hid), lambda k, place: (0, 0))] * 2,
        ),
        out_shape=(
            jax.ShapeDtypeStruct((slots, 4 * hid), F32),
            jax.ShapeDtypeStruct((slots, 4 * hid), BF),
        ),
        compiler_params=vmem,
        name="gate_up",
    )(place, rows, gate_mat, up_mat, gate_other, up_other)
    partial_got = shift(partial_out, "core", 1)

    weight_cols = pl.BlockSpec((hid, width), lambda k, place: (0, block(k, place)))
    whole = pl.BlockSpec((slots, 4 * hid), lambda k, place: (0, 0))
    expert_out = pl.pallas_call(
        down_kernel,
        grid_spec=pltpu.PrefetchScalarGridSpec(
            num_scalar_prefetch=1,
            grid=(n_y,),
            in_specs=[whole, whole, weight_cols, weight_cols],
            out_specs=pl.BlockSpec((slots, width), lambda k, place: (0, k)),
            scratch_shapes=[pltpu.VMEM((slots, 2 * hid), BF)],
        ),
        out_shape=jax.ShapeDtypeStruct((slots, wide), BF),
        compiler_params=vmem,
        name="down",
    )(place, partial, partial_got, down_mat, down_other)

    returned = lax.all_to_all(
        expert_out.reshape(n_node, SLOTS, wide), ("x", "z"), split_axis=0, concat_axis=0, tiled=True
    ).reshape(slots, wide)
    own, *others = pl.pallas_call(
        mix_kernel,
        out_shape=(jax.ShapeDtypeStruct((tokens, width), F32),)
        + (jax.ShapeDtypeStruct((tokens, width), BF),) * 3,
        compiler_params=vmem,
        name="mix",
    )(mix_hi, mix_lo, returned)
    arrived = [shift(part, "y", -k) for k, part in zip((1, 2, 3), others)]
    layer_out, scaled, squares = pl.pallas_call(
        layer_kernel,
        out_shape=(
            jax.ShapeDtypeStruct((tokens, width), BF),
            jax.ShapeDtypeStruct((tokens, width), BF),
            jax.ShapeDtypeStruct((tokens, 1), F32),
        ),
        compiler_params=vmem,
        name="layer",
    )(hidden, own, *arrived, gain.reshape(1, width))

    everyone = lax.all_gather(scaled, AXES, axis=0, tiled=True)

    squares = squares.reshape(1, tokens)
    squares = squares + shift(squares, "core", 1)
    squares = paired([squares] + [shift(squares, "y", k) for k in (1, 2, 3)])
    for axis in ("z", "x"):
        here = lax.axis_index(axis)
        size = lax.axis_size(axis)
        order = jnp.arange(size)[:, None, None]
        gathered = jnp.where(order == here, squares[None], 0.0)
        for k in range(1, size):
            from_there = shift(squares, axis, k)
            gathered = gathered + jnp.where(order == (here - k) % size, from_there[None], 0.0)
        squares = gathered.reshape(-1, tokens)
    total_tokens = n_node * tokens
    scale = lax.rsqrt(squares.reshape(total_tokens, 1) / model + 1e-06)

    vocab_rows = head.shape[0]
    first_id = lax.axis_index(AXES) * vocab_rows
    group = 4
    stats = pl.pallas_call(
        head_kernel,
        grid_spec=pltpu.PrefetchScalarGridSpec(
            num_scalar_prefetch=1,
            grid=(n_node // group, 2 * n_y),
            in_specs=[
                pl.BlockSpec((group, 1, tokens, width), lambda n, p, s: (n, p, 0, 0)),
                pl.BlockSpec((vocab_rows, model), lambda n, p, s: (0, 0)),
                pl.BlockSpec((group * tokens, 1), lambda n, p, s: (n, 0)),
                pl.BlockSpec((group * tokens, 1), lambda n, p, s: (n, 0)),
            ],
            out_specs=pl.BlockSpec((group * tokens, 128), lambda n, p, s: (n, 0)),
            scratch_shapes=[pltpu.VMEM((group * tokens, vocab_rows), F32)],
        ),
        out_shape=jax.ShapeDtypeStruct((total_tokens, 128), F32),
        compiler_params=vmem,
        name="head",
    )(
        first_id.reshape(1).astype(jnp.int32),
        everyone.reshape(n_node, 2 * n_y, tokens, width),
        head,
        scale,
        targets.reshape(total_tokens, 1),
    )
    stats = stats[:, :3].T
    stats = merged([stats, shift(stats, "core", 1)])
    for axis in ("y", "z", "x"):
        stats = merged([stats] + [shift(stats, axis, k) for k in (1, 2, 3)])
    peak, exp_total, target_logit = stats
    ref_logp = target_logit - peak - jnp.log(exp_total)
    kl = 0.5 * (policy_logp - ref_logp) * (policy_logp - ref_logp)
    return layer_out, ref_logp, kl


def solution(mesh):
    split = Mesh(mesh.devices.reshape(4, 4, 4, 2), AXES)
    node, local = ("x", "z"), ("y", "core")
    placed = (
        P(node, local),
        P(node, None),
        P(node, None),
        P(node, None, local),
        P(node, None, local),
        P(node, local, None),
        P(local),
        P(AXES, None),
        P(),
        P(),
    )
    return jax.shard_map(
        shards,
        mesh=split,
        in_specs=placed,
        out_specs=(P(node, local), P(), P()),
        check_vma=False,
    )
```

time: 538 us -> 410 us (0.76)
  waiting for transfers between devices: 282 us -> 167 us
  blocking collectives: 168 us -> 67.9 us
  Pallas kernels: 0 us -> 62.9 us
  matrix products: 43.5 us -> 0 us
  starting transfers between devices: 7.42 us -> 41.5 us
  local copies, waits for them, and re-layouts: 18.2 us -> 37.5 us
  other arithmetic: 4.24 us -> 17.2 us
    all_gather x3 -> x1, waiting for transfers between devices: 208 us -> 61.5 us  [shards(): everyone = lax.all_gather(scaled, AXES, axis=0, tiled=True)]
    psum x2 -> x0, blocking collectives: 77 us -> none  [the longest x1 64.6 us: shards(): lax.psum((exp_total * jnp.exp(peak - global_max), target_logit), ('node',...]
    pmax x1 -> x0, blocking collectives: 64.6 us -> none  [shards(): global_max = lax.pmax(peak, ('node', 'local'))]
    pallas_call x0 -> x6, Pallas kernels: none -> 62.9 us  [the longest x1 34 us: shards(): pl.pallas_call(head_kernel, grid_spec=pltpu.PrefetchScalarGridSpec(num_sc...]
    unnamed x5 -> x1, waiting for transfers between devices: 56.6 us -> 0.02 us
    ppermute x0 -> x30, waiting for transfers between devices: none -> 50.6 us  [shift(): lax.ppermute(value, axis, [(i, (i + step) % size) for i in range(size)])]
    dot_general x5 -> x0, matrix products: 43.5 us -> none  [the longest x1 17.4 us: shards(): jnp.dot(activated, w_down[0], preferred_element_type=jnp.float32)]
    all_to_all x1, blocking collectives: 25.9 us -> 67.9 us  [shards(): lax.all_to_all(expert_out.reshape(n_node, SLOTS, wide), ('x', 'z'), split...]
  transfers between devices with their start and end apart: 5 -> 32, of which waited for: 5 -> 29; matrix products, arithmetic and copies ran while one was open for 0% -> 2% of each run, Pallas kernels for 0% -> 4%
where the time goes in v1:
time: 410 us; the launch traced here: 408 us
  waiting for transfers between devices  167 us (41%)
  blocking collectives  67.9 us (17%)
  Pallas kernels  62.9 us (15%)
  starting transfers between devices  41.5 us (10%)
  local copies, waits for them, and re-layouts  37.5 us (9%)
  other arithmetic  17.2 us (4%)
  between operations  14.4 us (4%)
    all_to_all x1, blocking collectives, shards(): lax.all_to_all(expert_out.reshape(n_node, SLOTS, wide), ('x', 'z'), split...  67.9 us
    all_gather x1, waiting for transfers between devices, shards(): everyone = lax.all_gather(scaled, AXES, axis=0, tiled=True)  61.5 us
    all_to_all x1, waiting for transfers between devices, shards(): lax.all_to_all(send.reshape(n_node, SLOTS, wide), ('x', 'z'), split_axis=...  54.7 us
    ppermute x30, waiting for transfers between devices, shift(): lax.ppermute(value, axis, [(i, (i + step) % size) for i in range(size)])  50.6 us
    pallas_call x1, Pallas kernels, shards(): pl.pallas_call(head_kernel, grid_spec=pltpu.PrefetchScalarGridSpec(num_sc...  34 us
    ppermute x30, starting transfers between devices, shift(): lax.ppermute(value, axis, [(i, (i + step) % size) for i in range(size)])  33.6 us
    unnamed x34, local copies, waits for them, and re-layouts  20.5 us
    pallas_call x1, Pallas kernels, shards(): pl.pallas_call(up_kernel, grid_spec=pltpu.PrefetchScalarGridSpec(num_scal...  17.1 us
  transfers between devices with their start and end apart: 32, of which 29 were waited for; matrix products, arithmetic and copies ran while one was open for 2% of the time, Pallas kernels for 4%

profile of v1, /device:TPU:0, one launch (start us, length us, event | category | flops | bytes accessed | tf_op | source)
XLA Modules:
  0.0 408.4 jit_solution(514244051815057843)
XLA Ops:
  7.2 3.2 collective-permute-start.2
  13.5 4.5 %collective-permute-done.2.h3 = bf16[96,896]{1,0:T(8,128)(2,1)S(1)} collective-permute-done((bf16[96,896]{1,0:T(8,128)(2,1)}, bf16[96,896]{1,0:T(8,128)(2,1)S(1)}, u32[]{:S(2)}, u32[]{:S(2)}) %collective-permute-start.2) | collective-permute-done | bytes 172064 | tf_op jit(solution)/shard_map/ppermute | solution.py:17
  26.4 7.9 %all-to-all-start = ((bf16[16,40,3584]{2,1,0:T(8,128)(2,1)}), bf16[16,40,3584]{2,1,0:T(8,128)(2,1)}, u32[]{:S(2)}, u32[]{:S(2)}) async-start(bf16[16,40,3584]{2,1,0:T(8,128)(2,1)} %bitcast.20), calls=%async_computation | async-start | bytes 9175040 | tf_op jit(solution)/shard_map/all_to_all | solution.py:179
  35.2 6.1 %collective-permute-done.3.g_other = bf16[7168,256]{1,0:T(8,128)(2,1)} collective-permute-done((bf16[7168,256]{1,0:T(8,128)(2,1)}, bf16[7168,256]{1,0:T(8,128)(2,1)}, u32[]{:S(2)}, u32[]{:S(2)}) %collective-permute-start.3) | collective-permute-done | bytes 3670048 | tf_op jit(solution)/shard_map/ppermute | solution.py:17
  41.2 5.2 %collective-permute-done.4.u_other = bf16[7168,256]{1,0:T(8,128)(2,1)} collective-permute-done((bf16[7168,256]{1,0:T(8,128)(2,1)}, bf16[7168,256]{1,0:T(8,128)(2,1)}, u32[]{:S(2)}, u32[]{:S(2)}) %collective-permute-start.4) | collective-permute-done | bytes 3670048 | tf_op jit(solution)/shard_map/ppermute | solution.py:17
  46.5 54.7 %all-to-all-done = bf16[16,40,3584]{2,1,0:T(8,128)(2,1)} async-done(((bf16[16,40,3584]{2,1,0:T(8,128)(2,1)}), bf16[16,40,3584]{2,1,0:T(8,128)(2,1)}, u32[]{:S(2)}, u32[]{:S(2)}) %all-to-all-start) | async-done | bytes 4587552 | tf_op jit(solution)/shard_map/all_to_all | solution.py:179
  101.2 17.1 %gate_up.1 = (f32[640,1024]{1,0:T(8,128)S(1)}, bf16[640,1024]{1,0:T(8,128)(2,1)S(1)}) custom-call(s32[2]{0:T(128)S(1)} %pad_add_fusion.place_ref, bf16[640,3584]{1,0:T(8,128)(2,1)} %bitcast.3.rows_ref, bf16[7168,256]{1,0:T(8,128)(2,1)} %bitcast.26, bf16[7168,256]{1,0:T(8,128)(2,1)} %bitcast.28, bf16[7168,256]{1,0:T(8,128)(2,1)} %collective-permute-done.3.g_other, ...), custom_call_target="tpu_custom_call" | custom-call | tf_op jit(solution)/shard_map/gate_up/pallas_call | solution.py:189
  118.4 3.0 collective-permute-done.5.got_ref
  121.5 7.5 %down.1 = bf16[640,3584]{1,0:T(8,128)(2,1)} custom-call(s32[2]{0:T(128)S(1)} %pad_add_fusion.place_ref, f32[640,1024]{1,0:T(8,128)S(1)} %get-tuple-element.18.sum_ref, bf16[640,1024]{1,0:T(8,128)(2,1)S(1)} %collective-permute-done.5.got_ref, bf16[256,7168]{1,0:T(8,128)(2,1)} %bitcast.24, bf16[256,7168]{1,0:T(8,128)(2,1)} %collective-permute-done.6.d_other), custom_call_target="tpu_custom_call" | custom-call | tf_op jit(solution)/shard_map/down/pallas_call | solution.py:208
  129.0 67.9 %all_to_all.10 = bf16[16,40,3584]{2,1,0:T(8,128)(2,1)S(1)} all-to-all(bf16[16,40,3584]{2,1,0:T(8,128)(2,1)} %bitcast.22), channel_id=1, replica_groups=mesh['x'=4,'z'=4,'y'=4,'core'=2] {'x','z'}, dimensions={0} | all-to-all | bytes 9175040 | tf_op jit(solution)/shard_map/all_to_all | solution.py:222
  201.4 3.5 collective-permute-done.7.p1
  214.2 2.3 collective-permute-done.12
  221.3 3.1 collective-permute-done.15
  229.0 3.2 collective-permute-done.18
  233.3 61.5 %all-gather.2.cloned.1.call-done = bf16[12288,896]{1,0:T(8,128)(2,1)} async-done(((bf16[96,896]{1,0:T(8,128)(2,1)}), bf16[12288,896]{1,0:T(8,128)(2,1)}) %all-gather.2.cloned.1.call-update) | async-done | bytes 22020112 | tf_op jit(solution)/shard_map/all_gather | solution.py:244
  294.8 34.0 %head.1 = f32[1536,128]{1,0:T(8,128)S(1)} custom-call(s32[1]{0:T(128)} %bitcast.9.first_ref, bf16[16,8,96,896]{3,2,1,0:T(8,128)(2,1)} %bitcast.21, bf16[512,7168]{1,0:T(8,128)(2,1)} %head_ref.1, f32[1536,1]{1,0:T(8,128)S(1)} %reshape.372.scale_ref, s32[1536,1]{1,0:T(8,128)S(1)} %reshape.373.wanted_ref), custom_call_target="tpu_custom_call" | custom-call | tf_op jit(solution)/shard_map/head/pallas_call | solution.py:264
  334.0 2.5 slice_reduce_fusion.1
  337.4 3.1 collective-permute-start.21
  354.4 3.8 add_add_fusion.1
  360.1 2.7 collective-permute-start.24
  379.2 2.7 fusion.8
  384.7 3.6 exponential_multiply_fusion.2
  391.4 2.6 collective-permute-start.27
  397.8 2.4 collective-permute-done.28
  (136 shorter events, 85.9 us)
Async XLA Ops:
  7.2 10.8 %collective-permute-start.2 = (bf16[96,896]{1,0:T(8,128)(2,1)}, bf16[96,896]{1,0:T(8,128)(2,1)S(1)}, u32[]{:S(2)}, u32[]{:S(2)}) collective-permute-start(bf16[96,896]{1,0:T(8,128)(2,1)} %hidden_ref.1), channel_id=1, source_target_pairs={{0,6},{2,0},{4,2},{6,4},{1,7},{3,1},{5,3},{7,5},{8,14},{10,8},{12,... | collective-permute-start | bytes 516104 | tf_op jit(solution)/shard_map/ppermute | solution.py:17
  10.3 9.1 %collective-permute-start.1 = (bf16[96,896]{1,0:T(8,128)(2,1)}, bf16[96,896]{1,0:T(8,128)(2,1)S(1)}, u32[]{:S(2)}, u32[]{:S(2)}) collective-permute-start(bf16[96,896]{1,0:T(8,128)(2,1)} %hidden_ref.1), channel_id=1, source_target_pairs={{0,4},{2,6},{4,0},{6,2},{1,5},{3,7},{5,1},{7,3},{8,12},{10,14},{12... | collective-permute-start | bytes 516104 | tf_op jit(solution)/shard_map/ppermute | solution.py:17
  11.0 10.6 %collective-permute-start = (bf16[96,896]{1,0:T(8,128)(2,1)}, bf16[96,896]{1,0:T(8,128)(2,1)S(1)}, u32[]{:S(2)}, u32[]{:S(2)}) collective-permute-start(bf16[96,896]{1,0:T(8,128)(2,1)} %hidden_ref.1), channel_id=1, source_target_pairs={{0,2},{2,4},{4,6},{6,0},{1,3},{3,5},{5,7},{7,1},{8,10},{10,12},{12... | collective-permute-start | bytes 516104 | tf_op jit(solution)/shard_map/ppermute | solution.py:17
  26.4 74.8 %all-to-all-start = ((bf16[16,40,3584]{2,1,0:T(8,128)(2,1)}), bf16[16,40,3584]{2,1,0:T(8,128)(2,1)}, u32[]{:S(2)}, u32[]{:S(2)}) async-start(bf16[16,40,3584]{2,1,0:T(8,128)(2,1)} %bitcast.20), calls=%async_computation | async-start | bytes 9175040 | tf_op jit(solution)/shard_map/all_to_all | solution.py:179
  34.4 260.4 %all-gather.2.cloned.1.call-start = ((), (), s32[]{:S(2)}) async-start(), calls=%async_computation.2 | async-start | bytes 22192128 | tf_op jit(solution)/shard_map/all_gather | solution.py:244
  34.4 6.8 %collective-permute-start.3 = (bf16[7168,256]{1,0:T(8,128)(2,1)}, bf16[7168,256]{1,0:T(8,128)(2,1)}, u32[]{:S(2)}, u32[]{:S(2)}) collective-permute-start(bf16[7168,256]{1,0:T(8,128)(2,1)} %bitcast.25), channel_id=1, source_target_pairs={{0,1},{1,0},{2,3},{3,2},{4,5},{5,4},{6,7},{7,6},{8,9},{9,8},{10,11... | collective-permute-start | bytes 11010056 | tf_op jit(solution)/shard_map/ppermute | solution.py:17
  34.5 12.0 %collective-permute-start.4 = (bf16[7168,256]{1,0:T(8,128)(2,1)}, bf16[7168,256]{1,0:T(8,128)(2,1)}, u32[]{:S(2)}, u32[]{:S(2)}) collective-permute-start(bf16[7168,256]{1,0:T(8,128)(2,1)} %bitcast.27), channel_id=1, source_target_pairs={{0,1},{1,0},{2,3},{3,2},{4,5},{5,4},{6,7},{7,6},{8,9},{9,8},{10,11... | collective-permute-start | bytes 11010056 | tf_op jit(solution)/shard_map/ppermute | solution.py:17
  35.0 83.4 %collective-permute-start.6 = (bf16[256,7168]{1,0:T(8,128)(2,1)}, bf16[256,7168]{1,0:T(8,128)(2,1)}, u32[]{:S(2)}, u32[]{:S(2)}) collective-permute-start(bf16[256,7168]{1,0:T(8,128)(2,1)} %bitcast.23), channel_id=1, source_target_pairs={{0,1},{1,0},{2,3},{3,2},{4,5},{5,4},{6,7},{7,6},{8,9},{9,8},{10,11... | collective-permute-start | bytes 11010056 | tf_op jit(solution)/shard_map/ppermute | solution.py:17
  198.5 6.4 %collective-permute-start.7 = (bf16[96,896]{1,0:T(8,128)(2,1)S(1)}, bf16[96,896]{1,0:T(8,128)(2,1)S(1)}, u32[]{:S(2)}, u32[]{:S(2)}) collective-permute-start(bf16[96,896]{1,0:T(8,128)(2,1)S(1)} %get-tuple-element.21), channel_id=1, source_target_pairs={{0,6},{2,0},{4,2},{6,4},{1,7},{3,1},{5,3},{7,5},{8,14},{10,8},{12,... | collective-permute-start | bytes 516104 | tf_op jit(solution)/shard_map/ppermute | solution.py:17
  198.6 8.1 %collective-permute-start.8 = (bf16[96,896]{1,0:T(8,128)(2,1)S(1)}, bf16[96,896]{1,0:T(8,128)(2,1)S(1)}, u32[]{:S(2)}, u32[]{:S(2)}) collective-permute-start(bf16[96,896]{1,0:T(8,128)(2,1)S(1)} %get-tuple-element.22), channel_id=1, source_target_pairs={{0,4},{2,6},{4,0},{6,2},{1,5},{3,7},{5,1},{7,3},{8,12},{10,14},{12... | collective-permute-start | bytes 516104 | tf_op jit(solution)/shard_map/ppermute | solution.py:17
  200.1 8.3 %collective-permute-start.9 = (bf16[96,896]{1,0:T(8,128)(2,1)S(1)}, bf16[96,896]{1,0:T(8,128)(2,1)S(1)}, u32[]{:S(2)}, u32[]{:S(2)}) collective-permute-start(bf16[96,896]{1,0:T(8,128)(2,1)S(1)} %get-tuple-element.23), channel_id=1, source_target_pairs={{0,2},{2,4},{4,6},{6,0},{1,3},{3,5},{5,7},{7,1},{8,10},{10,12},{12... | collective-permute-start | bytes 516104 | tf_op jit(solution)/shard_map/ppermute | solution.py:17
  211.8 4.8 %collective-permute-start.12 = (f32[1,96]{1,0:T(1,128)S(1)}, f32[1,96]{1,0:T(1,128)S(1)}, u32[]{:S(2)}, u32[]{:S(2)}) collective-permute-start(f32[1,96]{1,0:T(1,128)S(1)} %bitcast_add_fusion), channel_id=1, source_target_pairs={{0,2},{2,4},{4,6},{6,0},{1,3},{3,5},{5,7},{7,1},{8,10},{10,12},{12... | collective-permute-start | bytes 1160 | tf_op jit(solution)/shard_map/ppermute | solution.py:17
  212.7 5.0 %collective-permute-start.11 = (f32[1,96]{1,0:T(1,128)S(1)}, f32[1,96]{1,0:T(1,128)S(1)}, u32[]{:S(2)}, u32[]{:S(2)}) collective-permute-start(f32[1,96]{1,0:T(1,128)S(1)} %bitcast_add_fusion), channel_id=1, source_target_pairs={{0,4},{2,6},{4,0},{6,2},{1,5},{3,7},{5,1},{7,3},{8,12},{10,14},{12... | collective-permute-start | bytes 1160 | tf_op jit(solution)/shard_map/ppermute | solution.py:17
  219.3 5.0 %collective-permute-start.15 = (f32[1,96]{1,0:T(1,128)S(1)}, f32[1,96]{1,0:T(1,128)S(1)}, u32[]{:S(2)}, u32[]{:S(2)}) collective-permute-start(f32[1,96]{1,0:T(1,128)S(1)} %add_add_fusion.4), channel_id=1, source_target_pairs={{0,16},{8,24},{16,0},{24,8},{1,17},{9,25},{17,1},{25,9},{2,18},{10... | collective-permute-start | bytes 1160 | tf_op jit(solution)/shard_map/ppermute | solution.py:17
  220.3 4.8 %collective-permute-start.14 = (f32[1,96]{1,0:T(1,128)S(1)}, f32[1,96]{1,0:T(1,128)S(1)}, u32[]{:S(2)}, u32[]{:S(2)}) collective-permute-start(f32[1,96]{1,0:T(1,128)S(1)} %add_add_fusion.4), channel_id=1, source_target_pairs={{0,8},{8,16},{16,24},{24,0},{1,9},{9,17},{17,25},{25,1},{2,10},{10... | collective-permute-start | bytes 1160 | tf_op jit(solution)/shard_map/ppermute | solution.py:17
  227.1 5.1 %collective-permute-start.18 = (f32[4,96]{1,0:T(4,128)S(1)}, f32[4,96]{1,0:T(4,128)S(1)}, u32[]{:S(2)}, u32[]{:S(2)}) collective-permute-start(f32[4,96]{1,0:T(4,128)S(1)} %select_add_fusion), channel_id=1, source_target_pairs={{0,64},{32,96},{64,0},{96,32},{1,65},{33,97},{65,1},{97,33},{2,66}... | collective-permute-start | bytes 4616 | tf_op jit(solution)/shard_map/ppermute | solution.py:17
  227.7 4.8 %collective-permute-start.17 = (f32[4,96]{1,0:T(4,128)S(1)}, f32[4,96]{1,0:T(4,128)S(1)}, u32[]{:S(2)}, u32[]{:S(2)}) collective-permute-start(f32[4,96]{1,0:T(4,128)S(1)} %select_add_fusion), channel_id=1, source_target_pairs={{0,32},{32,64},{64,96},{96,0},{1,33},{33,65},{65,97},{97,1},{2,34}... | collective-permute-start | bytes 4616 | tf_op jit(solution)/shard_map/ppermute | solution.py:17
  337.4 5.4 %collective-permute-start.21 = (f32[3,1536]{1,0:T(4,128)S(1)}, f32[3,1536]{1,0:T(4,128)S(1)}, u32[]{:S(2)}, u32[]{:S(2)}) collective-permute-start(f32[3,1536]{1,0:T(4,128)S(1)} %pad_maximum_fusion), channel_id=1, source_target_pairs={{0,4},{2,6},{4,0},{6,2},{1,5},{3,7},{5,1},{7,3},{8,12},{10,14},{12... | collective-permute-start | bytes 55304 | tf_op jit(solution)/shard_map/ppermute | solution.py:17
  340.4 5.9 %collective-permute-start.23 = (f32[3,1536]{1,0:T(4,128)S(1)}, f32[3,1536]{1,0:T(4,128)S(1)}, u32[]{:S(2)}, u32[]{:S(2)}) collective-permute-start(f32[3,1536]{1,0:T(4,128)S(1)} %pad_maximum_fusion), channel_id=1, source_target_pairs={{0,6},{2,0},{4,2},{6,4},{1,7},{3,1},{5,3},{7,5},{8,14},{10,8},{12,... | collective-permute-start | bytes 55304 | tf_op jit(solution)/shard_map/ppermute | solution.py:17
  341.6 5.0 %collective-permute-start.22 = (f32[3,1536]{1,0:T(4,128)S(1)}, f32[3,1536]{1,0:T(4,128)S(1)}, u32[]{:S(2)}, u32[]{:S(2)}) collective-permute-start(f32[3,1536]{1,0:T(4,128)S(1)} %pad_maximum_fusion), channel_id=1, source_target_pairs={{0,2},{2,4},{4,6},{6,0},{1,3},{3,5},{5,7},{7,1},{8,10},{10,12},{12... | collective-permute-start | bytes 55304 | tf_op jit(solution)/shard_map/ppermute | solution.py:17
  360.1 5.4 %collective-permute-start.24 = (f32[3,1536]{1,0:T(4,128)S(1)}, f32[3,1536]{1,0:T(4,128)S(1)}, u32[]{:S(2)}, u32[]{:S(2)}) collective-permute-start(f32[3,1536]{1,0:T(4,128)S(1)} %pad_maximum_fusion.1), channel_id=1, source_target_pairs={{0,16},{8,24},{16,0},{24,8},{1,17},{9,25},{17,1},{25,9},{2,18},{10... | collective-permute-start | bytes 55304 | tf_op jit(solution)/shard_map/ppermute | solution.py:17
  363.9 5.0 %collective-permute-start.25 = (f32[3,1536]{1,0:T(4,128)S(1)}, f32[3,1536]{1,0:T(4,128)S(1)}, u32[]{:S(2)}, u32[]{:S(2)}) collective-permute-start(f32[3,1536]{1,0:T(4,128)S(1)} %pad_maximum_fusion.1), channel_id=1, source_target_pairs={{0,8},{8,16},{16,24},{24,0},{1,9},{9,17},{17,25},{25,1},{2,10},{10... | collective-permute-start | bytes 55304 | tf_op jit(solution)/shard_map/ppermute | solution.py:17
  391.4 5.4 %collective-permute-start.27 = (f32[3,1536]{1,0:T(4,128)S(1)}, f32[3,1536]{1,0:T(4,128)S(1)}, u32[]{:S(2)}, u32[]{:S(2)}) collective-permute-start(f32[3,1536]{1,0:T(4,128)S(1)} %pad_maximum_fusion.2), channel_id=1, source_target_pairs={{0,64},{32,96},{64,0},{96,32},{1,65},{33,97},{65,1},{97,33},{2,66}... | collective-permute-start | bytes 55304 | tf_op jit(solution)/shard_map/ppermute | solution.py:17
  395.1 5.0 %collective-permute-start.28 = (f32[3,1536]{1,0:T(4,128)S(1)}, f32[3,1536]{1,0:T(4,128)S(1)}, u32[]{:S(2)}, u32[]{:S(2)}) collective-permute-start(f32[3,1536]{1,0:T(4,128)S(1)} %pad_maximum_fusion.2), channel_id=1, source_target_pairs={{0,32},{32,64},{64,96},{96,0},{1,33},{33,65},{65,97},{97,1},{2,34}... | collective-permute-start | bytes 55304 | tf_op jit(solution)/shard_map/ppermute | solution.py:17
  (17 other events, 114.2 us)
Sparse Core Ops, SparseCore 0:
  209.4 85.3 all-gather.1

commit v2 on v1

v2 whole, which is shorter than its diff:
```python
import functools
import jax
import jax.numpy as jnp
from jax import lax
from jax.experimental import pallas as pl
from jax.experimental.pallas import tpu as pltpu
from jax.sharding import Mesh, PartitionSpec as P

BF = jnp.bfloat16
F32 = jnp.float32
AXES = ("x", "z", "y", "core")
SLOTS = 40
FIRST = 512


def shift(value, axis, step):
    size = lax.axis_size(axis)
    return lax.ppermute(value, axis, [(i, (i + step) % size) for i in range(size)])


def dot(a, b):
    return jnp.dot(a, b, preferred_element_type=F32)


def route_kernel(routes_ref, weights_ref, hidden_ref, pick_ref, hi_ref, lo_ref, send_ref):
    tokens, top = routes_ref.shape
    columns = pick_ref.shape[1]
    experts = columns // SLOTS
    ids = lax.broadcasted_iota(jnp.int32, (tokens, experts), 1)
    named = jnp.zeros((tokens, experts), F32)
    gates = jnp.zeros((tokens, experts), F32)
    for k in range(top):
        hit = routes_ref[:, k : k + 1] == ids
        named = named + jnp.where(hit, 1.0, 0.0)
        gates = gates + jnp.where(hit, weights_ref[:, k : k + 1], 0.0)
    row = lax.broadcasted_iota(jnp.int32, (tokens, tokens), 0)
    col = lax.broadcasted_iota(jnp.int32, (tokens, tokens), 1)
    before = jnp.where(col < row, 1.0, 0.0).astype(BF)
    count = dot(before, named.astype(BF))
    expert = lax.broadcasted_iota(jnp.int32, (experts, columns), 0)
    column = lax.broadcasted_iota(jnp.int32, (experts, columns), 1)
    inside = (column >= expert * SLOTS) & (column < expert * SLOTS + SLOTS)
    spread = jnp.where(inside, 1.0, 0.0).astype(BF)
    slot = jnp.sum(jnp.where(inside, column - expert * SLOTS, 0).astype(F32), axis=0, keepdims=True)
    gates_hi = gates.astype(BF)
    gates_lo = (gates - gates_hi.astype(F32)).astype(BF)
    placed = (dot(named.astype(BF), spread) > 0.5) & (dot(count.astype(BF), spread) == slot)
    hi_ref[...] = jnp.where(placed, dot(gates_hi, spread), 0.0).astype(BF)
    lo_ref[...] = jnp.where(placed, dot(gates_lo, spread), 0.0).astype(BF)
    pick = jnp.where(placed, 1.0, 0.0).astype(BF)
    pick_ref[...] = pick
    send_ref[...] = picked(pick, hidden_ref[:, :FIRST]).astype(BF)


def picked(pick, rows):
    return lax.dot_general(pick, rows, (((0,), (0,)), ((), ())), preferred_element_type=F32)


def spread_kernel(pick_ref, h0, h1, h2, h3, send_ref):
    width = h0.shape[1]
    for k, ref in enumerate((h0, h1, h2, h3)):
        send_ref[:, k * width : (k + 1) * width] = picked(pick_ref[...], ref[...]).astype(BF)


def block_of(place_ref, k):
    return 2 * lax.rem(place_ref[0] + 4 - k, 4) + place_ref[1]


def up_kernel(place_ref, a0, a1, a2_top, a2_low, a3, b_ref, w0, w1, w2, w3, sum_ref, out_ref, w_ref, sems):
    step = pl.program_id(0)
    hidden = w0.shape[1]
    width = w0.shape[0] // 8
    second = width - FIRST

    def copies():
        made = []
        for j, w in enumerate((w0, w1, w2, w3)):
            cols = pl.ds(j * hidden, hidden)
            for k in range(4):
                start = pl.multiple_of(block_of(place_ref, k) * width, 128)
                made.append(
                    pltpu.make_async_copy(
                        w.at[pl.ds(start, FIRST), :],
                        w_ref.at[pl.ds(k * FIRST, FIRST), cols],
                        sems.at[j, 2 * k],
                    )
                )
                made.append(
                    pltpu.make_async_copy(
                        w.at[pl.ds(start + FIRST, second), :],
                        w_ref.at[pl.ds(4 * FIRST + k * second, second), cols],
                        sems.at[j, 2 * k + 1],
                    )
                )
        return made

    @pl.when(step == 0)
    def _():
        for copy in copies():
            copy.start()
        for copy in copies():
            copy.wait()

    def total(a2):
        for j in range(4):
            cols = slice(j * hidden, (j + 1) * hidden)
            part = dot(b_ref[...], w_ref[4 * FIRST :, cols])
            for k, ref in enumerate((a0, a1, a2, a3)):
                part = part + dot(ref[...], w_ref[k * FIRST : (k + 1) * FIRST, cols])
            sum_ref[:, cols] = part
            out_ref[:, cols] = part.astype(BF)

    @pl.when(step == 0)
    def _():
        total(a2_top)

    @pl.when(step == 1)
    def _():
        total(a2_low)


def down_kernel(
    place_ref, sum_ref, got_ref, w0, w1, a0, a1_top, a1_low, a2_top, a2_low, a3_top, a3_low, b_ref,
    w_ref, act_ref, sems
):
    step = pl.program_id(0)
    hidden = w0.shape[0]
    width = w0.shape[1] // 8
    second = width - FIRST

    def copies():
        made = []
        for j, w in enumerate((w0, w1)):
            rows = pl.ds(j * hidden, hidden)
            for k in range(4):
                start = pl.multiple_of(block_of(place_ref, k) * width, 128)
                made.append(
                    pltpu.make_async_copy(
                        w.at[:, pl.ds(start, FIRST)],
                        w_ref.at[rows, pl.ds(k * FIRST, FIRST)],
                        sems.at[j, 2 * k],
                    )
                )
                made.append(
                    pltpu.make_async_copy(
                        w.at[:, pl.ds(start + FIRST, second)],
                        w_ref.at[rows, pl.ds(4 * FIRST + k * second, second)],
                        sems.at[j, 2 * k + 1],
                    )
                )
        return made

    @pl.when(step == 0)
    def _():
        for copy in copies():
            copy.start()

    for j in range(2):
        own, got = 2 * j * hidden, 2 * (1 - j) * hidden
        gate = sum_ref[:, own : own + hidden] + got_ref[:, got : got + hidden].astype(F32)
        up = sum_ref[:, own + hidden : own + 2 * hidden] + got_ref[
            :, got + hidden : got + 2 * hidden
        ].astype(F32)
        act_ref[:, j * hidden : (j + 1) * hidden] = (gate / (1.0 + jnp.exp(-gate)) * up).astype(BF)

    @pl.when(step == 0)
    def _():
        for copy in copies():
            copy.wait()

    def out(start, size):
        return dot(act_ref[...], w_ref[:, start : start + size]).astype(BF)

    a0[...] = out(0, FIRST)
    b_ref[...] = out(4 * FIRST, 4 * second)

    @pl.when(step == 0)
    def _():
        for k, ref in ((1, a1_top), (2, a2_top), (3, a3_top)):
            ref[...] = out(k * FIRST, FIRST)

    @pl.when(step == 1)
    def _():
        for k, ref in ((1, a1_low), (2, a2_low), (3, a3_low)):
            ref[...] = out(k * FIRST, FIRST)


def add_kernel(a1, got1, a3, got3, out1, out3):
    out1[...] = (a1[...].astype(F32) + got1[...].astype(F32)).astype(BF)
    out3[...] = (a3[...].astype(F32) + got3[...].astype(F32)).astype(BF)


def ysum_kernel(a0, left_top, left_low, right_top, right_low, out_ref):
    half = left_top.shape[0]
    top = a0[:half].astype(F32) + left_top[...].astype(F32) + right_top[...].astype(F32)
    low = a0[half:].astype(F32) + left_low[...].astype(F32) + right_low[...].astype(F32)
    out_ref[:half] = top.astype(BF)
    out_ref[half:] = low.astype(BF)


def mix_kernel(hi_ref, lo_ref, back_ref, own_ref, p1, p2, p3):
    width = own_ref.shape[1]
    for k, ref in enumerate((own_ref, p1, p2, p3)):
        block = back_ref[:, k * width : (k + 1) * width]
        total = dot(hi_ref[...], block) + dot(lo_ref[...], block)
        ref[...] = total.astype(ref.dtype)


def layer_kernel(
    hidden_ref, hi_ref, lo_ref, back_ref, own_ref, p1, p2, p3, gain_ref, out_ref, scaled_ref, squares_ref
):
    first = dot(hi_ref[...], back_ref[...]) + dot(lo_ref[...], back_ref[...])
    second = own_ref[...] + p1[...].astype(F32) + p2[...].astype(F32) + p3[...].astype(F32)
    squares = 0.0
    for mix, cols in ((first, slice(0, FIRST)), (second, slice(FIRST, hidden_ref.shape[1]))):
        total = hidden_ref[:, cols].astype(F32) + mix
        out_ref[:, cols] = total.astype(BF)
        scaled_ref[:, cols] = (total * gain_ref[:, cols]).astype(BF)
        squares = squares + jnp.sum(total * total, axis=1, keepdims=True)
    squares_ref[...] = squares


def head_kernel(first_ref, rows_ref, head_ref, scale_ref, wanted_ref, stats_ref):
    nodes, parts, tokens, width = rows_ref.shape
    rows = jnp.concatenate([rows_ref[:, p].reshape(nodes * tokens, width) for p in range(parts)], axis=1)
    logits = lax.dot_general(
        rows, head_ref[...], (((1,), (1,)), ((), ())), preferred_element_type=F32
    )
    full = logits * scale_ref[...]
    peak = jnp.max(full, axis=1, keepdims=True)
    total = jnp.sum(jnp.exp(full - peak), axis=1, keepdims=True)
    ids = first_ref[0] + lax.broadcasted_iota(jnp.int32, full.shape, 1)
    target = jnp.sum(jnp.where(ids == wanted_ref[...], full, 0.0), axis=1, keepdims=True)
    lane = lax.broadcasted_iota(jnp.int32, (full.shape[0], 128), 1)
    columns = jnp.where(lane == 0, peak, jnp.where(lane == 1, total, target))
    stats_ref[...] = columns.T[:8]


def merge_kernel(*refs):
    *ins, out_ref = refs
    values = [ref[...] for ref in ins]
    peak = functools.reduce(jnp.maximum, [v[0:1] for v in values])
    total = paired([v[1:2] * jnp.exp(v[0:1] - peak) for v in values])
    target = paired([v[2:3] for v in values])
    row = lax.broadcasted_iota(jnp.int32, out_ref.shape, 0)
    out_ref[...] = jnp.where(row == 0, peak, jnp.where(row == 1, total, target))


def paired(terms):
    if len(terms) == 2:
        return terms[0] + terms[1]
    return (terms[0] + terms[2]) + (terms[1] + terms[3])


def merged(values):
    return pl.pallas_call(
        merge_kernel,
        out_shape=jax.ShapeDtypeStruct(values[0].shape, F32),
        name="merge",
    )(*values)


def like(*shape, dtype=BF):
    return jax.ShapeDtypeStruct(shape, dtype)


def over_nodes(rows):
    nodes = lax.axis_size("x") * lax.axis_size("z")
    cut = rows.reshape(nodes, rows.shape[0] // nodes, rows.shape[1])
    return lax.all_to_all(cut, ("x", "z"), split_axis=0, concat_axis=0, tiled=True).reshape(rows.shape)


def shards(hidden, routes, route_weights, w_gate, w_up, w_down, gain, head, targets, policy_logp):
    tokens, width = hidden.shape
    second = width - FIRST
    y = lax.axis_index("y")
    core = lax.axis_index("core")
    n_node = lax.axis_size("x") * lax.axis_size("z")
    slots = n_node * SLOTS
    half = slots // 2
    model = 8 * width
    hid = w_gate.shape[2]
    vmem = pltpu.CompilerParams(vmem_limit_bytes=48 * 1024 * 1024)
    hbm = pl.BlockSpec(memory_space=pl.ANY)

    near = [hidden[:, FIRST:]]
    near = near + [shift(near[0], "y", k) for k in (1, 2, 3)]
    pick, mix_hi, mix_lo, send_a = pl.pallas_call(
        route_kernel,
        out_shape=(like(tokens, slots), like(tokens, slots), like(tokens, slots), like(slots, FIRST)),
        compiler_params=vmem,
        name="route",
    )(routes, route_weights, hidden)
    a0 = over_nodes(send_a)
    send_b = pl.pallas_call(
        spread_kernel,
        out_shape=like(slots, 4 * second),
        compiler_params=vmem,
        name="spread",
    )(pick, *near)
    gate_mat, up_mat, down_mat = w_gate[0], w_up[0], w_down[0]
    gate_other, up_other, down_other = (shift(w, "core", 1) for w in (gate_mat, up_mat, down_mat))
    a1, a3 = shift(a0, "y", 1), shift(a0, "y", -1)
    b = over_nodes(send_b)
    a2_top, a2_low = shift(a1[:half], "y", 1), shift(a3[half:], "y", -1)

    place = jnp.stack([y, core]).astype(jnp.int32)

    def rows_of(columns):
        return pl.BlockSpec((half, columns), lambda i, place: (i, 0))

    def whole(columns):
        return pl.BlockSpec((half, columns), lambda i, place: (0, 0))

    partial, partial_out = pl.pallas_call(
        up_kernel,
        grid_spec=pltpu.PrefetchScalarGridSpec(
            num_scalar_prefetch=1,
            grid=(2,),
            in_specs=[rows_of(FIRST), rows_of(FIRST), whole(FIRST), whole(FIRST), rows_of(FIRST)]
            + [rows_of(4 * second)]
            + [hbm] * 4,
            out_specs=[rows_of(4 * hid)] * 2,
            scratch_shapes=[pltpu.VMEM((4 * width, 4 * hid), BF), pltpu.SemaphoreType.DMA((4, 8))],
        ),
        out_shape=(like(slots, 4 * hid, dtype=F32), like(slots, 4 * hid)),
        compiler_params=vmem,
        name="gate_up",
    )(place, a0, a1, a2_top, a2_low, a3, b, gate_mat, up_mat, gate_other, up_other)
    partial_got = shift(partial_out, "core", 1)

    a0, a1_top, a1_low, a2_top, a2_low, a3_top, a3_low, b = pl.pallas_call(
        down_kernel,
        grid_spec=pltpu.PrefetchScalarGridSpec(
            num_scalar_prefetch=1,
            grid=(2,),
            in_specs=[rows_of(4 * hid), rows_of(4 * hid), hbm, hbm],
            out_specs=[rows_of(FIRST)] + [whole(FIRST)] * 6 + [rows_of(4 * second)],
            scratch_shapes=[
                pltpu.VMEM((2 * hid, 4 * width), BF),
                pltpu.VMEM((half, 2 * hid), BF),
                pltpu.SemaphoreType.DMA((2, 8)),
            ],
        ),
        out_shape=(like(slots, FIRST),) + (like(half, FIRST),) * 6 + (like(slots, 4 * second),),
        compiler_params=vmem,
        name="down",
    )(place, partial, partial_got, down_mat, down_other)

    got1, got3 = shift(a2_top, "y", -1), shift(a2_low, "y", 1)
    left_low, right_top = shift(a1_low, "y", -1), shift(a3_top, "y", 1)
    back_b = over_nodes(b)
    a1_top, a3_low = pl.pallas_call(
        add_kernel, out_shape=(like(half, FIRST),) * 2, compiler_params=vmem, name="add"
    )(a1_top, got1, a3_low, got3)
    left_top, right_low = shift(a1_top, "y", -1), shift(a3_low, "y", 1)
    summed = pl.pallas_call(
        ysum_kernel, out_shape=like(slots, FIRST), compiler_params=vmem, name="ysum"
    )(a0, left_top, left_low, right_top, right_low)
    back_a = over_nodes(summed)
    own, *others = pl.pallas_call(
        mix_kernel,
        out_shape=(like(tokens, second, dtype=F32),) + (like(tokens, second),) * 3,
        compiler_params=vmem,
        name="mix",
    )(mix_hi, mix_lo, back_b)
    arrived = [shift(part, "y", -k) for k, part in zip((1, 2, 3), others)]
    layer_out, scaled, squares = pl.pallas_call(
        layer_kernel,
        out_shape=(like(tokens, width), like(tokens, width), like(tokens, 1, dtype=F32)),
        compiler_params=vmem,
        name="layer",
    )(hidden, mix_hi, mix_lo, back_a, own, *arrived, gain.reshape(1, width))

    everyone = lax.all_gather(scaled, AXES, axis=0, tiled=True)

    squares = squares.reshape(1, tokens)
    squares = squares + shift(squares, "core", 1)
    squares = paired([squares] + [shift(squares, "y", k) for k in (1, 2, 3)])
    for axis in ("z", "x"):
        here = lax.axis_index(axis)
        size = lax.axis_size(axis)
        order = jnp.arange(size)[:, None, None]
        gathered = jnp.where(order == here, squares[None], 0.0)
        for k in range(1, size):
            from_there = shift(squares, axis, k)
            gathered = gathered + jnp.where(order == (here - k) % size, from_there[None], 0.0)
        squares = gathered.reshape(-1, tokens)
    total_tokens = n_node * tokens
    scale = lax.rsqrt(squares.reshape(total_tokens, 1) / model + 1e-06)

    vocab_rows = head.shape[0]
    first_id = lax.axis_index(AXES) * vocab_rows
    group = 4
    stats = pl.pallas_call(
        head_kernel,
        grid_spec=pltpu.PrefetchScalarGridSpec(
            num_scalar_prefetch=1,
            grid=(n_node // group,),
            in_specs=[
                pl.BlockSpec((group, 8, tokens, width), lambda n, s: (n, 0, 0, 0)),
                pl.BlockSpec((vocab_rows, model), lambda n, s: (0, 0)),
                pl.BlockSpec((group * tokens, 1), lambda n, s: (n, 0)),
                pl.BlockSpec((group * tokens, 1), lambda n, s: (n, 0)),
            ],
            out_specs=pl.BlockSpec((8, group * tokens), lambda n, s: (0, n)),
        ),
        out_shape=like(8, total_tokens, dtype=F32),
        compiler_params=vmem,
        name="head",
    )(
        first_id.reshape(1).astype(jnp.int32),
        everyone.reshape(n_node, 8, tokens, width),
        head,
        scale,
        targets.reshape(total_tokens, 1),
    )
    stats = merged([stats, shift(stats, "core", 1)])
    for axis in ("y", "z", "x"):
        stats = merged([stats] + [shift(stats, axis, k) for k in (1, 2, 3)])
    peak, exp_total, target_logit = stats[0], stats[1], stats[2]
    ref_logp = target_logit - peak - jnp.log(exp_total)
    kl = 0.5 * (policy_logp - ref_logp) * (policy_logp - ref_logp)
    return layer_out, ref_logp, kl


def solution(mesh):
    split = Mesh(mesh.devices.reshape(4, 4, 4, 2), AXES)
    node, local = ("x", "z"), ("y", "core")
    placed = (
        P(node, local),
        P(node, None),
        P(node, None),
        P(node, None, local),
        P(node, None, local),
        P(node, local, None),
        P(local),
        P(AXES, None),
        P(),
        P(),
    )
    return jax.shard_map(
        shards,
        mesh=split,
        in_specs=placed,
        out_specs=(P(node, local), P(), P()),
        check_vma=False,
    )
```

time: 410 us -> 301 us (0.73)
  blocking collectives: 67.9 us -> 0 us
  starting transfers between devices: 41.5 us -> 64.1 us
  local copies, waits for them, and re-layouts: 37.5 us -> 17.3 us
  other arithmetic: 17.2 us -> 1.93 us
  waiting for transfers between devices: 167 us -> 153 us
  Pallas kernels: 62.9 us -> 49.4 us
    all_to_all x1 -> x0, blocking collectives: 67.9 us -> none  [shards(): lax.all_to_all(expert_out.reshape(n_node, SLOTS, wide), ('x', 'z'), split...]
    all_to_all x1 -> x4, waiting for transfers between devices: 54.7 us -> 11.3 us  [over_nodes(): lax.all_to_all(cut, ('x', 'z'), split_axis=0, concat_axis=0, tiled=True)]
    ppermute x30 -> x40, waiting for transfers between devices: 50.6 us -> 79.9 us  [shift(): lax.ppermute(value, axis, [(i, (i + step) % size) for i in range(size)])]
    all_to_all x1 -> x4, starting transfers between devices: 7.92 us -> 25.7 us  [over_nodes(): lax.all_to_all(cut, ('x', 'z'), split_axis=0, concat_axis=0, tiled=True)]
    pallas_call x1, Pallas kernels: 34 us -> 17.8 us  [shards(): pl.pallas_call(head_kernel, grid_spec=pltpu.PrefetchScalarGridSpec(num_sc...]
    pallas_call x3 -> x10, Pallas kernels: 4.31 us -> 12.9 us  [the longest x4 6.11 us: merged(): pl.pallas_call(merge_kernel, out_shape=jax.ShapeDtypeStruct(values[0].sha...]
    add x6 -> x1, other arithmetic: 7.14 us -> 0.01 us  [paired(): return terms[0] + terms[2] + (terms[1] + terms[3])]
    unnamed x34 -> x58, local copies, waits for them, and re-layouts: 20.5 us -> 14 us
  transfers between devices with their start and end apart: 32 -> 45, of which waited for: 29 -> 36; matrix products, arithmetic and copies ran while one was open for 2% -> 2% of each run, Pallas kernels for 4% -> 6%
where the time goes in v2:
time: 301 us; the launch traced here: 300 us
  waiting for transfers between devices  153 us (51%)
  starting transfers between devices  64.1 us (21%)
  Pallas kernels  49.4 us (16%)
  local copies, waits for them, and re-layouts  17.3 us (6%)
  between operations  14.4 us (5%)
    ppermute x40, waiting for transfers between devices, shift(): lax.ppermute(value, axis, [(i, (i + step) % size) for i in range(size)])  79.9 us
    all_gather x1, waiting for transfers between devices, shards(): everyone = lax.all_gather(scaled, AXES, axis=0, tiled=True)  61.3 us
    ppermute x40, starting transfers between devices, shift(): lax.ppermute(value, axis, [(i, (i + step) % size) for i in range(size)])  38.4 us
    all_to_all x4, starting transfers between devices, over_nodes(): lax.all_to_all(cut, ('x', 'z'), split_axis=0, concat_axis=0, tiled=True)  25.7 us
    pallas_call x1, Pallas kernels, shards(): pl.pallas_call(head_kernel, grid_spec=pltpu.PrefetchScalarGridSpec(num_sc...  17.8 us
    unnamed x58, local copies, waits for them, and re-layouts  14 us
    all_to_all x4, waiting for transfers between devices, over_nodes(): lax.all_to_all(cut, ('x', 'z'), split_axis=0, concat_axis=0, tiled=True)  11.3 us
    pallas_call x1, Pallas kernels, shards(): pl.pallas_call(up_kernel, grid_spec=pltpu.PrefetchScalarGridSpec(num_scal...  11.2 us
  transfers between devices with their start and end apart: 45, of which 36 were waited for; matrix products, arithmetic and copies ran while one was open for 2% of the time, Pallas kernels for 6%

profile of v2, /device:TPU:0, one launch (start us, length us, event | category | flops | bytes accessed | tf_op | source)
XLA Modules:
  0.0 299.8 jit_solution(14086292537814004563)
XLA Ops:
  11.9 8.0 %all-to-all-start = ((bf16[16,40,512]{2,1,0:T(8,128)(2,1)}), bf16[16,40,512]{2,1,0:T(8,128)(2,1)S(1)}, u32[]{:S(2)}, u32[]{:S(2)}) async-start(bf16[16,40,512]{2,1,0:T(8,128)(2,1)} %bitcast.2), calls=%async_computation | async-start | bytes 1310720 | tf_op jit(solution)/shard_map/all_to_all | solution.py:270
  20.8 3.0 %collective-permute-start.6 = (bf16[96,384]{1,0:T(8,128)(2,1)S(1)}, bf16[96,384]{1,0:T(8,128)(2,1)S(1)}, u32[]{:S(2)}, u32[]{:S(2)}) collective-permute-start(bf16[96,384]{1,0:T(8,128)(2,1)S(1)} %slice.20.h0), channel_id=1, source_target_pairs={{0,6},{2,0},{4,2},{6,4},{1,7},{3,1},{5,3},{7,5},{8,14},{10,8},{12,... | collective-permute-start | bytes 221192 | tf_op jit(solution)/shard_map/ppermute | solution.py:18
  24.5 3.2 %collective-permute-done.6.h3 = bf16[96,384]{1,0:T(8,128)(2,1)S(1)} collective-permute-done((bf16[96,384]{1,0:T(8,128)(2,1)S(1)}, bf16[96,384]{1,0:T(8,128)(2,1)S(1)}, u32[]{:S(2)}, u32[]{:S(2)}) %collective-permute-start.6) | collective-permute-done | bytes 73760 | tf_op jit(solution)/shard_map/ppermute | solution.py:18
  29.7 3.9 %collective-permute-done.4.h1 = bf16[96,384]{1,0:T(8,128)(2,1)S(1)} collective-permute-done((bf16[96,384]{1,0:T(8,128)(2,1)S(1)}, bf16[96,384]{1,0:T(8,128)(2,1)S(1)}, u32[]{:S(2)}, u32[]{:S(2)}) %collective-permute-start.4) | collective-permute-done | bytes 73760 | tf_op jit(solution)/shard_map/ppermute | solution.py:18
  35.6 7.1 %all-to-all-start.1 = ((bf16[16,40,1536]{2,1,0:T(8,128)(2,1)}), bf16[16,40,1536]{2,1,0:T(8,128)(2,1)S(1)}, u32[]{:S(2)}, u32[]{:S(2)}) async-start(bf16[16,40,1536]{2,1,0:T(8,128)(2,1)} %bitcast.4), calls=%async_computation.1 | async-start | bytes 3932160 | tf_op jit(solution)/shard_map/all_to_all | solution.py:270
  44.9 13.2 %collective-permute-done.2.a3 = bf16[640,512]{1,0:T(8,128)(2,1)S(1)} collective-permute-done((bf16[640,512]{1,0:T(8,128)(2,1)S(1)}, bf16[640,512]{1,0:T(8,128)(2,1)S(1)}, u32[]{:S(2)}, u32[]{:S(2)}) %collective-permute-start.2) | collective-permute-done | bytes 655392 | tf_op jit(solution)/shard_map/ppermute | solution.py:18
  58.8 3.0 collective-permute-start.3
  63.5 3.2 %collective-permute-done.3.a2_low = bf16[320,512]{1,0:T(8,128)(2,1)} collective-permute-done((bf16[320,512]{1,0:T(8,128)(2,1)}, bf16[320,512]{1,0:T(8,128)(2,1)}, u32[]{:S(2)}, u32[]{:S(2)}) %collective-permute-start.3) | collective-permute-done | bytes 327712 | tf_op jit(solution)/shard_map/ppermute | solution.py:18
  66.7 5.3 %collective-permute-done.1.a2_top = bf16[320,512]{1,0:T(8,128)(2,1)} collective-permute-done((bf16[320,512]{1,0:T(8,128)(2,1)}, bf16[320,512]{1,0:T(8,128)(2,1)}, u32[]{:S(2)}, u32[]{:S(2)}) %collective-permute-start.1) | collective-permute-done | bytes 327712 | tf_op jit(solution)/shard_map/ppermute | solution.py:18
  73.1 11.2 %gate_up.1 = (f32[640,1024]{1,0:T(8,128)}, bf16[640,1024]{1,0:T(8,128)(2,1)S(1)}) custom-call(s32[2]{0:T(128)S(1)} %pad_add_fusion.place_ref, bf16[640,512]{1,0:T(8,128)(2,1)S(1)} %bitcast.25, bf16[640,512]{1,0:T(8,128)(2,1)S(1)} %copy-done.2, bf16[320,512]{1,0:T(8,128)(2,1)} %collective-permute-done.1.a2_top, ...), custom_call_target="tpu_custom_call" | custom-call | tf_op jit(solution)/shard_map/gate_up/pallas_call | solution.py:315
  84.3 3.0 %collective-permute-done.9.got_ref = bf16[640,1024]{1,0:T(8,128)(2,1)S(1)} collective-permute-done((bf16[640,1024]{1,0:T(8,128)(2,1)S(1)}, bf16[640,1024]{1,0:T(8,128)(2,1)S(1)}, u32[]{:S(2)}, u32[]{:S(2)}) %collective-permute-start.9) | collective-permute-done | bytes 1310752 | tf_op jit(solution)/shard_map/ppermute | solution.py:18
  87.4 7.5 %down.1 = (bf16[640,512]{1,0:T(8,128)(2,1)S(1)}, bf16[320,512]{1,0:T(8,128)(2,1)S(1)}, bf16[320,512]{1,0:T(8,128)(2,1)S(1)}, bf16[320,512]{1,0:T(8,128)(2,1)S(1)...) custom-call(s32[2]{0:T(128)S(1)} %pad_add_fusion.place_ref, ...), custom_call_target="tpu_custom_call" | custom-call | tf_op jit(solution)/shard_map/down/pallas_call | solution.py:332
  99.7 6.9 %all-to-all-start.3 = ((bf16[16,40,1536]{2,1,0:T(8,128)(2,1)}), bf16[16,40,1536]{2,1,0:T(8,128)(2,1)S(1)}, u32[]{:S(2)}, u32[]{:S(2)}) async-start(bf16[16,40,1536]{2,1,0:T(8,128)(2,1)} %bitcast.27), calls=%async_computation.3 | async-start | bytes 3932160 | tf_op jit(solution)/shard_map/all_to_all | solution.py:270
  110.8 6.8 %collective-permute-done.11.got1 = bf16[320,512]{1,0:T(8,128)(2,1)S(1)} collective-permute-done((bf16[320,512]{1,0:T(8,128)(2,1)}, bf16[320,512]{1,0:T(8,128)(2,1)S(1)}, u32[]{:S(2)}, u32[]{:S(2)}) %collective-permute-start.11) | collective-permute-done | bytes 327712 | tf_op jit(solution)/shard_map/ppermute | solution.py:18
  125.8 4.6 %collective-permute-done.13.left_top = bf16[320,512]{1,0:T(8,128)(2,1)S(1)} collective-permute-done((bf16[320,512]{1,0:T(8,128)(2,1)S(1)}, bf16[320,512]{1,0:T(8,128)(2,1)S(1)}, u32[]{:S(2)}, u32[]{:S(2)}) %collective-permute-start.13) | collective-permute-done | bytes 327712 | tf_op jit(solution)/shard_map/ppermute | solution.py:18
  132.8 3.2 %all-to-all-done.3 = bf16[16,40,1536]{2,1,0:T(8,128)(2,1)S(1)} async-done(((bf16[16,40,1536]{2,1,0:T(8,128)(2,1)}), bf16[16,40,1536]{2,1,0:T(8,128)(2,1)S(1)}, u32[]{:S(2)}, u32[]{:S(2)}) %all-to-all-start.3) | async-done | bytes 1966112 | tf_op jit(solution)/shard_map/all_to_all | solution.py:270
  136.0 3.7 %all-to-all-start.2 = ((bf16[16,40,512]{2,1,0:T(8,128)(2,1)}), bf16[16,40,512]{2,1,0:T(8,128)(2,1)S(1)}, u32[]{:S(2)}, u32[]{:S(2)}) async-start(bf16[16,40,512]{2,1,0:T(8,128)(2,1)} %bitcast.9), calls=%async_computation.2 | async-start | bytes 1310720 | tf_op jit(solution)/shard_map/all_to_all | solution.py:270
  143.2 8.2 %all-to-all-done.2 = bf16[16,40,512]{2,1,0:T(8,128)(2,1)S(1)} async-done(((bf16[16,40,512]{2,1,0:T(8,128)(2,1)}), bf16[16,40,512]{2,1,0:T(8,128)(2,1)S(1)}, u32[]{:S(2)}, u32[]{:S(2)}) %all-to-all-start.2) | async-done | bytes 655392 | tf_op jit(solution)/shard_map/all_to_all | solution.py:270
  172.0 2.9 collective-permute-done.28
  176.3 61.3 %all-gather.2.cloned.1.call-done = bf16[12288,896]{1,0:T(8,128)(2,1)} async-done(((bf16[96,896]{1,0:T(8,128)(2,1)}), bf16[12288,896]{1,0:T(8,128)(2,1)}) %all-gather.2.cloned.1.call-update) | async-done | bytes 22020112 | tf_op jit(solution)/shard_map/all_gather | solution.py:375
  237.6 17.8 %head.1.refs_0_ = f32[8,1536]{1,0:T(8,128)S(1)} custom-call(s32[1]{0:T(128)} %bitcast.13.first_ref, bf16[16,8,96,896]{3,2,1,0:T(8,128)(2,1)} %bitcast.28, bf16[512,7168]{1,0:T(8,128)(2,1)} %head_ref.1, f32[1536,1]{1,0:T(8,128)S(1)} %reshape.381.scale_ref, s32[1536,1]{1,0:T(8,128)S(1)} %reshape.382.wanted_ref), custom_call_target="tpu_custom_call" | custom-call | tf_op jit(solution)/shard_map/head/pallas_call | solution.py:395
  264.1 3.4 %collective-permute-done.32.refs_2_ = f32[8,1536]{1,0:T(8,128)S(1)} collective-permute-done((f32[8,1536]{1,0:T(8,128)}, f32[8,1536]{1,0:T(8,128)S(1)}, u32[]{:S(2)}, u32[]{:S(2)}) %collective-permute-start.32) | collective-permute-done | bytes 49184 | tf_op jit(solution)/shard_map/ppermute | solution.py:18
  274.9 3.6 %collective-permute-done.35.refs_2_ = f32[8,1536]{1,0:T(8,128)S(1)} collective-permute-done((f32[8,1536]{1,0:T(8,128)}, f32[8,1536]{1,0:T(8,128)S(1)}, u32[]{:S(2)}, u32[]{:S(2)}) %collective-permute-start.35) | collective-permute-done | bytes 49184 | tf_op jit(solution)/shard_map/ppermute | solution.py:18
  285.6 3.0 %collective-permute-done.38.refs_2_ = f32[8,1536]{1,0:T(8,128)S(1)} collective-permute-done((f32[8,1536]{1,0:T(8,128)}, f32[8,1536]{1,0:T(8,128)S(1)}, u32[]{:S(2)}, u32[]{:S(2)}) %collective-permute-start.38) | collective-permute-done | bytes 49184 | tf_op jit(solution)/shard_map/ppermute | solution.py:18
  (156 shorter events, 88.5 us)
Async XLA Ops:
  7.2 64.8 %collective-permute-start.7 = (bf16[7168,256]{1,0:T(8,128)(2,1)}, bf16[7168,256]{1,0:T(8,128)(2,1)}, u32[]{:S(2)}, u32[]{:S(2)}) collective-permute-start(bf16[7168,256]{1,0:T(8,128)(2,1)} %bitcast.31), channel_id=1, source_target_pairs={{0,1},{1,0},{2,3},{3,2},{4,5},{5,4},{6,7},{7,6},{8,9},{9,8},{10,11... | collective-permute-start | bytes 11010056 | tf_op jit(solution)/shard_map/ppermute | solution.py:18
  7.3 64.7 %collective-permute-start.8 = (bf16[7168,256]{1,0:T(8,128)(2,1)}, bf16[7168,256]{1,0:T(8,128)(2,1)}, u32[]{:S(2)}, u32[]{:S(2)}) collective-permute-start(bf16[7168,256]{1,0:T(8,128)(2,1)} %bitcast.33), channel_id=1, source_target_pairs={{0,1},{1,0},{2,3},{3,2},{4,5},{5,4},{6,7},{7,6},{8,9},{9,8},{10,11... | collective-permute-start | bytes 11010056 | tf_op jit(solution)/shard_map/ppermute | solution.py:18
  11.9 23.8 %all-to-all-start = ((bf16[16,40,512]{2,1,0:T(8,128)(2,1)}), bf16[16,40,512]{2,1,0:T(8,128)(2,1)S(1)}, u32[]{:S(2)}, u32[]{:S(2)}) async-start(bf16[16,40,512]{2,1,0:T(8,128)(2,1)} %bitcast.2), calls=%async_computation | async-start | bytes 1310720 | tf_op jit(solution)/shard_map/all_to_all | solution.py:270
  19.8 64.5 %collective-permute-start.10 = (bf16[256,7168]{1,0:T(8,128)(2,1)}, bf16[256,7168]{1,0:T(8,128)(2,1)}, u32[]{:S(2)}, u32[]{:S(2)}) collective-permute-start(bf16[256,7168]{1,0:T(8,128)(2,1)} %bitcast.29), channel_id=1, source_target_pairs={{0,1},{1,0},{2,3},{3,2},{4,5},{5,4},{6,7},{7,6},{8,9},{9,8},{10,11... | collective-permute-start | bytes 11010056 | tf_op jit(solution)/shard_map/ppermute | solution.py:18
  20.8 6.8 %collective-permute-start.6 = (bf16[96,384]{1,0:T(8,128)(2,1)S(1)}, bf16[96,384]{1,0:T(8,128)(2,1)S(1)}, u32[]{:S(2)}, u32[]{:S(2)}) collective-permute-start(bf16[96,384]{1,0:T(8,128)(2,1)S(1)} %slice.20.h0), channel_id=1, source_target_pairs={{0,6},{2,0},{4,2},{6,4},{1,7},{3,1},{5,3},{7,5},{8,14},{10,8},{12,... | collective-permute-start | bytes 221192 | tf_op jit(solution)/shard_map/ppermute | solution.py:18
  23.8 5.9 %collective-permute-start.5 = (bf16[96,384]{1,0:T(8,128)(2,1)S(1)}, bf16[96,384]{1,0:T(8,128)(2,1)S(1)}, u32[]{:S(2)}, u32[]{:S(2)}) collective-permute-start(bf16[96,384]{1,0:T(8,128)(2,1)S(1)} %slice.20.h0), channel_id=1, source_target_pairs={{0,4},{2,6},{4,0},{6,2},{1,5},{3,7},{5,1},{7,3},{8,12},{10,14},{12... | collective-permute-start | bytes 221192 | tf_op jit(solution)/shard_map/ppermute | solution.py:18
  27.6 6.0 %collective-permute-start.4 = (bf16[96,384]{1,0:T(8,128)(2,1)S(1)}, bf16[96,384]{1,0:T(8,128)(2,1)S(1)}, u32[]{:S(2)}, u32[]{:S(2)}) collective-permute-start(bf16[96,384]{1,0:T(8,128)(2,1)S(1)} %slice.20.h0), channel_id=1, source_target_pairs={{0,2},{2,4},{4,6},{6,0},{1,3},{3,5},{5,7},{7,1},{8,10},{10,12},{12... | collective-permute-start | bytes 221192 | tf_op jit(solution)/shard_map/ppermute | solution.py:18
  35.6 36.3 %all-to-all-start.1 = ((bf16[16,40,1536]{2,1,0:T(8,128)(2,1)}), bf16[16,40,1536]{2,1,0:T(8,128)(2,1)S(1)}, u32[]{:S(2)}, u32[]{:S(2)}) async-start(bf16[16,40,1536]{2,1,0:T(8,128)(2,1)} %bitcast.4), calls=%async_computation.1 | async-start | bytes 3932160 | tf_op jit(solution)/shard_map/all_to_all | solution.py:270
  42.8 15.3 %collective-permute-start.2 = (bf16[640,512]{1,0:T(8,128)(2,1)S(1)}, bf16[640,512]{1,0:T(8,128)(2,1)S(1)}, u32[]{:S(2)}, u32[]{:S(2)}) collective-permute-start(bf16[640,512]{1,0:T(8,128)(2,1)S(1)} %bitcast.23), channel_id=1, source_target_pairs={{0,6},{2,0},{4,2},{6,4},{1,7},{3,1},{5,3},{7,5},{8,14},{10,8},{12,... | collective-permute-start | bytes 1966088 | tf_op jit(solution)/shard_map/ppermute | solution.py:18
  44.9 16.9 %collective-permute-start = (bf16[640,512]{1,0:T(8,128)(2,1)S(1)}, bf16[640,512]{1,0:T(8,128)(2,1)S(1)}, u32[]{:S(2)}, u32[]{:S(2)}) collective-permute-start(bf16[640,512]{1,0:T(8,128)(2,1)S(1)} %bitcast.24), channel_id=1, source_target_pairs={{0,2},{2,4},{4,6},{6,0},{1,3},{3,5},{5,7},{7,1},{8,10},{10,12},{12... | collective-permute-start | bytes 1966088 | tf_op jit(solution)/shard_map/ppermute | solution.py:18
  58.8 7.9 %collective-permute-start.3 = (bf16[320,512]{1,0:T(8,128)(2,1)}, bf16[320,512]{1,0:T(8,128)(2,1)}, u32[]{:S(2)}, u32[]{:S(2)}) collective-permute-start(bf16[320,512]{1,0:T(8,128)(2,1)} %slice.25), channel_id=1, source_target_pairs={{0,6},{2,0},{4,2},{6,4},{1,7},{3,1},{5,3},{7,5},{8,14},{10,8},{12,... | collective-permute-start | bytes 983048 | tf_op jit(solution)/shard_map/ppermute | solution.py:18
  63.4 8.6 %collective-permute-start.1 = (bf16[320,512]{1,0:T(8,128)(2,1)}, bf16[320,512]{1,0:T(8,128)(2,1)}, u32[]{:S(2)}, u32[]{:S(2)}) collective-permute-start(bf16[320,512]{1,0:T(8,128)(2,1)} %slice.24), channel_id=1, source_target_pairs={{0,2},{2,4},{4,6},{6,0},{1,3},{3,5},{5,7},{7,1},{8,10},{10,12},{12... | collective-permute-start | bytes 983048 | tf_op jit(solution)/shard_map/ppermute | solution.py:18
  99.7 36.2 %all-to-all-start.3 = ((bf16[16,40,1536]{2,1,0:T(8,128)(2,1)}), bf16[16,40,1536]{2,1,0:T(8,128)(2,1)S(1)}, u32[]{:S(2)}, u32[]{:S(2)}) async-start(bf16[16,40,1536]{2,1,0:T(8,128)(2,1)} %bitcast.27), calls=%async_computation.3 | async-start | bytes 3932160 | tf_op jit(solution)/shard_map/all_to_all | solution.py:270
  106.6 10.9 %collective-permute-start.11 = (bf16[320,512]{1,0:T(8,128)(2,1)}, bf16[320,512]{1,0:T(8,128)(2,1)S(1)}, u32[]{:S(2)}, u32[]{:S(2)}) collective-permute-start(bf16[320,512]{1,0:T(8,128)(2,1)} %copy-done.13), channel_id=1, source_target_pairs={{0,6},{2,0},{4,2},{6,4},{1,7},{3,1},{5,3},{7,5},{8,14},{10,8},{12,... | collective-permute-start | bytes 983048 | tf_op jit(solution)/shard_map/ppermute | solution.py:18
  106.7 12.1 %collective-permute-start.12 = (bf16[320,512]{1,0:T(8,128)(2,1)}, bf16[320,512]{1,0:T(8,128)(2,1)S(1)}, u32[]{:S(2)}, u32[]{:S(2)}) collective-permute-start(bf16[320,512]{1,0:T(8,128)(2,1)} %copy-done.12), channel_id=1, source_target_pairs={{0,2},{2,4},{4,6},{6,0},{1,3},{3,5},{5,7},{7,1},{8,10},{10,12},{12... | collective-permute-start | bytes 983048 | tf_op jit(solution)/shard_map/ppermute | solution.py:18
  108.7 15.8 %collective-permute-start.14 = (bf16[320,512]{1,0:T(8,128)(2,1)}, bf16[320,512]{1,0:T(8,128)(2,1)S(1)}, u32[]{:S(2)}, u32[]{:S(2)}) collective-permute-start(bf16[320,512]{1,0:T(8,128)(2,1)} %copy-done.11), channel_id=1, source_target_pairs={{0,6},{2,0},{4,2},{6,4},{1,7},{3,1},{5,3},{7,5},{8,14},{10,8},{12,... | collective-permute-start | bytes 983048 | tf_op jit(solution)/shard_map/ppermute | solution.py:18
  110.0 15.8 %collective-permute-start.15 = (bf16[320,512]{1,0:T(8,128)(2,1)}, bf16[320,512]{1,0:T(8,128)(2,1)S(1)}, u32[]{:S(2)}, u32[]{:S(2)}) collective-permute-start(bf16[320,512]{1,0:T(8,128)(2,1)} %copy-done.10), channel_id=1, source_target_pairs={{0,2},{2,4},{4,6},{6,0},{1,3},{3,5},{5,7},{7,1},{8,10},{10,12},{12... | collective-permute-start | bytes 983048 | tf_op jit(solution)/shard_map/ppermute | solution.py:18
  120.9 9.5 %collective-permute-start.13 = (bf16[320,512]{1,0:T(8,128)(2,1)S(1)}, bf16[320,512]{1,0:T(8,128)(2,1)S(1)}, u32[]{:S(2)}, u32[]{:S(2)}) collective-permute-start(bf16[320,512]{1,0:T(8,128)(2,1)S(1)} %get-tuple-element.37), channel_id=1, source_target_pairs={{0,6},{2,0},{4,2},{6,4},{1,7},{3,1},{5,3},{7,5},{8,14},{10,8},{12,... | collective-permute-start | bytes 983048 | tf_op jit(solution)/shard_map/ppermute | solution.py:18
  121.0 10.7 %collective-permute-start.16 = (bf16[320,512]{1,0:T(8,128)(2,1)S(1)}, bf16[320,512]{1,0:T(8,128)(2,1)S(1)}, u32[]{:S(2)}, u32[]{:S(2)}) collective-permute-start(bf16[320,512]{1,0:T(8,128)(2,1)S(1)} %get-tuple-element.40), channel_id=1, source_target_pairs={{0,2},{2,4},{4,6},{6,0},{1,3},{3,5},{5,7},{7,1},{8,10},{10,12},{12... | collective-permute-start | bytes 983048 | tf_op jit(solution)/shard_map/ppermute | solution.py:18
  136.0 15.3 %all-to-all-start.2 = ((bf16[16,40,512]{2,1,0:T(8,128)(2,1)}), bf16[16,40,512]{2,1,0:T(8,128)(2,1)S(1)}, u32[]{:S(2)}, u32[]{:S(2)}) async-start(bf16[16,40,512]{2,1,0:T(8,128)(2,1)} %bitcast.9), calls=%async_computation.2 | async-start | bytes 1310720 | tf_op jit(solution)/shard_map/all_to_all | solution.py:270
  139.7 98.0 %all-gather.2.cloned.1.call-start = ((), (), s32[]{:S(2)}) async-start(), calls=%async_computation.4 | async-start | bytes 22192128 | tf_op jit(solution)/shard_map/all_gather | solution.py:375
  140.6 10.8 %collective-permute-start.17 = (bf16[96,384]{1,0:T(8,128)(2,1)S(1)}, bf16[96,384]{1,0:T(8,128)(2,1)S(1)}, u32[]{:S(2)}, u32[]{:S(2)}) collective-permute-start(bf16[96,384]{1,0:T(8,128)(2,1)S(1)} %get-tuple-element.43), channel_id=1, source_target_pairs={{0,6},{2,0},{4,2},{6,4},{1,7},{3,1},{5,3},{7,5},{8,14},{10,8},{12,... | collective-permute-start | bytes 221192 | tf_op jit(solution)/shard_map/ppermute | solution.py:18
  140.8 10.5 %collective-permute-start.18 = (bf16[96,384]{1,0:T(8,128)(2,1)S(1)}, bf16[96,384]{1,0:T(8,128)(2,1)S(1)}, u32[]{:S(2)}, u32[]{:S(2)}) collective-permute-start(bf16[96,384]{1,0:T(8,128)(2,1)S(1)} %get-tuple-element.44), channel_id=1, source_target_pairs={{0,4},{2,6},{4,0},{6,2},{1,5},{3,7},{5,1},{7,3},{8,12},{10,14},{12... | collective-permute-start | bytes 221192 | tf_op jit(solution)/shard_map/ppermute | solution.py:18
  143.2 8.2 %collective-permute-start.19 = (bf16[96,384]{1,0:T(8,128)(2,1)S(1)}, bf16[96,384]{1,0:T(8,128)(2,1)S(1)}, u32[]{:S(2)}, u32[]{:S(2)}) collective-permute-start(bf16[96,384]{1,0:T(8,128)(2,1)S(1)} %get-tuple-element.45), channel_id=1, source_target_pairs={{0,2},{2,4},{4,6},{6,0},{1,3},{3,5},{5,7},{7,1},{8,10},{10,12},{12... | collective-permute-start | bytes 221192 | tf_op jit(solution)/shard_map/ppermute | solution.py:18
  (49 other events, 278.2 us)
Sparse Core Ops, SparseCore 0:
  152.6 84.9 all-gather.1

commit v3 on v2

--- a/solution.py
+++ b/solution.py
@@ -11,6 +11,7 @@
 AXES = ("x", "z", "y", "core")
 SLOTS = 40
 FIRST = 512
+VMEM = 48
 
 
 def shift(value, axis, step):
@@ -20,6 +21,22 @@
 
 def dot(a, b):
     return jnp.dot(a, b, preferred_element_type=F32)
+
+
+def near_kernel(hidden_ref, gain_ref, near_ref):
+    tokens, width = hidden_ref.shape
+    second = near_ref.shape[1]
+    near_ref[:tokens] = hidden_ref[:, FIRST:]
+    gain = gain_ref[...]
+    hi = gain.astype(BF).astype(F32)
+    rows = jnp.zeros((near_ref.shape[0] - tokens, second), F32)
+    row = lax.broadcasted_iota(jnp.int32, rows.shape, 0)
+    for i, part in enumerate((hi, gain - hi)):
+        for j, start in enumerate(range(0, width, second)):
+            piece = part[:, start : start + second]
+            piece = jnp.pad(piece, ((0, 0), (0, second - piece.shape[1])))
+            rows = jnp.where(row == 4 * i + j, piece, rows)
+    near_ref[tokens:] = rows.astype(BF)
 
 
 def route_kernel(routes_ref, weights_ref, hidden_ref, pick_ref, hi_ref, lo_ref, send_ref):
@@ -56,10 +73,17 @@
     return lax.dot_general(pick, rows, (((0,), (0,)), ((), ())), preferred_element_type=F32)
 
 
-def spread_kernel(pick_ref, h0, h1, h2, h3, send_ref):
-    width = h0.shape[1]
+def spread_kernel(pick_ref, h0, h1, h2, h3, send_ref, inverse_ref):
+    tokens = pick_ref.shape[0]
+    second = h0.shape[1]
+    width = inverse_ref.shape[1]
     for k, ref in enumerate((h0, h1, h2, h3)):
-        send_ref[:, k * width : (k + 1) * width] = picked(pick_ref[...], ref[...]).astype(BF)
+        send_ref[:, k * second : (k + 1) * second] = picked(pick_ref[...], ref[:tokens]).astype(BF)
+        rows = ref[tokens:].astype(F32)
+        for j, start in enumerate(range(0, width, second)):
+            size = min(second, width - start)
+            gain = rows[j : j + 1, :size] + rows[4 + j : 5 + j, :size]
+            inverse_ref[k : k + 1, start : start + size] = 1.0 / (gain * gain)
 
 
 def block_of(place_ref, k):
@@ -206,44 +230,116 @@
         ref[...] = total.astype(ref.dtype)
 
 
-def layer_kernel(
-    hidden_ref, hi_ref, lo_ref, back_ref, own_ref, p1, p2, p3, gain_ref, out_ref, scaled_ref, squares_ref
-):
+def layer_kernel(hidden_ref, hi_ref, lo_ref, back_ref, own_ref, p1, p2, p3, gain_ref, out_ref, scaled_ref):
     first = dot(hi_ref[...], back_ref[...]) + dot(lo_ref[...], back_ref[...])
     second = own_ref[...] + p1[...].astype(F32) + p2[...].astype(F32) + p3[...].astype(F32)
-    squares = 0.0
     for mix, cols in ((first, slice(0, FIRST)), (second, slice(FIRST, hidden_ref.shape[1]))):
         total = hidden_ref[:, cols].astype(F32) + mix
         out_ref[:, cols] = total.astype(BF)
         scaled_ref[:, cols] = (total * gain_ref[:, cols]).astype(BF)
-        squares = squares + jnp.sum(total * total, axis=1, keepdims=True)
-    squares_ref[...] = squares
-
-
-def head_kernel(first_ref, rows_ref, head_ref, scale_ref, wanted_ref, stats_ref):
+
+
+def squares_of(rows, inverse):
+    total = jnp.zeros((rows.shape[0], 128), F32)
+    for c in range(0, rows.shape[1], 128):
+        value = rows[:, c : c + 128].astype(F32)
+        total = total + value * value * inverse[:, c : c + 128]
+    return total
+
+
+def half_head_kernel(place_ref, inverse_ref, w0, w1, *refs):
+    *pieces, own_ref, other_ref, w_ref, rows_ref, sems = refs
+    vocab = w0.shape[0]
+    tokens, width = pieces[0].shape[2:]
+    line_a, behind_a, far_a1, far_a2, ahead_a = pieces[:5]
+    line_b, behind_b, far_b1, far_b2, ahead_b = pieces[5:]
+
+    copies = []
+    for j, w in enumerate((w0, w1)):
+        for k in range(4):
+            start = pl.multiple_of(block_of(place_ref, k) * width, 128)
+            copies.append(
+                pltpu.make_async_copy(
+                    w.at[:, pl.ds(start, width)],
+                    w_ref.at[pl.ds(j * vocab, vocab), pl.ds(k * width, width)],
+                    sems.at[j, k],
+                )
+            )
+    for copy in copies:
+        copy.start()
+
+    def piece_of(line, behind, far1, far2, ahead, along, across):
+        if along == 2:
+            return (far1, across) if across < 2 else (far2, across - 2)
+        return ({0: line, 1: behind, 3: ahead}[along], across)
+
+    for back_x in range(4):
+        for back_z in range(4):
+            at = (back_x * 4 + back_z) * tokens
+            squares = 0.0
+            for ref, i, base in (
+                piece_of(line_a, behind_a, far_a1, far_a2, ahead_a, back_z, back_x) + (0,),
+                piece_of(line_b, behind_b, far_b1, far_b2, ahead_b, back_x, back_z) + (2,),
+            ):
+                for k in range(2):
+                    rows = ref[i, k]
+                    first = (base + k) * width
+                    rows_ref[at : at + tokens, first : first + width] = rows
+                    squares = squares + squares_of(rows, inverse_ref[base + k : base + k + 1])
+            own_ref[at : at + tokens, vocab:] = squares
+            other_ref[at : at + tokens, vocab:] = squares
+    for copy in copies:
+        copy.wait()
+    for at in range(0, rows_ref.shape[0], 384):
+        for j, ref in ((1, other_ref), (0, own_ref)):
+            ref[at : at + 384, :vocab] = lax.dot_general(
+                rows_ref[at : at + 384],
+                w_ref[j * vocab : (j + 1) * vocab, :],
+                (((1,), (1,)), ((), ())),
+                preferred_element_type=F32,
+            )
+
+
+def columns_of(full, ids, wanted):
+    peak = jnp.max(full, axis=1, keepdims=True)
+    total = jnp.sum(jnp.exp(full - peak), axis=1, keepdims=True)
+    target = jnp.sum(jnp.where(ids == wanted, full, 0.0), axis=1, keepdims=True)
+    lane = lax.broadcasted_iota(jnp.int32, (full.shape[0], 128), 1)
+    return jnp.where(lane == 0, peak, jnp.where(lane == 1, total, target)).T
+
+
+def whole_head_kernel(model, first_ref, place_ref, rows_ref, head_ref, own_ref, other_ref, wanted_ref, stats_ref):
     nodes, parts, tokens, width = rows_ref.shape
     rows = jnp.concatenate([rows_ref[:, p].reshape(nodes * tokens, width) for p in range(parts)], axis=1)
-    logits = lax.dot_general(
-        rows, head_ref[...], (((1,), (1,)), ((), ())), preferred_element_type=F32
-    )
-    full = logits * scale_ref[...]
-    peak = jnp.max(full, axis=1, keepdims=True)
-    total = jnp.sum(jnp.exp(full - peak), axis=1, keepdims=True)
+    logits = lax.dot_general(rows, head_ref[...], (((1,), (1,)), ((), ())), preferred_element_type=F32)
+    squares = 0.0
+    for p in range(parts):
+        k = lax.rem(place_ref[0] + 4 - p // 2, 4)
+        mine = place_ref[1] == p % 2
+        inverse = jnp.where(mine, own_ref[pl.ds(k, 1), :], other_ref[pl.ds(k, 1), :])
+        squares = squares + squares_of(rows[:, p * width : (p + 1) * width], inverse)
+    scale = lax.rsqrt(jnp.sum(squares, axis=1, keepdims=True) / model + 1e-06)
+    ids = first_ref[0] + lax.broadcasted_iota(jnp.int32, logits.shape, 1)
+    columns = columns_of(logits * scale, ids, wanted_ref[...])
+    stats_ref[...] = columns[:8]
+
+
+def stats_kernel(model, first_ref, order_ref, own_ref, got_ref, wanted_ref, whole_ref, stats_ref):
+    vocab = own_ref.shape[1] - 128
+    nodes, tokens, _ = wanted_ref.shape
+    wanted = jnp.concatenate([wanted_ref[order_ref[i]] for i in range(nodes)], axis=0)
+    squares = jnp.sum(own_ref[:, vocab:] + got_ref[:, vocab:], axis=1, keepdims=True)
+    scale = lax.rsqrt(squares / model + 1e-06)
+    full = (own_ref[:, :vocab] + got_ref[:, :vocab]) * scale
     ids = first_ref[0] + lax.broadcasted_iota(jnp.int32, full.shape, 1)
-    target = jnp.sum(jnp.where(ids == wanted_ref[...], full, 0.0), axis=1, keepdims=True)
-    lane = lax.broadcasted_iota(jnp.int32, (full.shape[0], 128), 1)
-    columns = jnp.where(lane == 0, peak, jnp.where(lane == 1, total, target))
-    stats_ref[...] = columns.T[:8]
-
-
-def merge_kernel(*refs):
-    *ins, out_ref = refs
-    values = [ref[...] for ref in ins]
-    peak = functools.reduce(jnp.maximum, [v[0:1] for v in values])
-    total = paired([v[1:2] * jnp.exp(v[0:1] - peak) for v in values])
-    target = paired([v[2:3] for v in values])
-    row = lax.broadcasted_iota(jnp.int32, out_ref.shape, 0)
-    out_ref[...] = jnp.where(row == 0, peak, jnp.where(row == 1, total, target))
+    columns = columns_of(full, ids, wanted)
+    stats_ref[...] = jnp.zeros_like(stats_ref)
+    for i in range(nodes):
+        lanes = slice(i * tokens, (i + 1) * tokens)
+        for j in range(3):
+            stats_ref[j * nodes + i : j * nodes + i + 1, :tokens] = whole_ref[j : j + 1, lanes]
+            row = j * nodes + order_ref[i]
+            stats_ref[pl.ds(row, 1), 64 : 64 + tokens] = columns[j : j + 1, lanes]
 
 
 def paired(terms):
@@ -252,16 +348,47 @@
     return (terms[0] + terms[2]) + (terms[1] + terms[3])
 
 
-def merged(values):
-    return pl.pallas_call(
-        merge_kernel,
-        out_shape=jax.ShapeDtypeStruct(values[0].shape, F32),
-        name="merge",
-    )(*values)
+def combined(refs):
+    third = refs[0].shape[0] // 3
+    peaks = [ref[:third] for ref in refs]
+    peak = functools.reduce(jnp.maximum, peaks)
+    total = paired([ref[third : 2 * third] * jnp.exp(own - peak) for ref, own in zip(refs, peaks)])
+    return peak, total, paired([ref[2 * third :] for ref in refs])
+
+
+def merge_kernel(*refs):
+    *ins, out_ref = refs
+    third = out_ref.shape[0] // 3
+    for j, value in enumerate(combined(ins)):
+        out_ref[j * third : (j + 1) * third] = value
+
+
+def final_kernel(*refs):
+    *ins, policy_ref, logp_ref, kl_ref = refs
+    half = policy_ref.shape[1] // 2
+    peak, total, target = combined(ins)
+    logp = target - peak - jnp.log(total)
+    logp = jnp.concatenate([logp[:, :half], logp[:, 64 : 64 + half]], axis=1)
+    logp_ref[...] = logp
+    kl_ref[...] = 0.5 * (policy_ref[...] - logp) * (policy_ref[...] - logp)
+
+
+def neighbours(stats, axis):
+    return [stats] + [shift(stats, axis, k) for k in range(1, lax.axis_size(axis))]
+
+
+def ring(block, axis):
+    half = block.shape[0] // 2
+    behind, ahead = shift(block, axis, 1), shift(block, axis, -1)
+    return behind, shift(behind[:half], axis, 1), shift(ahead[half:], axis, -1), ahead
 
 
 def like(*shape, dtype=BF):
     return jax.ShapeDtypeStruct(shape, dtype)
+
+
+def vmem(mib):
+    return pltpu.CompilerParams(vmem_limit_bytes=mib * 1024 * 1024)
 
 
 def over_nodes(rows):
@@ -280,30 +407,36 @@
     half = slots // 2
     model = 8 * width
     hid = w_gate.shape[2]
-    vmem = pltpu.CompilerParams(vmem_limit_bytes=48 * 1024 * 1024)
     hbm = pl.BlockSpec(memory_space=pl.ANY)
-
-    near = [hidden[:, FIRST:]]
+    in_vmem = pl.BlockSpec(memory_space=pltpu.VMEM)
+
+    near_own = pl.pallas_call(
+        near_kernel, out_shape=like(tokens + 16, second), compiler_params=vmem(VMEM), name="near"
+    )(hidden, gain.reshape(1, width))
+    near = [near_own]
     near = near + [shift(near[0], "y", k) for k in (1, 2, 3)]
     pick, mix_hi, mix_lo, send_a = pl.pallas_call(
         route_kernel,
         out_shape=(like(tokens, slots), like(tokens, slots), like(tokens, slots), like(slots, FIRST)),
-        compiler_params=vmem,
+        compiler_params=vmem(VMEM),
         name="route",
     )(routes, route_weights, hidden)
     a0 = over_nodes(send_a)
-    send_b = pl.pallas_call(
+    send_b, inverse = pl.pallas_call(
         spread_kernel,
-        out_shape=like(slots, 4 * second),
-        compiler_params=vmem,
+        out_shape=(like(slots, 4 * second), like(4, width, dtype=F32)),
+        compiler_params=vmem(VMEM),
         name="spread",
     )(pick, *near)
     gate_mat, up_mat, down_mat = w_gate[0], w_up[0], w_down[0]
     gate_other, up_other, down_other = (shift(w, "core", 1) for w in (gate_mat, up_mat, down_mat))
+    a0, send_b = lax.optimization_barrier((a0, send_b))
     a1, a3 = shift(a0, "y", 1), shift(a0, "y", -1)
     b = over_nodes(send_b)
     a2_top, a2_low = shift(a1[:half], "y", 1), shift(a3[half:], "y", -1)
 
+    head_other = shift(head, "core", 1)
+    inverse_other = shift(inverse, "core", 1)
     place = jnp.stack([y, core]).astype(jnp.int32)
 
     def rows_of(columns):
@@ -324,7 +457,7 @@
             scratch_shapes=[pltpu.VMEM((4 * width, 4 * hid), BF), pltpu.SemaphoreType.DMA((4, 8))],
         ),
         out_shape=(like(slots, 4 * hid, dtype=F32), like(slots, 4 * hid)),
-        compiler_params=vmem,
+        compiler_params=vmem(VMEM),
         name="gate_up",
     )(place, a0, a1, a2_top, a2_low, a3, b, gate_mat, up_mat, gate_other, up_other)
     partial_got = shift(partial_out, "core", 1)
@@ -343,7 +476,7 @@
             ],
         ),
         out_shape=(like(slots, FIRST),) + (like(half, FIRST),) * 6 + (like(slots, 4 * second),),
-        compiler_params=vmem,
+        compiler_params=vmem(58),
         name="down",
     )(place, partial, partial_got, down_mat, down_other)
 
@@ -351,77 +484,112 @@
     left_low, right_top = shift(a1_low, "y", -1), shift(a3_top, "y", 1)
     back_b = over_nodes(b)
     a1_top, a3_low = pl.pallas_call(
-        add_kernel, out_shape=(like(half, FIRST),) * 2, compiler_params=vmem, name="add"
+        add_kernel, out_shape=(like(half, FIRST),) * 2, compiler_params=vmem(VMEM), name="add"
     )(a1_top, got1, a3_low, got3)
     left_top, right_low = shift(a1_top, "y", -1), shift(a3_low, "y", 1)
     summed = pl.pallas_call(
-        ysum_kernel, out_shape=like(slots, FIRST), compiler_params=vmem, name="ysum"
+        ysum_kernel, out_shape=like(slots, FIRST), compiler_params=vmem(VMEM), name="ysum"
     )(a0, left_top, left_low, right_top, right_low)
     back_a = over_nodes(summed)
     own, *others = pl.pallas_call(
         mix_kernel,
         out_shape=(like(tokens, second, dtype=F32),) + (like(tokens, second),) * 3,
-        compiler_params=vmem,
+        compiler_params=vmem(VMEM),
         name="mix",
     )(mix_hi, mix_lo, back_b)
     arrived = [shift(part, "y", -k) for k, part in zip((1, 2, 3), others)]
-    layer_out, scaled, squares = pl.pallas_call(
+    layer_out, scaled = pl.pallas_call(
         layer_kernel,
-        out_shape=(like(tokens, width), like(tokens, width), like(tokens, 1, dtype=F32)),
-        compiler_params=vmem,
+        out_shape=(like(tokens, width), like(tokens, width)),
+        compiler_params=vmem(VMEM),
         name="layer",
     )(hidden, mix_hi, mix_lo, back_a, own, *arrived, gain.reshape(1, width))
 
-    everyone = lax.all_gather(scaled, AXES, axis=0, tiled=True)
-
-    squares = squares.reshape(1, tokens)
-    squares = squares + shift(squares, "core", 1)
-    squares = paired([squares] + [shift(squares, "y", k) for k in (1, 2, 3)])
-    for axis in ("z", "x"):
-        here = lax.axis_index(axis)
-        size = lax.axis_size(axis)
-        order = jnp.arange(size)[:, None, None]
-        gathered = jnp.where(order == here, squares[None], 0.0)
-        for k in range(1, size):
-            from_there = shift(squares, axis, k)
-            gathered = gathered + jnp.where(order == (here - k) % size, from_there[None], 0.0)
-        squares = gathered.reshape(-1, tokens)
-    total_tokens = n_node * tokens
-    scale = lax.rsqrt(squares.reshape(total_tokens, 1) / model + 1e-06)
+    part = tokens // 2
+    everyone = lax.all_gather(scaled[:part], AXES, axis=0, tiled=True)
+    by_y = [scaled[part:]]
+    by_y = by_y + [shift(by_y[0], "y", k) for k in (1, 2, 3)]
+    part_a, part_b = jnp.stack(by_y[:2]), jnp.stack(by_y[2:])
+    behind_a, far_a1, far_a2, ahead_a = ring(part_a, "x")
+    behind_b, far_b1, far_b2, ahead_b = ring(part_b, "z")
+    line_a = jnp.stack([part_a, behind_a, jnp.concatenate([far_a1, far_a2]), ahead_a])
+    line_b = jnp.stack([part_b, behind_b, jnp.concatenate([far_b1, far_b2]), ahead_b])
+    behind_a, far_a1, far_a2, ahead_a = ring(line_a, "z")
+    behind_b, far_b1, far_b2, ahead_b = ring(line_b, "x")
 
     vocab_rows = head.shape[0]
-    first_id = lax.axis_index(AXES) * vocab_rows
-    group = 4
-    stats = pl.pallas_call(
-        head_kernel,
+    first_id = (lax.axis_index(AXES) * vocab_rows).reshape(1).astype(jnp.int32)
+    x, z = lax.axis_index("x"), lax.axis_index("z")
+    order = [((x - i) % 4) * 4 + (z - j) % 4 for i in range(4) for j in range(4)]
+    wanted = targets.reshape(n_node, 2, part, 1)
+    pieces = (line_a, behind_a, far_a1, far_a2, ahead_a, line_b, behind_b, far_b1, far_b2, ahead_b)
+    rows = n_node * part
+    own, other = pl.pallas_call(
+        half_head_kernel,
         grid_spec=pltpu.PrefetchScalarGridSpec(
             num_scalar_prefetch=1,
+            grid=(),
+            in_specs=[in_vmem] + [hbm] * 2 + [in_vmem] * len(pieces),
+            out_specs=[in_vmem] * 2,
+            scratch_shapes=[
+                pltpu.VMEM((2 * vocab_rows, 4 * width), BF),
+                pltpu.VMEM((rows, 4 * width), BF),
+                pltpu.SemaphoreType.DMA((2, 4)),
+            ],
+        ),
+        out_shape=(like(rows, vocab_rows + 128, dtype=F32),) * 2,
+        compiler_params=vmem(VMEM),
+        cost_estimate=pl.CostEstimate(
+            flops=16 * rows * width * vocab_rows, bytes_accessed=16 * width * vocab_rows, transcendentals=0
+        ),
+        name="half_head",
+    )(place, inverse, head, head_other, *pieces)
+    got = shift(other, "core", 1)
+    everyone, own = lax.optimization_barrier((everyone, own))
+    group = 8
+    whole_stats = pl.pallas_call(
+        functools.partial(whole_head_kernel, model),
+        grid_spec=pltpu.PrefetchScalarGridSpec(
+            num_scalar_prefetch=2,
             grid=(n_node // group,),
             in_specs=[
-                pl.BlockSpec((group, 8, tokens, width), lambda n, s: (n, 0, 0, 0)),
-                pl.BlockSpec((vocab_rows, model), lambda n, s: (0, 0)),
-                pl.BlockSpec((group * tokens, 1), lambda n, s: (n, 0)),
-                pl.BlockSpec((group * tokens, 1), lambda n, s: (n, 0)),
+                pl.BlockSpec((group, 8, part, width), lambda n, s, t: (n, 0, 0, 0)),
+                pl.BlockSpec((vocab_rows, model), lambda n, s, t: (0, 0)),
+                pl.BlockSpec((4, width), lambda n, s, t: (0, 0)),
+                pl.BlockSpec((4, width), lambda n, s, t: (0, 0)),
+                pl.BlockSpec((group * part, 1), lambda n, s, t: (n, 0)),
             ],
-            out_specs=pl.BlockSpec((8, group * tokens), lambda n, s: (0, n)),
+            out_specs=pl.BlockSpec((8, group * part), lambda n, s, t: (0, n)),
         ),
-        out_shape=like(8, total_tokens, dtype=F32),
-        compiler_params=vmem,
-        name="head",
+        out_shape=like(8, rows, dtype=F32),
+        compiler_params=vmem(VMEM),
+        name="whole_head",
     )(
-        first_id.reshape(1).astype(jnp.int32),
-        everyone.reshape(n_node, 8, tokens, width),
+        first_id,
+        place,
+        everyone.reshape(n_node, 8, part, width),
         head,
-        scale,
-        targets.reshape(total_tokens, 1),
+        inverse,
+        inverse_other,
+        wanted[:, 0].reshape(rows, 1),
     )
-    stats = merged([stats, shift(stats, "core", 1)])
-    for axis in ("y", "z", "x"):
-        stats = merged([stats] + [shift(stats, axis, k) for k in (1, 2, 3)])
-    peak, exp_total, target_logit = stats[0], stats[1], stats[2]
-    ref_logp = target_logit - peak - jnp.log(exp_total)
-    kl = 0.5 * (policy_logp - ref_logp) * (policy_logp - ref_logp)
-    return layer_out, ref_logp, kl
+    stats = pl.pallas_call(
+        functools.partial(stats_kernel, model),
+        grid_spec=pltpu.PrefetchScalarGridSpec(
+            num_scalar_prefetch=2, grid=(), in_specs=[in_vmem] * 4, out_specs=in_vmem
+        ),
+        out_shape=like(3 * n_node, 128, dtype=F32),
+        compiler_params=vmem(VMEM),
+        name="stats",
+    )(first_id, jnp.stack(order).astype(jnp.int32), own, got, wanted[:, 1], whole_stats)
+    for axis in ("core", "y", "z"):
+        stats = pl.pallas_call(
+            merge_kernel, out_shape=like(3 * n_node, 128, dtype=F32), name="merge"
+        )(*neighbours(stats, axis))
+    ref_logp, kl = pl.pallas_call(
+        final_kernel, out_shape=(like(n_node, tokens, dtype=F32),) * 2, name="final"
+    )(*neighbours(stats, "x"), policy_logp.reshape(n_node, tokens))
+    return layer_out, ref_logp.reshape(-1), kl.reshape(-1)
 
 
 def solution(mesh):

time: 301 us -> 300 us (level)
  waiting for transfers between devices: 153 us -> 94.6 us
  starting transfers between devices: 64.1 us -> 109 us
  Pallas kernels: 49.4 us -> 58.6 us
    all_gather x1, waiting for transfers between devices: 61.3 us -> 0.02 us  [shards(): everyone = lax.all_gather(scaled[:part], AXES, axis=0, tiled=True)]
    ppermute x40 -> x52, starting transfers between devices: 38.4 us -> 80.6 us  [shift(): lax.ppermute(value, axis, [(i, (i + step) % size) for i in range(size)])]
    ppermute x40 -> x52, waiting for transfers between devices: 79.9 us -> 86.4 us  [shift(): lax.ppermute(value, axis, [(i, (i + step) % size) for i in range(size)])]
    pallas_call x6 -> x9, Pallas kernels: 26 us -> 32.4 us  [the longest x1 13 us: shards(): pl.pallas_call(functools.partial(whole_head_kernel, model), grid_spec=plt...]
    reshape x1 -> x4, local copies, waits for them, and re-layouts: 0.26 us -> 3.49 us  [the longest x2 2.73 us: shards(): return (layer_out, ref_logp.reshape(-1), kl.reshape(-1))]
    all_to_all x4, waiting for transfers between devices: 11.3 us -> 8.21 us  [over_nodes(): lax.all_to_all(cut, ('x', 'z'), split_axis=0, concat_axis=0, tiled=True)]
    all_to_all x4, starting transfers between devices: 25.7 us -> 28.7 us  [over_nodes(): lax.all_to_all(cut, ('x', 'z'), split_axis=0, concat_axis=0, tiled=True)]
    unnamed x58 -> x60, local copies, waits for them, and re-layouts: 14 us -> 12.2 us
  transfers between devices with their start and end apart: 45 -> 57, of which waited for: 36 -> 29; matrix products, arithmetic and copies ran while one was open for 2% -> 2% of each run, Pallas kernels for 6% -> 14%
where the time goes in v3:
time: 300 us; the launch traced here: 297 us
  starting transfers between devices  109 us (36%)
  waiting for transfers between devices  94.6 us (32%)
  Pallas kernels  58.6 us (20%)
  local copies, waits for them, and re-layouts  19.2 us (6%)
  between operations  14.9 us (5%)
    ppermute x52, waiting for transfers between devices, shift(): lax.ppermute(value, axis, [(i, (i + step) % size) for i in range(size)])  86.4 us
    ppermute x52, starting transfers between devices, shift(): lax.ppermute(value, axis, [(i, (i + step) % size) for i in range(size)])  80.6 us
    all_to_all x4, starting transfers between devices, over_nodes(): lax.all_to_all(cut, ('x', 'z'), split_axis=0, concat_axis=0, tiled=True)  28.7 us
    pallas_call x1, Pallas kernels, shards(): pl.pallas_call(functools.partial(whole_head_kernel, model), grid_spec=plt...  13 us
    unnamed x60, local copies, waits for them, and re-layouts  12.2 us
    pallas_call x1, Pallas kernels, shards(): pl.pallas_call(up_kernel, grid_spec=pltpu.PrefetchScalarGridSpec(num_scal...  11.4 us
    pallas_call x1, Pallas kernels, shards(): pl.pallas_call(half_head_kernel, grid_spec=pltpu.PrefetchScalarGridSpec(n...  11.2 us
    pallas_call x1, Pallas kernels, shards(): pl.pallas_call(down_kernel, grid_spec=pltpu.PrefetchScalarGridSpec(num_sc...  9.55 us
  transfers between devices with their start and end apart: 57, of which 29 were waited for; matrix products, arithmetic and copies ran while one was open for 2% of the time, Pallas kernels for 14%

profile of v3, /device:TPU:0, one launch (start us, length us, event | category | flops | bytes accessed | tf_op | source)
XLA Modules:
  0.0 297.0 jit_solution(9444573523587026669)
XLA Ops:
  11.9 8.0 %all-to-all-start = ((bf16[16,40,512]{2,1,0:T(8,128)(2,1)}), bf16[16,40,512]{2,1,0:T(8,128)(2,1)S(1)}, u32[]{:S(2)}, u32[]{:S(2)}) async-start(bf16[16,40,512]{2,1,0:T(8,128)(2,1)} %bitcast.2), calls=%async_computation | async-start | bytes 1310720 | tf_op jit(solution)/shard_map/all_to_all | solution.py:397
  34.3 7.1 %all-to-all-start.1 = ((bf16[16,40,1536]{2,1,0:T(8,128)(2,1)}), bf16[16,40,1536]{2,1,0:T(8,128)(2,1)S(1)}, u32[]{:S(2)}, u32[]{:S(2)}) async-start(bf16[16,40,1536]{2,1,0:T(8,128)(2,1)} %bitcast.55), calls=%async_computation.1 | async-start | bytes 3932160 | tf_op jit(solution)/shard_map/all_to_all | solution.py:397
  45.0 12.8 %collective-permute-done.3.a1 = bf16[640,512]{1,0:T(8,128)(2,1)S(1)} collective-permute-done((bf16[640,512]{1,0:T(8,128)(2,1)S(1)}, bf16[640,512]{1,0:T(8,128)(2,1)S(1)}, u32[]{:S(2)}, u32[]{:S(2)}) %collective-permute-start.3) | collective-permute-done | bytes 655392 | tf_op jit(solution)/shard_map/ppermute | solution.py:19
  63.4 3.7 %collective-permute-done.4.a2_top = bf16[320,512]{1,0:T(8,128)(2,1)} collective-permute-done((bf16[320,512]{1,0:T(8,128)(2,1)}, bf16[320,512]{1,0:T(8,128)(2,1)}, u32[]{:S(2)}, u32[]{:S(2)}) %collective-permute-start.4) | collective-permute-done | bytes 327712 | tf_op jit(solution)/shard_map/ppermute | solution.py:19
  69.7 11.4 %gate_up.1 = (f32[640,1024]{1,0:T(8,128)}, bf16[640,1024]{1,0:T(8,128)(2,1)S(1)}) custom-call(s32[2]{0:T(128)S(1)} %pad_add_fusion.place_ref, bf16[640,512]{1,0:T(8,128)(2,1)S(1)} %bitcast.53, bf16[640,512]{1,0:T(8,128)(2,1)S(1)} %collective-permute-done.3.a1, bf16[320,512]{1,0:T(8,128)(2,1)} %collective-permute-done.4.a2_top, ...), custom_call_target="tpu_custom_call" | custom-call | tf_op jit(solution)/shard_map/gate_up/pallas_call | solution.py:448
  85.3 9.6 %down.1 = (bf16[640,512]{1,0:T(8,128)(2,1)}, bf16[320,512]{1,0:T(8,128)(2,1)}, bf16[320,512]{1,0:T(8,128)(2,1)}, bf16[320,512]{1,0:T(8,128)(2,1)}, bf16[320,512]...) custom-call(s32[2]{0:T(128)} %copy-done.11, ...), custom_call_target="tpu_custom_call" | custom-call | tf_op jit(solution)/shard_map/down/pallas_call | solution.py:465
  94.9 6.7 %all-to-all-start.3 = ((bf16[16,40,1536]{2,1,0:T(8,128)(2,1)}), bf16[16,40,1536]{2,1,0:T(8,128)(2,1)S(1)}, u32[]{:S(2)}, u32[]{:S(2)}) async-start(bf16[16,40,1536]{2,1,0:T(8,128)(2,1)} %bitcast.63), calls=%async_computation.3 | async-start | bytes 3932160 | tf_op jit(solution)/shard_map/all_to_all | solution.py:397
  101.6 3.8 %collective-permute-start.11 = (bf16[320,512]{1,0:T(8,128)(2,1)}, bf16[320,512]{1,0:T(8,128)(2,1)S(1)}, u32[]{:S(2)}, u32[]{:S(2)}) collective-permute-start(bf16[320,512]{1,0:T(8,128)(2,1)} %get-tuple-element.46), channel_id=1, source_target_pairs={{0,6},{2,0},{4,2},{6,4},{1,7},{3,1},{5,3},{7,5},{8,14},{10,8},{12,... | collective-permute-start | bytes 983048 | tf_op jit(solution)/shard_map/ppermute | solution.py:19
  105.4 3.5 %collective-permute-start.14 = (bf16[320,512]{1,0:T(8,128)(2,1)S(1)}, bf16[320,512]{1,0:T(8,128)(2,1)S(1)}, u32[]{:S(2)}, u32[]{:S(2)}) collective-permute-start(bf16[320,512]{1,0:T(8,128)(2,1)S(1)} %copy-done.28), channel_id=1, source_target_pairs={{0,6},{2,0},{4,2},{6,4},{1,7},{3,1},{5,3},{7,5},{8,14},{10,8},{12,... | collective-permute-start | bytes 983048 | tf_op jit(solution)/shard_map/ppermute | solution.py:19
  108.9 4.9 %collective-permute-done.11.got1 = bf16[320,512]{1,0:T(8,128)(2,1)S(1)} collective-permute-done((bf16[320,512]{1,0:T(8,128)(2,1)}, bf16[320,512]{1,0:T(8,128)(2,1)S(1)}, u32[]{:S(2)}, u32[]{:S(2)}) %collective-permute-start.11) | collective-permute-done | bytes 327712 | tf_op jit(solution)/shard_map/ppermute | solution.py:19
  113.8 3.6 %collective-permute-done.12.got3 = bf16[320,512]{1,0:T(8,128)(2,1)S(1)} collective-permute-done((bf16[320,512]{1,0:T(8,128)(2,1)}, bf16[320,512]{1,0:T(8,128)(2,1)S(1)}, u32[]{:S(2)}, u32[]{:S(2)}) %collective-permute-start.12) | collective-permute-done | bytes 327712 | tf_op jit(solution)/shard_map/ppermute | solution.py:19
  126.7 3.4 %collective-permute-done.16.right_low = bf16[320,512]{1,0:T(8,128)(2,1)S(1)} collective-permute-done((bf16[320,512]{1,0:T(8,128)(2,1)S(1)}, bf16[320,512]{1,0:T(8,128)(2,1)S(1)}, u32[]{:S(2)}, u32[]{:S(2)}) %collective-permute-start.16) | collective-permute-done | bytes 327712 | tf_op jit(solution)/shard_map/ppermute | solution.py:19
  131.1 6.9 %all-to-all-start.2 = ((bf16[16,40,512]{2,1,0:T(8,128)(2,1)}), bf16[16,40,512]{2,1,0:T(8,128)(2,1)S(1)}, u32[]{:S(2)}, u32[]{:S(2)}) async-start(bf16[16,40,512]{2,1,0:T(8,128)(2,1)} %bitcast.9), calls=%async_computation.2 | async-start | bytes 1310720 | tf_op jit(solution)/shard_map/all_to_all | solution.py:397
  141.5 7.9 %all-to-all-done.2 = bf16[16,40,512]{2,1,0:T(8,128)(2,1)S(1)} async-done(((bf16[16,40,512]{2,1,0:T(8,128)(2,1)}), bf16[16,40,512]{2,1,0:T(8,128)(2,1)S(1)}, u32[]{:S(2)}, u32[]{:S(2)}) %all-to-all-start.2) | async-done | bytes 655392 | tf_op jit(solution)/shard_map/all_to_all | solution.py:397
  153.4 4.6 %collective-permute-done.30 = bf16[48,896]{1,0:T(8,128)(2,1)S(1)} collective-permute-done((bf16[48,896]{1,0:T(8,128)(2,1)S(1)}, bf16[48,896]{1,0:T(8,128)(2,1)S(1)}, u32[]{:S(2)}, u32[]{:S(2)}) %collective-permute-start.30) | collective-permute-done | bytes 86048 | tf_op jit(solution)/shard_map/ppermute | solution.py:19
  178.9 12.5 %collective-permute-done.36.refs_6_ = bf16[4,2,48,896]{3,2,1,0:T(8,128)(2,1)S(1)} collective-permute-done((bf16[4,2,48,896]{3,2,1,0:T(8,128)(2,1)S(1)}, bf16[4,2,48,896]{3,2,1,0:T(8,128)(2,1)S(1)}, u32[]{:S(2)}, u32[]{:S(2)}) %collective-permute-start.36) | collective-permute-done | bytes 688160 | tf_op jit(solution)/shard_map/ppermute | solution.py:19
  191.7 3.8 %collective-permute-start.39 = (bf16[2,2,48,896]{3,2,1,0:T(8,128)(2,1)S(1)}, bf16[2,2,48,896]{3,2,1,0:T(8,128)(2,1)S(1)}, u32[]{:S(2)}, u32[]{:S(2)}) collective-permute-start(bf16[2,2,48,896]{3,2,1,0:T(8,128)(2,1)S(1)} %slice.65), channel_id=1, source_target_pairs={{0,96},{32,0},{64,32},{96,64},{1,97},{33,1},{65,33},{97,65},{2,98}... | collective-permute-start | bytes 1032200 | tf_op jit(solution)/shard_map/ppermute | solution.py:19
  195.6 13.3 %collective-permute-start.29 = (bf16[2,2,48,896]{3,2,1,0:T(8,128)(2,1)S(1)}, bf16[2,2,48,896]{3,2,1,0:T(8,128)(2,1)S(1)}, u32[]{:S(2)}, u32[]{:S(2)}) collective-permute-start(bf16[2,2,48,896]{3,2,1,0:T(8,128)(2,1)S(1)} %slice.61), channel_id=1, source_target_pairs={{0,24},{8,0},{16,8},{24,16},{1,25},{9,1},{17,9},{25,17},{2,26},{10... | collective-permute-start | bytes 1032200 | tf_op jit(solution)/shard_map/ppermute | solution.py:19
  209.0 13.5 %collective-permute-done.29.refs_3_ = bf16[2,2,48,896]{3,2,1,0:T(8,128)(2,1)S(1)} collective-permute-done((bf16[2,2,48,896]{3,2,1,0:T(8,128)(2,1)S(1)}, bf16[2,2,48,896]{3,2,1,0:T(8,128)(2,1)S(1)}, u32[]{:S(2)}, u32[]{:S(2)}) %collective-permute-start.29) | collective-permute-done | bytes 344096 | tf_op jit(solution)/shard_map/ppermute | solution.py:19
  222.5 11.2 %half_head.1 = (f32[768,640]{1,0:T(8,128)}, f32[768,640]{1,0:T(8,128)}) custom-call(s32[2]{0:T(128)S(1)} %copy-done.12, f32[4,896]{1,0:T(4,128)S(1)} %get-tuple-element.60.inverse_ref.own_ref, bf16[512,7168]{1,0:T(8,128)(2,1)} %head_ref.1, bf16[512,7168]{1,0:T(8,128)(2,1)} %copy-done.26, bf16[4,2,48,896]{3,2,1,0:T(8,128)(2,1)S(1)} %pad_maximum_fusion.refs_0_, ...), custom_call_target="tpu_custom_call" | custom-call | flops 5637144576 | bytes 7340032 | tf_op jit(solution)/shard_map/half_head/pallas_call | solution.py:527
  237.4 13.0 %whole_head.1.whole_ref = f32[8,768]{1,0:T(8,128)S(1)} custom-call(s32[1]{0:T(128)} %bitcast.13.first_ref, s32[2]{0:T(128)S(1)} %copy-done.12, bf16[16,8,48,896]{3,2,1,0:T(8,128)(2,1)} %bitcast.56, bf16[512,7168]{1,0:T(8,128)(2,1)} %head_ref.1, f32[4,896]{1,0:T(4,128)S(1)} %get-tuple-element.60.inverse_ref.own_ref, ...), custom_call_target="tpu_custom_call" | custom-call | tf_op jit(solution)/shard_map/whole_head/pallas_call | solution.py:550
  256.9 3.6 %collective-permute-start.44 = (f32[48,128]{1,0:T(8,128)}, f32[48,128]{1,0:T(8,128)S(1)}, u32[]{:S(2)}, u32[]{:S(2)}) collective-permute-start(f32[48,128]{1,0:T(8,128)} %merge.3.refs_0_), channel_id=1, source_target_pairs={{0,4},{2,6},{4,0},{6,2},{1,5},{3,7},{5,1},{7,3},{8,12},{10,14},{12... | collective-permute-start | bytes 73736 | tf_op jit(solution)/shard_map/ppermute | solution.py:19
  266.9 4.8 %collective-permute-start.47 = (f32[48,128]{1,0:T(8,128)}, f32[48,128]{1,0:T(8,128)S(1)}, u32[]{:S(2)}, u32[]{:S(2)}) collective-permute-start(f32[48,128]{1,0:T(8,128)} %merge.4.refs_0_), channel_id=1, source_target_pairs={{0,16},{8,24},{16,0},{24,8},{1,17},{9,25},{17,1},{25,9},{2,18},{10... | collective-permute-start | bytes 73736 | tf_op jit(solution)/shard_map/ppermute | solution.py:19
  277.8 3.3 %collective-permute-start.50 = (f32[48,128]{1,0:T(8,128)}, f32[48,128]{1,0:T(8,128)S(1)}, u32[]{:S(2)}, u32[]{:S(2)}) collective-permute-start(f32[48,128]{1,0:T(8,128)} %merge.5.refs_0_), channel_id=1, source_target_pairs={{0,64},{32,96},{64,0},{96,32},{1,65},{33,97},{65,1},{97,33},{2,66}... | collective-permute-start | bytes 73736 | tf_op jit(solution)/shard_map/ppermute | solution.py:19
  (194 shorter events, 105.3 us)
Async XLA Ops:
  7.2 61.4 %collective-permute-start.7 = (bf16[7168,256]{1,0:T(8,128)(2,1)}, bf16[7168,256]{1,0:T(8,128)(2,1)}, u32[]{:S(2)}, u32[]{:S(2)}) collective-permute-start(bf16[7168,256]{1,0:T(8,128)(2,1)} %bitcast.59), channel_id=1, source_target_pairs={{0,1},{1,0},{2,3},{3,2},{4,5},{5,4},{6,7},{7,6},{8,9},{9,8},{10,11... | collective-permute-start | bytes 11010056 | tf_op jit(solution)/shard_map/ppermute | solution.py:19
  7.3 61.3 %collective-permute-start.8 = (bf16[7168,256]{1,0:T(8,128)(2,1)}, bf16[7168,256]{1,0:T(8,128)(2,1)}, u32[]{:S(2)}, u32[]{:S(2)}) collective-permute-start(bf16[7168,256]{1,0:T(8,128)(2,1)} %bitcast.61), channel_id=1, source_target_pairs={{0,1},{1,0},{2,3},{3,2},{4,5},{5,4},{6,7},{7,6},{8,9},{9,8},{10,11... | collective-permute-start | bytes 11010056 | tf_op jit(solution)/shard_map/ppermute | solution.py:19
  11.9 22.5 %all-to-all-start = ((bf16[16,40,512]{2,1,0:T(8,128)(2,1)}), bf16[16,40,512]{2,1,0:T(8,128)(2,1)S(1)}, u32[]{:S(2)}, u32[]{:S(2)}) async-start(bf16[16,40,512]{2,1,0:T(8,128)(2,1)} %bitcast.2), calls=%async_computation | async-start | bytes 1310720 | tf_op jit(solution)/shard_map/all_to_all | solution.py:397
  19.8 61.3 %collective-permute-start.10 = (bf16[256,7168]{1,0:T(8,128)(2,1)}, bf16[256,7168]{1,0:T(8,128)(2,1)}, u32[]{:S(2)}, u32[]{:S(2)}) collective-permute-start(bf16[256,7168]{1,0:T(8,128)(2,1)} %bitcast.57), channel_id=1, source_target_pairs={{0,1},{1,0},{2,3},{3,2},{4,5},{5,4},{6,7},{7,6},{8,9},{9,8},{10,11... | collective-permute-start | bytes 11010056 | tf_op jit(solution)/shard_map/ppermute | solution.py:19
  34.3 34.2 %all-to-all-start.1 = ((bf16[16,40,1536]{2,1,0:T(8,128)(2,1)}), bf16[16,40,1536]{2,1,0:T(8,128)(2,1)S(1)}, u32[]{:S(2)}, u32[]{:S(2)}) async-start(bf16[16,40,1536]{2,1,0:T(8,128)(2,1)} %bitcast.55), calls=%async_computation.1 | async-start | bytes 3932160 | tf_op jit(solution)/shard_map/all_to_all | solution.py:397
  41.5 16.3 %collective-permute-start.3 = (bf16[640,512]{1,0:T(8,128)(2,1)S(1)}, bf16[640,512]{1,0:T(8,128)(2,1)S(1)}, u32[]{:S(2)}, u32[]{:S(2)}) collective-permute-start(bf16[640,512]{1,0:T(8,128)(2,1)S(1)} %bitcast.51), channel_id=1, source_target_pairs={{0,2},{2,4},{4,6},{6,0},{1,3},{3,5},{5,7},{7,1},{8,10},{10,12},{12... | collective-permute-start | bytes 1966088 | tf_op jit(solution)/shard_map/ppermute | solution.py:19
  42.0 16.5 %collective-permute-start.5 = (bf16[640,512]{1,0:T(8,128)(2,1)S(1)}, bf16[640,512]{1,0:T(8,128)(2,1)S(1)}, u32[]{:S(2)}, u32[]{:S(2)}) collective-permute-start(bf16[640,512]{1,0:T(8,128)(2,1)S(1)} %bitcast.52), channel_id=1, source_target_pairs={{0,6},{2,0},{4,2},{6,4},{1,7},{3,1},{5,3},{7,5},{8,14},{10,8},{12,... | collective-permute-start | bytes 1966088 | tf_op jit(solution)/shard_map/ppermute | solution.py:19
  94.9 36.2 %all-to-all-start.3 = ((bf16[16,40,1536]{2,1,0:T(8,128)(2,1)}), bf16[16,40,1536]{2,1,0:T(8,128)(2,1)S(1)}, u32[]{:S(2)}, u32[]{:S(2)}) async-start(bf16[16,40,1536]{2,1,0:T(8,128)(2,1)} %bitcast.63), calls=%async_computation.3 | async-start | bytes 3932160 | tf_op jit(solution)/shard_map/all_to_all | solution.py:397
  101.6 12.2 %collective-permute-start.11 = (bf16[320,512]{1,0:T(8,128)(2,1)}, bf16[320,512]{1,0:T(8,128)(2,1)S(1)}, u32[]{:S(2)}, u32[]{:S(2)}) collective-permute-start(bf16[320,512]{1,0:T(8,128)(2,1)} %get-tuple-element.46), channel_id=1, source_target_pairs={{0,6},{2,0},{4,2},{6,4},{1,7},{3,1},{5,3},{7,5},{8,14},{10,8},{12,... | collective-permute-start | bytes 983048 | tf_op jit(solution)/shard_map/ppermute | solution.py:19
  105.4 12.1 %collective-permute-start.12 = (bf16[320,512]{1,0:T(8,128)(2,1)}, bf16[320,512]{1,0:T(8,128)(2,1)S(1)}, u32[]{:S(2)}, u32[]{:S(2)}) collective-permute-start(bf16[320,512]{1,0:T(8,128)(2,1)} %get-tuple-element.48), channel_id=1, source_target_pairs={{0,2},{2,4},{4,6},{6,0},{1,3},{3,5},{5,7},{7,1},{8,10},{10,12},{12... | collective-permute-start | bytes 983048 | tf_op jit(solution)/shard_map/ppermute | solution.py:19
  105.4 16.2 %collective-permute-start.14 = (bf16[320,512]{1,0:T(8,128)(2,1)S(1)}, bf16[320,512]{1,0:T(8,128)(2,1)S(1)}, u32[]{:S(2)}, u32[]{:S(2)}) collective-permute-start(bf16[320,512]{1,0:T(8,128)(2,1)S(1)} %copy-done.28), channel_id=1, source_target_pairs={{0,6},{2,0},{4,2},{6,4},{1,7},{3,1},{5,3},{7,5},{8,14},{10,8},{12,... | collective-permute-start | bytes 983048 | tf_op jit(solution)/shard_map/ppermute | solution.py:19
  108.9 15.6 %collective-permute-start.15 = (bf16[320,512]{1,0:T(8,128)(2,1)S(1)}, bf16[320,512]{1,0:T(8,128)(2,1)S(1)}, u32[]{:S(2)}, u32[]{:S(2)}) collective-permute-start(bf16[320,512]{1,0:T(8,128)(2,1)S(1)} %copy-done.27), channel_id=1, source_target_pairs={{0,2},{2,4},{4,6},{6,0},{1,3},{3,5},{5,7},{7,1},{8,10},{10,12},{12... | collective-permute-start | bytes 983048 | tf_op jit(solution)/shard_map/ppermute | solution.py:19
  131.1 18.2 %all-to-all-start.2 = ((bf16[16,40,512]{2,1,0:T(8,128)(2,1)}), bf16[16,40,512]{2,1,0:T(8,128)(2,1)S(1)}, u32[]{:S(2)}, u32[]{:S(2)}) async-start(bf16[16,40,512]{2,1,0:T(8,128)(2,1)} %bitcast.9), calls=%async_computation.2 | async-start | bytes 1310720 | tf_op jit(solution)/shard_map/all_to_all | solution.py:397
  138.0 97.1 %all-gather.2.cloned.1.call-start = ((), (), s32[]{:S(2)}) async-start(), calls=%async_computation.4 | async-start | bytes 11096064 | tf_op jit(solution)/shard_map/all_gather | solution.py:509
  151.1 57.8 %collective-permute-start.20 = (bf16[512,7168]{1,0:T(8,128)(2,1)}, bf16[512,7168]{1,0:T(8,128)(2,1)S(1)}, u32[]{:S(2)}, u32[]{:S(2)}) collective-permute-start(bf16[512,7168]{1,0:T(8,128)(2,1)} %head_ref.1), channel_id=1, source_target_pairs={{0,1},{1,0},{2,3},{3,2},{4,5},{5,4},{6,7},{7,6},{8,9},{9,8},{10,11... | collective-permute-start | bytes 22020104 | tf_op jit(solution)/shard_map/ppermute | solution.py:19
  172.2 19.3 %collective-permute-start.36 = (bf16[4,2,48,896]{3,2,1,0:T(8,128)(2,1)S(1)}, bf16[4,2,48,896]{3,2,1,0:T(8,128)(2,1)S(1)}, u32[]{:S(2)}, u32[]{:S(2)}) collective-permute-start(bf16[4,2,48,896]{3,2,1,0:T(8,128)(2,1)S(1)} %pad_maximum_fusion.1.refs_5_), channel_id=1, source_target_pairs={{0,32},{32,64},{64,96},{96,0},{1,33},{33,65},{65,97},{97,1},{2,34}... | collective-permute-start | bytes 2064392 | tf_op jit(solution)/shard_map/ppermute | solution.py:19
  172.3 19.4 %collective-permute-start.38 = (bf16[4,2,48,896]{3,2,1,0:T(8,128)(2,1)S(1)}, bf16[4,2,48,896]{3,2,1,0:T(8,128)(2,1)S(1)}, u32[]{:S(2)}, u32[]{:S(2)}) collective-permute-start(bf16[4,2,48,896]{3,2,1,0:T(8,128)(2,1)S(1)} %pad_maximum_fusion.1.refs_5_), channel_id=1, source_target_pairs={{0,96},{32,0},{64,32},{96,64},{1,97},{33,1},{65,33},{97,65},{2,98}... | collective-permute-start | bytes 2064392 | tf_op jit(solution)/shard_map/ppermute | solution.py:19
  175.6 19.8 %collective-permute-start.26 = (bf16[4,2,48,896]{3,2,1,0:T(8,128)(2,1)S(1)}, bf16[4,2,48,896]{3,2,1,0:T(8,128)(2,1)S(1)}, u32[]{:S(2)}, u32[]{:S(2)}) collective-permute-start(bf16[4,2,48,896]{3,2,1,0:T(8,128)(2,1)S(1)} %pad_maximum_fusion.refs_0_), channel_id=1, source_target_pairs={{0,8},{8,16},{16,24},{24,0},{1,9},{9,17},{17,25},{25,1},{2,10},{10... | collective-permute-start | bytes 2064392 | tf_op jit(solution)/shard_map/ppermute | solution.py:19
  175.7 19.8 %collective-permute-start.28 = (bf16[4,2,48,896]{3,2,1,0:T(8,128)(2,1)S(1)}, bf16[4,2,48,896]{3,2,1,0:T(8,128)(2,1)S(1)}, u32[]{:S(2)}, u32[]{:S(2)}) collective-permute-start(bf16[4,2,48,896]{3,2,1,0:T(8,128)(2,1)S(1)} %pad_maximum_fusion.refs_0_), channel_id=1, source_target_pairs={{0,24},{8,0},{16,8},{24,16},{1,25},{9,1},{17,9},{25,17},{2,26},{10... | collective-permute-start | bytes 2064392 | tf_op jit(solution)/shard_map/ppermute | solution.py:19
  191.5 17.5 %collective-permute-start.37 = (bf16[2,2,48,896]{3,2,1,0:T(8,128)(2,1)S(1)}, bf16[2,2,48,896]{3,2,1,0:T(8,128)(2,1)S(1)}, u32[]{:S(2)}, u32[]{:S(2)}) collective-permute-start(bf16[2,2,48,896]{3,2,1,0:T(8,128)(2,1)S(1)} %slice.64), channel_id=1, source_target_pairs={{0,32},{32,64},{64,96},{96,0},{1,33},{33,65},{65,97},{97,1},{2,34}... | collective-permute-start | bytes 1032200 | tf_op jit(solution)/shard_map/ppermute | solution.py:19
  191.7 17.3 %collective-permute-start.39 = (bf16[2,2,48,896]{3,2,1,0:T(8,128)(2,1)S(1)}, bf16[2,2,48,896]{3,2,1,0:T(8,128)(2,1)S(1)}, u32[]{:S(2)}, u32[]{:S(2)}) collective-permute-start(bf16[2,2,48,896]{3,2,1,0:T(8,128)(2,1)S(1)} %slice.65), channel_id=1, source_target_pairs={{0,96},{32,0},{64,32},{96,64},{1,97},{33,1},{65,33},{97,65},{2,98}... | collective-permute-start | bytes 1032200 | tf_op jit(solution)/shard_map/ppermute | solution.py:19
  195.5 13.5 %collective-permute-start.27 = (bf16[2,2,48,896]{3,2,1,0:T(8,128)(2,1)S(1)}, bf16[2,2,48,896]{3,2,1,0:T(8,128)(2,1)S(1)}, u32[]{:S(2)}, u32[]{:S(2)}) collective-permute-start(bf16[2,2,48,896]{3,2,1,0:T(8,128)(2,1)S(1)} %slice.60), channel_id=1, source_target_pairs={{0,8},{8,16},{16,24},{24,0},{1,9},{9,17},{17,25},{25,1},{2,10},{10... | collective-permute-start | bytes 1032200 | tf_op jit(solution)/shard_map/ppermute | solution.py:19
  195.6 26.9 %collective-permute-start.29 = (bf16[2,2,48,896]{3,2,1,0:T(8,128)(2,1)S(1)}, bf16[2,2,48,896]{3,2,1,0:T(8,128)(2,1)S(1)}, u32[]{:S(2)}, u32[]{:S(2)}) collective-permute-start(bf16[2,2,48,896]{3,2,1,0:T(8,128)(2,1)S(1)} %slice.61), channel_id=1, source_target_pairs={{0,24},{8,0},{16,8},{24,16},{1,25},{9,1},{17,9},{25,17},{2,26},{10... | collective-permute-start | bytes 1032200 | tf_op jit(solution)/shard_map/ppermute | solution.py:19
  233.7 16.7 %collective-permute-start.40 = (f32[768,640]{1,0:T(8,128)}, f32[768,640]{1,0:T(8,128)S(1)}, u32[]{:S(2)}, u32[]{:S(2)}) collective-permute-start(f32[768,640]{1,0:T(8,128)} %get-tuple-element.63), channel_id=1, source_target_pairs={{0,1},{1,0},{2,3},{3,2},{4,5},{5,4},{6,7},{7,6},{8,9},{9,8},{10,11... | collective-permute-start | bytes 5898248 | tf_op jit(solution)/shard_map/ppermute | solution.py:19
  (62 other events, 456.0 us)
Sparse Core Ops, SparseCore 0:
  151.3 75.6 all-gather.1

commit v4 on v3

--- a/solution.py
+++ b/solution.py
@@ -40,45 +40,40 @@
 
 
 def route_kernel(routes_ref, weights_ref, hidden_ref, pick_ref, hi_ref, lo_ref, send_ref):
-    tokens, top = routes_ref.shape
-    columns = pick_ref.shape[1]
-    experts = columns // SLOTS
-    ids = lax.broadcasted_iota(jnp.int32, (tokens, experts), 1)
-    named = jnp.zeros((tokens, experts), F32)
-    gates = jnp.zeros((tokens, experts), F32)
+    top, tokens = routes_ref.shape
+    slots = pick_ref.shape[0]
+    experts = slots // SLOTS
+    ids = lax.broadcasted_iota(jnp.int32, (experts, tokens), 0)
+    named = jnp.zeros((experts, tokens), F32)
+    gates = jnp.zeros((experts, tokens), F32)
     for k in range(top):
-        hit = routes_ref[:, k : k + 1] == ids
+        hit = routes_ref[k : k + 1, :] == ids
         named = named + jnp.where(hit, 1.0, 0.0)
-        gates = gates + jnp.where(hit, weights_ref[:, k : k + 1], 0.0)
+        gates = gates + jnp.where(hit, weights_ref[k : k + 1, :], 0.0)
     row = lax.broadcasted_iota(jnp.int32, (tokens, tokens), 0)
     col = lax.broadcasted_iota(jnp.int32, (tokens, tokens), 1)
-    before = jnp.where(col < row, 1.0, 0.0).astype(BF)
-    count = dot(before, named.astype(BF))
-    expert = lax.broadcasted_iota(jnp.int32, (experts, columns), 0)
-    column = lax.broadcasted_iota(jnp.int32, (experts, columns), 1)
-    inside = (column >= expert * SLOTS) & (column < expert * SLOTS + SLOTS)
+    count = dot(named.astype(BF), jnp.where(row < col, 1.0, 0.0).astype(BF))
+    slot = lax.broadcasted_iota(jnp.int32, (slots, experts), 0)
+    expert = lax.broadcasted_iota(jnp.int32, (slots, experts), 1)
+    inside = (slot >= expert * SLOTS) & (slot < expert * SLOTS + SLOTS)
     spread = jnp.where(inside, 1.0, 0.0).astype(BF)
-    slot = jnp.sum(jnp.where(inside, column - expert * SLOTS, 0).astype(F32), axis=0, keepdims=True)
+    at = jnp.sum(jnp.where(inside, slot - expert * SLOTS, 0).astype(F32), axis=1, keepdims=True)
     gates_hi = gates.astype(BF)
     gates_lo = (gates - gates_hi.astype(F32)).astype(BF)
-    placed = (dot(named.astype(BF), spread) > 0.5) & (dot(count.astype(BF), spread) == slot)
-    hi_ref[...] = jnp.where(placed, dot(gates_hi, spread), 0.0).astype(BF)
-    lo_ref[...] = jnp.where(placed, dot(gates_lo, spread), 0.0).astype(BF)
+    placed = (dot(spread, named.astype(BF)) > 0.5) & (dot(spread, count.astype(BF)) == at)
+    hi_ref[...] = jnp.where(placed, dot(spread, gates_hi), 0.0).astype(BF)
+    lo_ref[...] = jnp.where(placed, dot(spread, gates_lo), 0.0).astype(BF)
     pick = jnp.where(placed, 1.0, 0.0).astype(BF)
     pick_ref[...] = pick
-    send_ref[...] = picked(pick, hidden_ref[:, :FIRST]).astype(BF)
-
-
-def picked(pick, rows):
-    return lax.dot_general(pick, rows, (((0,), (0,)), ((), ())), preferred_element_type=F32)
+    send_ref[...] = dot(pick, hidden_ref[:, :FIRST]).astype(BF)
 
 
 def spread_kernel(pick_ref, h0, h1, h2, h3, send_ref, inverse_ref):
-    tokens = pick_ref.shape[0]
+    tokens = pick_ref.shape[1]
     second = h0.shape[1]
     width = inverse_ref.shape[1]
     for k, ref in enumerate((h0, h1, h2, h3)):
-        send_ref[:, k * second : (k + 1) * second] = picked(pick_ref[...], ref[:tokens]).astype(BF)
+        send_ref[:, k * second : (k + 1) * second] = dot(pick_ref[...], ref[:tokens]).astype(BF)
         rows = ref[tokens:].astype(F32)
         for j, start in enumerate(range(0, width, second)):
             size = min(second, width - start)
@@ -86,51 +81,78 @@
             inverse_ref[k : k + 1, start : start + size] = 1.0 / (gain * gain)
 
 
+def mixed(hi_ref, lo_ref, rows):
+    across = (((0,), (0,)), ((), ()))
+    hi = lax.dot_general(hi_ref[...], rows, across, preferred_element_type=F32)
+    return hi + lax.dot_general(lo_ref[...], rows, across, preferred_element_type=F32)
+
+
 def block_of(place_ref, k):
     return 2 * lax.rem(place_ref[0] + 4 - k, 4) + place_ref[1]
 
 
-def up_kernel(place_ref, a0, a1, a2_top, a2_low, a3, b_ref, w0, w1, w2, w3, sum_ref, out_ref, w_ref, sems):
+def up_copies(place_ref, sources, w_ref, sems, places, offset, size, base):
+    hidden = sources[0].shape[1]
+    width = sources[0].shape[0] // 8
+    made = []
+    for j, w in enumerate(sources):
+        for i, k in enumerate(places):
+            start = pl.multiple_of(block_of(place_ref, k) * width + offset, 128)
+            made.append(
+                pltpu.make_async_copy(
+                    w.at[pl.ds(start, size), :],
+                    w_ref.at[pl.ds(base + i * size, size), pl.ds(j * hidden, hidden)],
+                    sems.at[j, i],
+                )
+            )
+    return made
+
+
+def up_first_kernel(place_ref, a0, a1, a3, w0, w1, w2, w3, sum_ref, w_ref, sems):
+    hidden = w0.shape[1]
+
+    @pl.when(pl.program_id(0) == 0)
+    def _():
+        copies = up_copies(place_ref, (w0, w1, w2, w3), w_ref, sems, (0, 1, 3), 0, FIRST, 0)
+        for copy in copies:
+            copy.start()
+        for copy in copies:
+            copy.wait()
+
+    @pl.loop(0, 4)
+    def _(j):
+        cols = pl.ds(pl.multiple_of(j * hidden, hidden), hidden)
+        part = dot(a0[...], w_ref[:FIRST, cols])
+        for k, ref in ((1, a1), (2, a3)):
+            part = part + dot(ref[...], w_ref[k * FIRST : (k + 1) * FIRST, cols])
+        sum_ref[:, cols] = part
+
+
+def up_second_kernel(
+    place_ref, before_ref, b_ref, a2_top, a2_low, w0, w1, w2, w3, sum_ref, out_ref, w_ref, sems
+):
     step = pl.program_id(0)
     hidden = w0.shape[1]
-    width = w0.shape[0] // 8
-    second = width - FIRST
-
-    def copies():
-        made = []
-        for j, w in enumerate((w0, w1, w2, w3)):
-            cols = pl.ds(j * hidden, hidden)
-            for k in range(4):
-                start = pl.multiple_of(block_of(place_ref, k) * width, 128)
-                made.append(
-                    pltpu.make_async_copy(
-                        w.at[pl.ds(start, FIRST), :],
-                        w_ref.at[pl.ds(k * FIRST, FIRST), cols],
-                        sems.at[j, 2 * k],
-                    )
-                )
-                made.append(
-                    pltpu.make_async_copy(
-                        w.at[pl.ds(start + FIRST, second), :],
-                        w_ref.at[pl.ds(4 * FIRST + k * second, second), cols],
-                        sems.at[j, 2 * k + 1],
-                    )
-                )
-        return made
+    second = w0.shape[0] // 8 - FIRST
 
     @pl.when(step == 0)
     def _():
-        for copy in copies():
+        sources = (w0, w1, w2, w3)
+        copies = up_copies(place_ref, sources, w_ref, sems.at[0], (2,), 0, FIRST, 0)
+        copies = copies + up_copies(
+            place_ref, sources, w_ref, sems.at[1], (0, 1, 2, 3), FIRST, second, FIRST
+        )
+        for copy in copies:
             copy.start()
-        for copy in copies():
+        for copy in copies:
             copy.wait()
 
     def total(a2):
-        for j in range(4):
-            cols = slice(j * hidden, (j + 1) * hidden)
-            part = dot(b_ref[...], w_ref[4 * FIRST :, cols])
-            for k, ref in enumerate((a0, a1, a2, a3)):
-                part = part + dot(ref[...], w_ref[k * FIRST : (k + 1) * FIRST, cols])
+        @pl.loop(0, 4)
+        def _(j):
+            cols = pl.ds(pl.multiple_of(j * hidden, hidden), hidden)
+            part = dot(b_ref[...], w_ref[FIRST:, cols]) + dot(a2[...], w_ref[:FIRST, cols])
+            part = part + before_ref[:, cols]
             sum_ref[:, cols] = part
             out_ref[:, cols] = part.astype(BF)
 
@@ -225,13 +247,11 @@
 def mix_kernel(hi_ref, lo_ref, back_ref, own_ref, p1, p2, p3):
     width = own_ref.shape[1]
     for k, ref in enumerate((own_ref, p1, p2, p3)):
-        block = back_ref[:, k * width : (k + 1) * width]
-        total = dot(hi_ref[...], block) + dot(lo_ref[...], block)
-        ref[...] = total.astype(ref.dtype)
+        ref[...] = mixed(hi_ref, lo_ref, back_ref[:, k * width : (k + 1) * width]).astype(ref.dtype)
 
 
 def layer_kernel(hidden_ref, hi_ref, lo_ref, back_ref, own_ref, p1, p2, p3, gain_ref, out_ref, scaled_ref):
-    first = dot(hi_ref[...], back_ref[...]) + dot(lo_ref[...], back_ref[...])
+    first = mixed(hi_ref, lo_ref, back_ref[...])
     second = own_ref[...] + p1[...].astype(F32) + p2[...].astype(F32) + p3[...].astype(F32)
     for mix, cols in ((first, slice(0, FIRST)), (second, slice(FIRST, hidden_ref.shape[1]))):
         total = hidden_ref[:, cols].astype(F32) + mix
@@ -268,36 +288,46 @@
     for copy in copies:
         copy.start()
 
-    def piece_of(line, behind, far1, far2, ahead, along, across):
-        if along == 2:
-            return (far1, across) if across < 2 else (far2, across - 2)
-        return ({0: line, 1: behind, 3: ahead}[along], across)
-
-    for back_x in range(4):
-        for back_z in range(4):
-            at = (back_x * 4 + back_z) * tokens
-            squares = 0.0
-            for ref, i, base in (
-                piece_of(line_a, behind_a, far_a1, far_a2, ahead_a, back_z, back_x) + (0,),
-                piece_of(line_b, behind_b, far_b1, far_b2, ahead_b, back_x, back_z) + (2,),
-            ):
-                for k in range(2):
-                    rows = ref[i, k]
-                    first = (base + k) * width
-                    rows_ref[at : at + tokens, first : first + width] = rows
-                    squares = squares + squares_of(rows, inverse_ref[base + k : base + k + 1])
-            own_ref[at : at + tokens, vocab:] = squares
-            other_ref[at : at + tokens, vocab:] = squares
+    own_ref[:, vocab:] = jnp.zeros_like(own_ref[:, vocab:])
+
+    def take(ref, place_of, base):
+        @pl.loop(0, ref.shape[0])
+        def _(i):
+            at = pl.ds(pl.multiple_of(place_of(i) * tokens, tokens), tokens)
+            squares = own_ref[at, vocab:]
+            for k in range(2):
+                rows = ref[i, k]
+                first = (base + k) * width
+                rows_ref[at, first : first + width] = rows
+                squares = squares + squares_of(rows, inverse_ref[base + k : base + k + 1])
+            own_ref[at, vocab:] = squares
+
+    for back, ref, skip in (
+        (0, line_a, 0), (1, behind_a, 0), (2, far_a1, 0), (2, far_a2, 2), (3, ahead_a, 0)
+    ):
+        take(ref, lambda i, back=back, skip=skip: (i + skip) * 4 + back, 0)
+    for back, ref, skip in (
+        (0, line_b, 0), (1, behind_b, 0), (2, far_b1, 0), (2, far_b2, 2), (3, ahead_b, 0)
+    ):
+        take(ref, lambda i, back=back, skip=skip: back * 4 + i + skip, 2)
+    other_ref[:, vocab:] = own_ref[:, vocab:]
     for copy in copies:
         copy.wait()
-    for at in range(0, rows_ref.shape[0], 384):
-        for j, ref in ((1, other_ref), (0, own_ref)):
-            ref[at : at + 384, :vocab] = lax.dot_general(
-                rows_ref[at : at + 384],
-                w_ref[j * vocab : (j + 1) * vocab, :],
-                (((1,), (1,)), ((), ())),
-                preferred_element_type=F32,
-            )
+
+    @pl.loop(0, rows_ref.shape[0] // 384)
+    def _(i):
+        at = pl.ds(pl.multiple_of(i * 384, 384), 384)
+
+        @pl.loop(0, vocab // 256)
+        def _(n):
+            cols = pl.ds(pl.multiple_of(n * 256, 256), 256)
+            for j, ref in ((1, other_ref), (0, own_ref)):
+                ref[at, cols] = lax.dot_general(
+                    rows_ref[at],
+                    w_ref[pl.ds(pl.multiple_of(j * vocab + n * 256, 256), 256), :],
+                    (((1,), (1,)), ((), ())),
+                    preferred_element_type=F32,
+                )
 
 
 def columns_of(full, ids, wanted):
@@ -308,16 +338,19 @@
     return jnp.where(lane == 0, peak, jnp.where(lane == 1, total, target)).T
 
 
-def whole_head_kernel(model, first_ref, place_ref, rows_ref, head_ref, own_ref, other_ref, wanted_ref, stats_ref):
+def whole_head_kernel(model, first_ref, place_ref, rows_ref, head_ref, own_ref, other_ref, wanted_ref, stats_ref, all_ref):
     nodes, parts, tokens, width = rows_ref.shape
-    rows = jnp.concatenate([rows_ref[:, p].reshape(nodes * tokens, width) for p in range(parts)], axis=1)
-    logits = lax.dot_general(rows, head_ref[...], (((1,), (1,)), ((), ())), preferred_element_type=F32)
     squares = 0.0
     for p in range(parts):
+        rows = rows_ref[:, p].reshape(nodes * tokens, width)
+        all_ref[:, p * width : (p + 1) * width] = rows
         k = lax.rem(place_ref[0] + 4 - p // 2, 4)
         mine = place_ref[1] == p % 2
         inverse = jnp.where(mine, own_ref[pl.ds(k, 1), :], other_ref[pl.ds(k, 1), :])
-        squares = squares + squares_of(rows[:, p * width : (p + 1) * width], inverse)
+        squares = squares + squares_of(rows, inverse)
+    logits = lax.dot_general(
+        all_ref[...], head_ref[...], (((1,), (1,)), ((), ())), preferred_element_type=F32
+    )
     scale = lax.rsqrt(jnp.sum(squares, axis=1, keepdims=True) / model + 1e-06)
     ids = first_ref[0] + lax.broadcasted_iota(jnp.int32, logits.shape, 1)
     columns = columns_of(logits * scale, ids, wanted_ref[...])
@@ -365,10 +398,18 @@
 
 def final_kernel(*refs):
     *ins, policy_ref, logp_ref, kl_ref = refs
-    half = policy_ref.shape[1] // 2
     peak, total, target = combined(ins)
-    logp = target - peak - jnp.log(total)
-    logp = jnp.concatenate([logp[:, :half], logp[:, 64 : 64 + half]], axis=1)
+    spaced = target - peak - jnp.log(total)
+    half = policy_ref.shape[0] * 128 // (2 * spaced.shape[0])
+    tokens = 2 * half
+    packed = jnp.concatenate([spaced[:, :half], spaced[:, 64 : 64 + half]], axis=1)
+    lines = []
+    for at in range(0, spaced.shape[0] * tokens, 128):
+        node, lane = at // tokens, at % tokens
+        pieces = [packed[node : node + 1, lane:]]
+        pieces.append(packed[node + 1 : node + 2, : 128 - (tokens - lane)])
+        lines.append(jnp.concatenate(pieces, axis=1))
+    logp = jnp.concatenate(lines, axis=0)
     logp_ref[...] = logp
     kl_ref[...] = 0.5 * (policy_ref[...] - logp) * (policy_ref[...] - logp)
 
@@ -417,10 +458,10 @@
     near = near + [shift(near[0], "y", k) for k in (1, 2, 3)]
     pick, mix_hi, mix_lo, send_a = pl.pallas_call(
         route_kernel,
-        out_shape=(like(tokens, slots), like(tokens, slots), like(tokens, slots), like(slots, FIRST)),
+        out_shape=(like(slots, tokens),) * 3 + (like(slots, FIRST),),
         compiler_params=vmem(VMEM),
         name="route",
-    )(routes, route_weights, hidden)
+    )(routes.T, route_weights.T, hidden)
     a0 = over_nodes(send_a)
     send_b, inverse = pl.pallas_call(
         spread_kernel,
@@ -445,21 +486,38 @@
     def whole(columns):
         return pl.BlockSpec((half, columns), lambda i, place: (0, 0))
 
-    partial, partial_out = pl.pallas_call(
-        up_kernel,
+    partial = pl.pallas_call(
+        up_first_kernel,
         grid_spec=pltpu.PrefetchScalarGridSpec(
             num_scalar_prefetch=1,
             grid=(2,),
-            in_specs=[rows_of(FIRST), rows_of(FIRST), whole(FIRST), whole(FIRST), rows_of(FIRST)]
-            + [rows_of(4 * second)]
-            + [hbm] * 4,
+            in_specs=[rows_of(FIRST)] * 3 + [hbm] * 4,
+            out_specs=rows_of(4 * hid),
+            scratch_shapes=[pltpu.VMEM((3 * FIRST, 4 * hid), BF), pltpu.SemaphoreType.DMA((4, 3))],
+        ),
+        out_shape=like(slots, 4 * hid, dtype=F32),
+        compiler_params=vmem(VMEM),
+        cost_estimate=pl.CostEstimate(
+            flops=24 * slots * FIRST * hid, bytes_accessed=24 * FIRST * hid, transcendentals=0
+        ),
+        name="up_first",
+    )(place, a0, a1, a3, gate_mat, up_mat, gate_other, up_other)
+    partial, partial_out = pl.pallas_call(
+        up_second_kernel,
+        grid_spec=pltpu.PrefetchScalarGridSpec(
+            num_scalar_prefetch=1,
+            grid=(2,),
+            in_specs=[rows_of(4 * hid), rows_of(4 * second), whole(FIRST), whole(FIRST)] + [hbm] * 4,
             out_specs=[rows_of(4 * hid)] * 2,
-            scratch_shapes=[pltpu.VMEM((4 * width, 4 * hid), BF), pltpu.SemaphoreType.DMA((4, 8))],
+            scratch_shapes=[
+                pltpu.VMEM((FIRST + 4 * second, 4 * hid), BF),
+                pltpu.SemaphoreType.DMA((2, 4, 4)),
+            ],
         ),
         out_shape=(like(slots, 4 * hid, dtype=F32), like(slots, 4 * hid)),
         compiler_params=vmem(VMEM),
-        name="gate_up",
-    )(place, a0, a1, a2_top, a2_low, a3, b, gate_mat, up_mat, gate_other, up_other)
+        name="up_second",
+    )(place, partial, b, a2_top, a2_low, gate_mat, up_mat, gate_other, up_other)
     partial_got = shift(partial_out, "core", 1)
 
     a0, a1_top, a1_low, a2_top, a2_low, a3_top, a3_low, b = pl.pallas_call(
@@ -560,6 +618,7 @@
                 pl.BlockSpec((group * part, 1), lambda n, s, t: (n, 0)),
             ],
             out_specs=pl.BlockSpec((8, group * part), lambda n, s, t: (0, n)),
+            scratch_shapes=[pltpu.VMEM((group * part, model), BF)],
         ),
         out_shape=like(8, rows, dtype=F32),
         compiler_params=vmem(VMEM),
@@ -587,8 +646,8 @@
             merge_kernel, out_shape=like(3 * n_node, 128, dtype=F32), name="merge"
         )(*neighbours(stats, axis))
     ref_logp, kl = pl.pallas_call(
-        final_kernel, out_shape=(like(n_node, tokens, dtype=F32),) * 2, name="final"
-    )(*neighbours(stats, "x"), policy_logp.reshape(n_node, tokens))
+        final_kernel, out_shape=(like(n_node * tokens // 128, 128, dtype=F32),) * 2, name="final"
+    )(*neighbours(stats, "x"), policy_logp.reshape(-1, 128))
     return layer_out, ref_logp.reshape(-1), kl.reshape(-1)
 
 

time: 300 us -> 285 us (0.950)
  starting transfers between devices: 109 us -> 95.7 us
  Pallas kernels: 58.6 us -> 65.5 us
  waiting for transfers between devices: 94.6 us -> 89.6 us
    ppermute x52, starting transfers between devices: 80.6 us -> 69.5 us  [shift(): lax.ppermute(value, axis, [(i, (i + step) % size) for i in range(size)])]
    ppermute x52, waiting for transfers between devices: 86.4 us -> 78.6 us  [shift(): lax.ppermute(value, axis, [(i, (i + step) % size) for i in range(size)])]
    pallas_call x3 -> x4, Pallas kernels: 14.6 us -> 19.1 us  [the longest x1 9.82 us: shards(): pl.pallas_call(up_second_kernel, grid_spec=pltpu.PrefetchScalarGridSpec(n...]
    reshape x3 -> x0, local copies, waits for them, and re-layouts: 3.4 us -> none  [the longest x2 2.73 us: shards(): return (layer_out, ref_logp.reshape(-1), kl.reshape(-1))]
    unnamed x60 -> x64, local copies, waits for them, and re-layouts: 12.2 us -> 14.1 us
  transfers between devices with their start and end apart: 57 -> 57, of which waited for: 29 -> 31; matrix products, arithmetic and copies ran while one was open for 2% -> 1% of each run, Pallas kernels for 14% -> 17%
where the time goes in v4:
time: 285 us; the launch traced here: 283 us
  starting transfers between devices  95.7 us (34%)
  waiting for transfers between devices  89.6 us (31%)
  Pallas kernels  65.5 us (23%)
  local copies, waits for them, and re-layouts  17.7 us (6%)
  between operations  14.7 us (5%)
    ppermute x52, waiting for transfers between devices, shift(): lax.ppermute(value, axis, [(i, (i + step) % size) for i in range(size)])  78.6 us
    ppermute x52, starting transfers between devices, shift(): lax.ppermute(value, axis, [(i, (i + step) % size) for i in range(size)])  69.5 us
    all_to_all x4, starting transfers between devices, over_nodes(): lax.all_to_all(cut, ('x', 'z'), split_axis=0, concat_axis=0, tiled=True)  26.1 us
    pallas_call x1, Pallas kernels, shards(): pl.pallas_call(functools.partial(whole_head_kernel, model), grid_spec=plt...  14.5 us
    unnamed x64, local copies, waits for them, and re-layouts  14.1 us
    pallas_call x1, Pallas kernels, shards(): pl.pallas_call(half_head_kernel, grid_spec=pltpu.PrefetchScalarGridSpec(n...  12.5 us
    all_to_all x4, waiting for transfers between devices, over_nodes(): lax.all_to_all(cut, ('x', 'z'), split_axis=0, concat_axis=0, tiled=True)  11 us
    pallas_call x1, Pallas kernels, shards(): pl.pallas_call(up_second_kernel, grid_spec=pltpu.PrefetchScalarGridSpec(n...  9.82 us
  transfers between devices with their start and end apart: 57, of which 31 were waited for; matrix products, arithmetic and copies ran while one was open for 1% of the time, Pallas kernels for 17%

profile of v4, /device:TPU:0, one launch (start us, length us, event | category | flops | bytes accessed | tf_op | source)
XLA Modules:
  0.0 283.5 jit_solution(1298196142092177807)
XLA Ops:
  12.3 8.0 %all-to-all-start = ((bf16[16,40,512]{2,1,0:T(8,128)(2,1)}), bf16[16,40,512]{2,1,0:T(8,128)(2,1)S(1)}, u32[]{:S(2)}, u32[]{:S(2)}) async-start(bf16[16,40,512]{2,1,0:T(8,128)(2,1)} %bitcast.4), calls=%async_computation | async-start | bytes 1310720 | tf_op jit(solution)/shard_map/all_to_all | solution.py:438
  34.7 7.1 %all-to-all-start.1 = ((bf16[16,40,1536]{2,1,0:T(8,128)(2,1)}), bf16[16,40,1536]{2,1,0:T(8,128)(2,1)S(1)}, u32[]{:S(2)}, u32[]{:S(2)}) async-start(bf16[16,40,1536]{2,1,0:T(8,128)(2,1)} %bitcast.60), calls=%async_computation.1 | async-start | bytes 3932160 | tf_op jit(solution)/shard_map/all_to_all | solution.py:438
  45.3 12.8 %collective-permute-done.3.a1 = bf16[640,512]{1,0:T(8,128)(2,1)S(1)} collective-permute-done((bf16[640,512]{1,0:T(8,128)(2,1)S(1)}, bf16[640,512]{1,0:T(8,128)(2,1)S(1)}, u32[]{:S(2)}, u32[]{:S(2)}) %collective-permute-start.3) | collective-permute-done | bytes 655392 | tf_op jit(solution)/shard_map/ppermute | solution.py:19
  60.5 3.2 %collective-permute-start.8 = (bf16[320,512]{1,0:T(8,128)(2,1)}, bf16[320,512]{1,0:T(8,128)(2,1)}, u32[]{:S(2)}, u32[]{:S(2)}) collective-permute-start(bf16[320,512]{1,0:T(8,128)(2,1)} %slice.57), channel_id=1, source_target_pairs={{0,6},{2,0},{4,2},{6,4},{1,7},{3,1},{5,3},{7,5},{8,14},{10,8},{12,... | collective-permute-start | bytes 983048 | tf_op jit(solution)/shard_map/ppermute | solution.py:19
  64.9 6.1 %up_first.1.before_ref = f32[640,1024]{1,0:T(8,128)S(1)} custom-call(s32[2]{0:T(128)S(1)} %pad_add_fusion.place_ref, bf16[640,512]{1,0:T(8,128)(2,1)S(1)} %bitcast.58, bf16[640,512]{1,0:T(8,128)(2,1)S(1)} %collective-permute-done.3.a1, bf16[640,512]{1,0:T(8,128)(2,1)S(1)} %copy-done.7, bf16[7168,256]{1,0:T(8,128)(2,1)} %bitcast.64, ...), custom_call_target="tpu_custom_call" | custom-call | flops 2013265920 | bytes 3145728 | tf_op jit(solution)/shard_map/up_first/pallas_call | solution.py:489
  72.5 9.8 %up_second.1 = (f32[640,1024]{1,0:T(8,128)}, bf16[640,1024]{1,0:T(8,128)(2,1)S(1)}) custom-call(s32[2]{0:T(128)S(1)} %pad_add_fusion.place_ref, f32[640,1024]{1,0:T(8,128)} %copy-done, bf16[640,1536]{1,0:T(8,128)(2,1)S(1)} %bitcast.55, bf16[320,512]{1,0:T(8,128)(2,1)} %collective-permute-done.7.a2_top, bf16[320,512]{1,0:T(8,128)(2,1)} %collective-permute-done.8.a2_low, ...), custom_call_target="tpu_custom_call" | custom-call | tf_op jit(solution)/shard_map/up_second/pallas_call | solution.py:505
  86.5 9.5 %down.1 = (bf16[640,512]{1,0:T(8,128)(2,1)}, bf16[320,512]{1,0:T(8,128)(2,1)}, bf16[320,512]{1,0:T(8,128)(2,1)}, bf16[320,512]{1,0:T(8,128)(2,1)}, bf16[320,512]...) custom-call(s32[2]{0:T(128)} %copy-done.14, ...), custom_call_target="tpu_custom_call" | custom-call | tf_op jit(solution)/shard_map/down/pallas_call | solution.py:523
  96.1 7.0 %all-to-all-start.3 = ((bf16[16,40,1536]{2,1,0:T(8,128)(2,1)}), bf16[16,40,1536]{2,1,0:T(8,128)(2,1)S(1)}, u32[]{:S(2)}, u32[]{:S(2)}) async-start(bf16[16,40,1536]{2,1,0:T(8,128)(2,1)} %bitcast.72), calls=%async_computation.3 | async-start | bytes 3932160 | tf_op jit(solution)/shard_map/all_to_all | solution.py:438
  107.3 6.8 %collective-permute-done.11.got1 = bf16[320,512]{1,0:T(8,128)(2,1)S(1)} collective-permute-done((bf16[320,512]{1,0:T(8,128)(2,1)}, bf16[320,512]{1,0:T(8,128)(2,1)S(1)}, u32[]{:S(2)}, u32[]{:S(2)}) %collective-permute-start.11) | collective-permute-done | bytes 327712 | tf_op jit(solution)/shard_map/ppermute | solution.py:19
  122.7 4.2 %collective-permute-done.13.left_top = bf16[320,512]{1,0:T(8,128)(2,1)S(1)} collective-permute-done((bf16[320,512]{1,0:T(8,128)(2,1)S(1)}, bf16[320,512]{1,0:T(8,128)(2,1)S(1)}, u32[]{:S(2)}, u32[]{:S(2)}) %collective-permute-start.13) | collective-permute-done | bytes 327712 | tf_op jit(solution)/shard_map/ppermute | solution.py:19
  132.5 4.0 %all-to-all-start.2 = ((bf16[16,40,512]{2,1,0:T(8,128)(2,1)}), bf16[16,40,512]{2,1,0:T(8,128)(2,1)S(1)}, u32[]{:S(2)}, u32[]{:S(2)}) async-start(bf16[16,40,512]{2,1,0:T(8,128)(2,1)} %bitcast.11), calls=%async_computation.2 | async-start | bytes 1310720 | tf_op jit(solution)/shard_map/all_to_all | solution.py:438
  139.9 7.9 %all-to-all-done.2 = bf16[16,40,512]{2,1,0:T(8,128)(2,1)S(1)} async-done(((bf16[16,40,512]{2,1,0:T(8,128)(2,1)}), bf16[16,40,512]{2,1,0:T(8,128)(2,1)S(1)}, u32[]{:S(2)}, u32[]{:S(2)}) %all-to-all-start.2) | async-done | bytes 655392 | tf_op jit(solution)/shard_map/all_to_all | solution.py:438
  152.5 4.1 %collective-permute-done.30 = bf16[48,896]{1,0:T(8,128)(2,1)S(1)} collective-permute-done((bf16[48,896]{1,0:T(8,128)(2,1)S(1)}, bf16[48,896]{1,0:T(8,128)(2,1)S(1)}, u32[]{:S(2)}, u32[]{:S(2)}) %collective-permute-start.30) | collective-permute-done | bytes 86048 | tf_op jit(solution)/shard_map/ppermute | solution.py:19
  163.8 3.3 %collective-permute-start.35 = (bf16[1,48,896]{2,1,0:T(8,128)(2,1)S(1)}, bf16[1,48,896]{2,1,0:T(8,128)(2,1)S(1)}, u32[]{:S(2)}, u32[]{:S(2)}) collective-permute-start(bf16[1,48,896]{2,1,0:T(8,128)(2,1)S(1)} %slice.63), channel_id=1, source_target_pairs={{0,24},{8,0},{16,8},{24,16},{1,25},{9,1},{17,9},{25,17},{2,26},{10... | collective-permute-start | bytes 258056 | tf_op jit(solution)/shard_map/ppermute | solution.py:19
  167.2 3.3 %collective-permute-start.25 = (bf16[1,48,896]{2,1,0:T(8,128)(2,1)S(1)}, bf16[1,48,896]{2,1,0:T(8,128)(2,1)S(1)}, u32[]{:S(2)}, u32[]{:S(2)}) collective-permute-start(bf16[1,48,896]{2,1,0:T(8,128)(2,1)S(1)} %slice.59), channel_id=1, source_target_pairs={{0,96},{32,0},{64,32},{96,64},{1,97},{33,1},{65,33},{97,65},{2,98}... | collective-permute-start | bytes 258056 | tf_op jit(solution)/shard_map/ppermute | solution.py:19
  177.4 12.6 %collective-permute-done.36.refs_6_ = bf16[4,2,48,896]{3,2,1,0:T(8,128)(2,1)S(1)} collective-permute-done((bf16[4,2,48,896]{3,2,1,0:T(8,128)(2,1)S(1)}, bf16[4,2,48,896]{3,2,1,0:T(8,128)(2,1)S(1)}, u32[]{:S(2)}, u32[]{:S(2)}) %collective-permute-start.36) | collective-permute-done | bytes 688160 | tf_op jit(solution)/shard_map/ppermute | solution.py:19
  190.5 3.8 %collective-permute-start.39 = (bf16[2,2,48,896]{3,2,1,0:T(8,128)(2,1)S(1)}, bf16[2,2,48,896]{3,2,1,0:T(8,128)(2,1)S(1)}, u32[]{:S(2)}, u32[]{:S(2)}) collective-permute-start(bf16[2,2,48,896]{3,2,1,0:T(8,128)(2,1)S(1)} %slice.65), channel_id=1, source_target_pairs={{0,96},{32,0},{64,32},{96,64},{1,97},{33,1},{65,33},{97,65},{2,98}... | collective-permute-start | bytes 1032200 | tf_op jit(solution)/shard_map/ppermute | solution.py:19
  194.4 3.3 %collective-permute-start.29 = (bf16[2,2,48,896]{3,2,1,0:T(8,128)(2,1)S(1)}, bf16[2,2,48,896]{3,2,1,0:T(8,128)(2,1)S(1)}, u32[]{:S(2)}, u32[]{:S(2)}) collective-permute-start(bf16[2,2,48,896]{3,2,1,0:T(8,128)(2,1)S(1)} %slice.61), channel_id=1, source_target_pairs={{0,24},{8,0},{16,8},{24,16},{1,25},{9,1},{17,9},{25,17},{2,26},{10... | collective-permute-start | bytes 1032200 | tf_op jit(solution)/shard_map/ppermute | solution.py:19
  199.0 3.8 %collective-permute-done.27.refs_2_ = bf16[2,2,48,896]{3,2,1,0:T(8,128)(2,1)S(1)} collective-permute-done((bf16[2,2,48,896]{3,2,1,0:T(8,128)(2,1)S(1)}, bf16[2,2,48,896]{3,2,1,0:T(8,128)(2,1)S(1)}, u32[]{:S(2)}, u32[]{:S(2)}) %collective-permute-start.27) | collective-permute-done | bytes 344096 | tf_op jit(solution)/shard_map/ppermute | solution.py:19
  202.8 5.6 %collective-permute-done.29.refs_3_ = bf16[2,2,48,896]{3,2,1,0:T(8,128)(2,1)S(1)} collective-permute-done((bf16[2,2,48,896]{3,2,1,0:T(8,128)(2,1)S(1)}, bf16[2,2,48,896]{3,2,1,0:T(8,128)(2,1)S(1)}, u32[]{:S(2)}, u32[]{:S(2)}) %collective-permute-start.29) | collective-permute-done | bytes 344096 | tf_op jit(solution)/shard_map/ppermute | solution.py:19
  208.4 12.5 %half_head.1 = (f32[768,640]{1,0:T(8,128)}, f32[768,640]{1,0:T(8,128)}) custom-call(s32[2]{0:T(128)S(1)} %copy-done.15, f32[4,896]{1,0:T(4,128)S(1)} %get-tuple-element.60.inverse_ref.own_ref, bf16[512,7168]{1,0:T(8,128)(2,1)} %head_ref.1, bf16[512,7168]{1,0:T(8,128)(2,1)} %copy-done.30, bf16[4,2,48,896]{3,2,1,0:T(8,128)(2,1)S(1)} %pad_maximum_fusion.refs_0_, ...), custom_call_target="tpu_custom_call" | custom-call | flops 5637144576 | bytes 7340032 | tf_op jit(solution)/shard_map/half_head/pallas_call | solution.py:585
  224.9 14.5 %whole_head.1.whole_ref = f32[8,768]{1,0:T(8,128)S(1)} custom-call(s32[1]{0:T(128)} %bitcast.15.first_ref, s32[2]{0:T(128)S(1)} %copy-done.15, bf16[16,8,48,896]{3,2,1,0:T(8,128)(2,1)} %bitcast.69, bf16[512,7168]{1,0:T(8,128)(2,1)} %head_ref.1, f32[4,896]{1,0:T(4,128)S(1)} %get-tuple-element.60.inverse_ref.own_ref, ...), custom_call_target="tpu_custom_call" | custom-call | tf_op jit(solution)/shard_map/whole_head/pallas_call | solution.py:608
  244.5 4.1 %collective-permute-start.43 = (f32[48,128]{1,0:T(8,128)}, f32[48,128]{1,0:T(8,128)S(1)}, u32[]{:S(2)}, u32[]{:S(2)}) collective-permute-start(f32[48,128]{1,0:T(8,128)} %merge.3.refs_0_), channel_id=1, source_target_pairs={{0,2},{2,4},{4,6},{6,0},{1,3},{3,5},{5,7},{7,1},{8,10},{10,12},{12... | collective-permute-start | bytes 73736 | tf_op jit(solution)/shard_map/ppermute | solution.py:19
  256.8 5.3 %collective-permute-start.47 = (f32[48,128]{1,0:T(8,128)}, f32[48,128]{1,0:T(8,128)S(1)}, u32[]{:S(2)}, u32[]{:S(2)}) collective-permute-start(f32[48,128]{1,0:T(8,128)} %merge.4.refs_0_), channel_id=1, source_target_pairs={{0,16},{8,24},{16,0},{24,8},{1,17},{9,25},{17,1},{25,9},{2,18},{10... | collective-permute-start | bytes 73736 | tf_op jit(solution)/shard_map/ppermute | solution.py:19
  (196 shorter events, 106.2 us)
Async XLA Ops:
  7.2 56.6 %collective-permute-start.5 = (bf16[7168,256]{1,0:T(8,128)(2,1)}, bf16[7168,256]{1,0:T(8,128)(2,1)}, u32[]{:S(2)}, u32[]{:S(2)}) collective-permute-start(bf16[7168,256]{1,0:T(8,128)(2,1)} %bitcast.63), channel_id=1, source_target_pairs={{0,1},{1,0},{2,3},{3,2},{4,5},{5,4},{6,7},{7,6},{8,9},{9,8},{10,11... | collective-permute-start | bytes 11010056 | tf_op jit(solution)/shard_map/ppermute | solution.py:19
  7.3 56.5 %collective-permute-start.6 = (bf16[7168,256]{1,0:T(8,128)(2,1)}, bf16[7168,256]{1,0:T(8,128)(2,1)}, u32[]{:S(2)}, u32[]{:S(2)}) collective-permute-start(bf16[7168,256]{1,0:T(8,128)(2,1)} %bitcast.66), channel_id=1, source_target_pairs={{0,1},{1,0},{2,3},{3,2},{4,5},{5,4},{6,7},{7,6},{8,9},{9,8},{10,11... | collective-permute-start | bytes 11010056 | tf_op jit(solution)/shard_map/ppermute | solution.py:19
  12.3 22.4 %all-to-all-start = ((bf16[16,40,512]{2,1,0:T(8,128)(2,1)}), bf16[16,40,512]{2,1,0:T(8,128)(2,1)S(1)}, u32[]{:S(2)}, u32[]{:S(2)}) async-start(bf16[16,40,512]{2,1,0:T(8,128)(2,1)} %bitcast.4), calls=%async_computation | async-start | bytes 1310720 | tf_op jit(solution)/shard_map/all_to_all | solution.py:438
  20.2 62.2 %collective-permute-start.10 = (bf16[256,7168]{1,0:T(8,128)(2,1)}, bf16[256,7168]{1,0:T(8,128)(2,1)}, u32[]{:S(2)}, u32[]{:S(2)}) collective-permute-start(bf16[256,7168]{1,0:T(8,128)(2,1)} %bitcast.70), channel_id=1, source_target_pairs={{0,1},{1,0},{2,3},{3,2},{4,5},{5,4},{6,7},{7,6},{8,9},{9,8},{10,11... | collective-permute-start | bytes 11010056 | tf_op jit(solution)/shard_map/ppermute | solution.py:19
  34.7 37.8 %all-to-all-start.1 = ((bf16[16,40,1536]{2,1,0:T(8,128)(2,1)}), bf16[16,40,1536]{2,1,0:T(8,128)(2,1)S(1)}, u32[]{:S(2)}, u32[]{:S(2)}) async-start(bf16[16,40,1536]{2,1,0:T(8,128)(2,1)} %bitcast.60), calls=%async_computation.1 | async-start | bytes 3932160 | tf_op jit(solution)/shard_map/all_to_all | solution.py:438
  41.8 16.3 %collective-permute-start.3 = (bf16[640,512]{1,0:T(8,128)(2,1)S(1)}, bf16[640,512]{1,0:T(8,128)(2,1)S(1)}, u32[]{:S(2)}, u32[]{:S(2)}) collective-permute-start(bf16[640,512]{1,0:T(8,128)(2,1)S(1)} %bitcast.56), channel_id=1, source_target_pairs={{0,2},{2,4},{4,6},{6,0},{1,3},{3,5},{5,7},{7,1},{8,10},{10,12},{12... | collective-permute-start | bytes 1966088 | tf_op jit(solution)/shard_map/ppermute | solution.py:19
  42.4 16.5 %collective-permute-start.4 = (bf16[640,512]{1,0:T(8,128)(2,1)S(1)}, bf16[640,512]{1,0:T(8,128)(2,1)S(1)}, u32[]{:S(2)}, u32[]{:S(2)}) collective-permute-start(bf16[640,512]{1,0:T(8,128)(2,1)S(1)} %bitcast.57), channel_id=1, source_target_pairs={{0,6},{2,0},{4,2},{6,4},{1,7},{3,1},{5,3},{7,5},{8,14},{10,8},{12,... | collective-permute-start | bytes 1966088 | tf_op jit(solution)/shard_map/ppermute | solution.py:19
  58.9 13.6 %collective-permute-start.7 = (bf16[320,512]{1,0:T(8,128)(2,1)}, bf16[320,512]{1,0:T(8,128)(2,1)}, u32[]{:S(2)}, u32[]{:S(2)}) collective-permute-start(bf16[320,512]{1,0:T(8,128)(2,1)} %slice.56), channel_id=1, source_target_pairs={{0,2},{2,4},{4,6},{6,0},{1,3},{3,5},{5,7},{7,1},{8,10},{10,12},{12... | collective-permute-start | bytes 983048 | tf_op jit(solution)/shard_map/ppermute | solution.py:19
  60.5 12.0 %collective-permute-start.8 = (bf16[320,512]{1,0:T(8,128)(2,1)}, bf16[320,512]{1,0:T(8,128)(2,1)}, u32[]{:S(2)}, u32[]{:S(2)}) collective-permute-start(bf16[320,512]{1,0:T(8,128)(2,1)} %slice.57), channel_id=1, source_target_pairs={{0,6},{2,0},{4,2},{6,4},{1,7},{3,1},{5,3},{7,5},{8,14},{10,8},{12,... | collective-permute-start | bytes 983048 | tf_op jit(solution)/shard_map/ppermute | solution.py:19
  96.1 36.4 %all-to-all-start.3 = ((bf16[16,40,1536]{2,1,0:T(8,128)(2,1)}), bf16[16,40,1536]{2,1,0:T(8,128)(2,1)S(1)}, u32[]{:S(2)}, u32[]{:S(2)}) async-start(bf16[16,40,1536]{2,1,0:T(8,128)(2,1)} %bitcast.72), calls=%async_computation.3 | async-start | bytes 3932160 | tf_op jit(solution)/shard_map/all_to_all | solution.py:438
  103.1 10.9 %collective-permute-start.11 = (bf16[320,512]{1,0:T(8,128)(2,1)}, bf16[320,512]{1,0:T(8,128)(2,1)S(1)}, u32[]{:S(2)}, u32[]{:S(2)}) collective-permute-start(bf16[320,512]{1,0:T(8,128)(2,1)} %get-tuple-element.46), channel_id=1, source_target_pairs={{0,6},{2,0},{4,2},{6,4},{1,7},{3,1},{5,3},{7,5},{8,14},{10,8},{12,... | collective-permute-start | bytes 983048 | tf_op jit(solution)/shard_map/ppermute | solution.py:19
  103.6 12.1 %collective-permute-start.12 = (bf16[320,512]{1,0:T(8,128)(2,1)}, bf16[320,512]{1,0:T(8,128)(2,1)S(1)}, u32[]{:S(2)}, u32[]{:S(2)}) collective-permute-start(bf16[320,512]{1,0:T(8,128)(2,1)} %get-tuple-element.48), channel_id=1, source_target_pairs={{0,2},{2,4},{4,6},{6,0},{1,3},{3,5},{5,7},{7,1},{8,10},{10,12},{12... | collective-permute-start | bytes 983048 | tf_op jit(solution)/shard_map/ppermute | solution.py:19
  105.2 15.8 %collective-permute-start.14 = (bf16[320,512]{1,0:T(8,128)(2,1)}, bf16[320,512]{1,0:T(8,128)(2,1)S(1)}, u32[]{:S(2)}, u32[]{:S(2)}) collective-permute-start(bf16[320,512]{1,0:T(8,128)(2,1)} %get-tuple-element.50), channel_id=1, source_target_pairs={{0,6},{2,0},{4,2},{6,4},{1,7},{3,1},{5,3},{7,5},{8,14},{10,8},{12,... | collective-permute-start | bytes 983048 | tf_op jit(solution)/shard_map/ppermute | solution.py:19
  106.9 15.8 %collective-permute-start.15 = (bf16[320,512]{1,0:T(8,128)(2,1)S(1)}, bf16[320,512]{1,0:T(8,128)(2,1)S(1)}, u32[]{:S(2)}, u32[]{:S(2)}) collective-permute-start(bf16[320,512]{1,0:T(8,128)(2,1)S(1)} %copy-done.31), channel_id=1, source_target_pairs={{0,2},{2,4},{4,6},{6,0},{1,3},{3,5},{5,7},{7,1},{8,10},{10,12},{12... | collective-permute-start | bytes 983048 | tf_op jit(solution)/shard_map/ppermute | solution.py:19
  117.9 10.4 %collective-permute-start.16 = (bf16[320,512]{1,0:T(8,128)(2,1)S(1)}, bf16[320,512]{1,0:T(8,128)(2,1)S(1)}, u32[]{:S(2)}, u32[]{:S(2)}) collective-permute-start(bf16[320,512]{1,0:T(8,128)(2,1)S(1)} %get-tuple-element.52), channel_id=1, source_target_pairs={{0,2},{2,4},{4,6},{6,0},{1,3},{3,5},{5,7},{7,1},{8,10},{10,12},{12... | collective-permute-start | bytes 983048 | tf_op jit(solution)/shard_map/ppermute | solution.py:19
  132.5 15.4 %all-to-all-start.2 = ((bf16[16,40,512]{2,1,0:T(8,128)(2,1)}), bf16[16,40,512]{2,1,0:T(8,128)(2,1)S(1)}, u32[]{:S(2)}, u32[]{:S(2)}) async-start(bf16[16,40,512]{2,1,0:T(8,128)(2,1)} %bitcast.11), calls=%async_computation.2 | async-start | bytes 1310720 | tf_op jit(solution)/shard_map/all_to_all | solution.py:438
  136.5 86.2 %all-gather.2.cloned.1.call-start = ((), (), s32[]{:S(2)}) async-start(), calls=%async_computation.4 | async-start | bytes 11096064 | tf_op jit(solution)/shard_map/all_gather | solution.py:567
  149.6 48.1 %collective-permute-start.20 = (bf16[512,7168]{1,0:T(8,128)(2,1)}, bf16[512,7168]{1,0:T(8,128)(2,1)S(1)}, u32[]{:S(2)}, u32[]{:S(2)}) collective-permute-start(bf16[512,7168]{1,0:T(8,128)(2,1)} %head_ref.1), channel_id=1, source_target_pairs={{0,1},{1,0},{2,3},{3,2},{4,5},{5,4},{6,7},{7,6},{8,9},{9,8},{10,11... | collective-permute-start | bytes 22020104 | tf_op jit(solution)/shard_map/ppermute | solution.py:19
  170.6 19.4 %collective-permute-start.36 = (bf16[4,2,48,896]{3,2,1,0:T(8,128)(2,1)S(1)}, bf16[4,2,48,896]{3,2,1,0:T(8,128)(2,1)S(1)}, u32[]{:S(2)}, u32[]{:S(2)}) collective-permute-start(bf16[4,2,48,896]{3,2,1,0:T(8,128)(2,1)S(1)} %pad_maximum_fusion.1.refs_5_), channel_id=1, source_target_pairs={{0,32},{32,64},{64,96},{96,0},{1,33},{33,65},{65,97},{97,1},{2,34}... | collective-permute-start | bytes 2064392 | tf_op jit(solution)/shard_map/ppermute | solution.py:19
  170.7 19.8 %collective-permute-start.38 = (bf16[4,2,48,896]{3,2,1,0:T(8,128)(2,1)S(1)}, bf16[4,2,48,896]{3,2,1,0:T(8,128)(2,1)S(1)}, u32[]{:S(2)}, u32[]{:S(2)}) collective-permute-start(bf16[4,2,48,896]{3,2,1,0:T(8,128)(2,1)S(1)} %pad_maximum_fusion.1.refs_5_), channel_id=1, source_target_pairs={{0,96},{32,0},{64,32},{96,64},{1,97},{33,1},{65,33},{97,65},{2,98}... | collective-permute-start | bytes 2064392 | tf_op jit(solution)/shard_map/ppermute | solution.py:19
  174.1 20.2 %collective-permute-start.26 = (bf16[4,2,48,896]{3,2,1,0:T(8,128)(2,1)S(1)}, bf16[4,2,48,896]{3,2,1,0:T(8,128)(2,1)S(1)}, u32[]{:S(2)}, u32[]{:S(2)}) collective-permute-start(bf16[4,2,48,896]{3,2,1,0:T(8,128)(2,1)S(1)} %pad_maximum_fusion.refs_0_), channel_id=1, source_target_pairs={{0,8},{8,16},{16,24},{24,0},{1,9},{9,17},{17,25},{25,1},{2,10},{10... | collective-permute-start | bytes 2064392 | tf_op jit(solution)/shard_map/ppermute | solution.py:19
  174.2 20.2 %collective-permute-start.28 = (bf16[4,2,48,896]{3,2,1,0:T(8,128)(2,1)S(1)}, bf16[4,2,48,896]{3,2,1,0:T(8,128)(2,1)S(1)}, u32[]{:S(2)}, u32[]{:S(2)}) collective-permute-start(bf16[4,2,48,896]{3,2,1,0:T(8,128)(2,1)S(1)} %pad_maximum_fusion.refs_0_), channel_id=1, source_target_pairs={{0,24},{8,0},{16,8},{24,16},{1,25},{9,1},{17,9},{25,17},{2,26},{10... | collective-permute-start | bytes 2064392 | tf_op jit(solution)/shard_map/ppermute | solution.py:19
  194.4 14.0 %collective-permute-start.29 = (bf16[2,2,48,896]{3,2,1,0:T(8,128)(2,1)S(1)}, bf16[2,2,48,896]{3,2,1,0:T(8,128)(2,1)S(1)}, u32[]{:S(2)}, u32[]{:S(2)}) collective-permute-start(bf16[2,2,48,896]{3,2,1,0:T(8,128)(2,1)S(1)} %slice.61), channel_id=1, source_target_pairs={{0,24},{8,0},{16,8},{24,16},{1,25},{9,1},{17,9},{25,17},{2,26},{10... | collective-permute-start | bytes 1032200 | tf_op jit(solution)/shard_map/ppermute | solution.py:19
  220.9 18.5 %collective-permute-start.40 = (f32[768,640]{1,0:T(8,128)}, f32[768,640]{1,0:T(8,128)S(1)}, u32[]{:S(2)}, u32[]{:S(2)}) collective-permute-start(f32[768,640]{1,0:T(8,128)} %get-tuple-element.63), channel_id=1, source_target_pairs={{0,1},{1,0},{2,3},{3,2},{4,5},{5,4},{6,7},{7,6},{8,9},{9,8},{10,11... | collective-permute-start | bytes 5898248 | tf_op jit(solution)/shard_map/ppermute | solution.py:19
  (65 other events, 407.6 us)
Sparse Core Ops, SparseCore 0:
  149.7 71.3 all-gather.1

commit v5 on v4

--- a/solution.py
+++ b/solution.py
@@ -267,12 +267,11 @@
     return total
 
 
-def half_head_kernel(place_ref, inverse_ref, w0, w1, *refs):
-    *pieces, own_ref, other_ref, w_ref, rows_ref, sems = refs
+def head_kernel(place_ref, inverse_ref, w0, w1, *refs):
+    *pieces, own_ref, other_ref, w_ref, rows_ref, sems, row_sems = refs
     vocab = w0.shape[0]
     tokens, width = pieces[0].shape[2:]
-    line_a, behind_a, far_a1, far_a2, ahead_a = pieces[:5]
-    line_b, behind_b, far_b1, far_b2, ahead_b = pieces[5:]
+    blocks = rows_ref.shape[0]
 
     copies = []
     for j, w in enumerate((w0, w1)):
@@ -285,49 +284,48 @@
                     sems.at[j, k],
                 )
             )
-    for copy in copies:
+    moves = []
+    base = 0
+    for i, piece in enumerate(pieces):
+        count = piece.shape[0]
+        for k in range(4):
+            moves.append(
+                pltpu.make_async_copy(
+                    piece.at[:, k],
+                    rows_ref.at[pl.ds(base, count), :, pl.ds(k * width, width)],
+                    row_sems.at[i, k],
+                )
+            )
+        base += count
+    for copy in moves + copies[4:] + copies[:4]:
         copy.start()
-
-    own_ref[:, vocab:] = jnp.zeros_like(own_ref[:, vocab:])
-
-    def take(ref, place_of, base):
-        @pl.loop(0, ref.shape[0])
-        def _(i):
-            at = pl.ds(pl.multiple_of(place_of(i) * tokens, tokens), tokens)
-            squares = own_ref[at, vocab:]
-            for k in range(2):
-                rows = ref[i, k]
-                first = (base + k) * width
-                rows_ref[at, first : first + width] = rows
-                squares = squares + squares_of(rows, inverse_ref[base + k : base + k + 1])
-            own_ref[at, vocab:] = squares
-
-    for back, ref, skip in (
-        (0, line_a, 0), (1, behind_a, 0), (2, far_a1, 0), (2, far_a2, 2), (3, ahead_a, 0)
-    ):
-        take(ref, lambda i, back=back, skip=skip: (i + skip) * 4 + back, 0)
-    for back, ref, skip in (
-        (0, line_b, 0), (1, behind_b, 0), (2, far_b1, 0), (2, far_b2, 2), (3, ahead_b, 0)
-    ):
-        take(ref, lambda i, back=back, skip=skip: back * 4 + i + skip, 2)
-    other_ref[:, vocab:] = own_ref[:, vocab:]
-    for copy in copies:
-        copy.wait()
-
-    @pl.loop(0, rows_ref.shape[0] // 384)
+    for move in moves:
+        move.wait()
+
+    @pl.loop(0, blocks)
     def _(i):
-        at = pl.ds(pl.multiple_of(i * 384, 384), 384)
-
-        @pl.loop(0, vocab // 256)
-        def _(n):
-            cols = pl.ds(pl.multiple_of(n * 256, 256), 256)
-            for j, ref in ((1, other_ref), (0, own_ref)):
-                ref[at, cols] = lax.dot_general(
-                    rows_ref[at],
-                    w_ref[pl.ds(pl.multiple_of(j * vocab + n * 256, 256), 256), :],
-                    (((1,), (1,)), ((), ())),
-                    preferred_element_type=F32,
-                )
+        at = pl.ds(pl.multiple_of(i * tokens, tokens), tokens)
+        squares = jnp.zeros((tokens, 128), F32)
+        for k in range(4):
+            rows = rows_ref[i, :, k * width : (k + 1) * width]
+            squares = squares + squares_of(rows, inverse_ref[k : k + 1])
+        own_ref[at, vocab:] = squares
+        other_ref[at, vocab:] = squares
+
+    for j, ref in ((1, other_ref), (0, own_ref)):
+        for copy in copies[4 * j : 4 * j + 4]:
+            copy.wait()
+
+        @pl.loop(0, blocks // 8)
+        def _(i, j=j, ref=ref):
+            at = pl.ds(pl.multiple_of(i * 8 * tokens, 8 * tokens), 8 * tokens)
+            rows = rows_ref[pl.ds(i * 8, 8)].reshape(8 * tokens, 4 * width)
+            ref[at, :vocab] = lax.dot_general(
+                rows,
+                w_ref[j * vocab : (j + 1) * vocab, :],
+                (((1,), (1,)), ((), ())),
+                preferred_element_type=F32,
+            )
 
 
 def columns_of(full, ids, wanted):
@@ -338,41 +336,23 @@
     return jnp.where(lane == 0, peak, jnp.where(lane == 1, total, target)).T
 
 
-def whole_head_kernel(model, first_ref, place_ref, rows_ref, head_ref, own_ref, other_ref, wanted_ref, stats_ref, all_ref):
-    nodes, parts, tokens, width = rows_ref.shape
-    squares = 0.0
-    for p in range(parts):
-        rows = rows_ref[:, p].reshape(nodes * tokens, width)
-        all_ref[:, p * width : (p + 1) * width] = rows
-        k = lax.rem(place_ref[0] + 4 - p // 2, 4)
-        mine = place_ref[1] == p % 2
-        inverse = jnp.where(mine, own_ref[pl.ds(k, 1), :], other_ref[pl.ds(k, 1), :])
-        squares = squares + squares_of(rows, inverse)
-    logits = lax.dot_general(
-        all_ref[...], head_ref[...], (((1,), (1,)), ((), ())), preferred_element_type=F32
-    )
-    scale = lax.rsqrt(jnp.sum(squares, axis=1, keepdims=True) / model + 1e-06)
-    ids = first_ref[0] + lax.broadcasted_iota(jnp.int32, logits.shape, 1)
-    columns = columns_of(logits * scale, ids, wanted_ref[...])
-    stats_ref[...] = columns[:8]
-
-
-def stats_kernel(model, first_ref, order_ref, own_ref, got_ref, wanted_ref, whole_ref, stats_ref):
+def stats_kernel(model, first_ref, order_ref, own_ref, got_ref, wanted_ref, before_ref, stats_ref):
     vocab = own_ref.shape[1] - 128
-    nodes, tokens, _ = wanted_ref.shape
-    wanted = jnp.concatenate([wanted_ref[order_ref[i]] for i in range(nodes)], axis=0)
+    nodes, _, tokens, _ = wanted_ref.shape
+    blocks = own_ref.shape[0] // tokens
+    halves = [i // (blocks // 2) for i in range(blocks)]
+    wanted = jnp.concatenate([wanted_ref[order_ref[i], halves[i]] for i in range(blocks)], axis=0)
     squares = jnp.sum(own_ref[:, vocab:] + got_ref[:, vocab:], axis=1, keepdims=True)
     scale = lax.rsqrt(squares / model + 1e-06)
     full = (own_ref[:, :vocab] + got_ref[:, :vocab]) * scale
     ids = first_ref[0] + lax.broadcasted_iota(jnp.int32, full.shape, 1)
     columns = columns_of(full, ids, wanted)
-    stats_ref[...] = jnp.zeros_like(stats_ref)
-    for i in range(nodes):
-        lanes = slice(i * tokens, (i + 1) * tokens)
+    stats_ref[...] = before_ref[...]
+    for i in range(blocks):
         for j in range(3):
-            stats_ref[j * nodes + i : j * nodes + i + 1, :tokens] = whole_ref[j : j + 1, lanes]
-            row = j * nodes + order_ref[i]
-            stats_ref[pl.ds(row, 1), 64 : 64 + tokens] = columns[j : j + 1, lanes]
+            row = columns[j : j + 1, i * tokens : (i + 1) * tokens]
+            lane = 64 * halves[i]
+            stats_ref[pl.ds(j * nodes + order_ref[i], 1), lane : lane + tokens] = row
 
 
 def paired(terms):
@@ -477,7 +457,6 @@
     a2_top, a2_low = shift(a1[:half], "y", 1), shift(a3[half:], "y", -1)
 
     head_other = shift(head, "core", 1)
-    inverse_other = shift(inverse, "core", 1)
     place = jnp.stack([y, core]).astype(jnp.int32)
 
     def rows_of(columns):
@@ -564,83 +543,80 @@
     )(hidden, mix_hi, mix_lo, back_a, own, *arrived, gain.reshape(1, width))
 
     part = tokens // 2
-    everyone = lax.all_gather(scaled[:part], AXES, axis=0, tiled=True)
-    by_y = [scaled[part:]]
-    by_y = by_y + [shift(by_y[0], "y", k) for k in (1, 2, 3)]
-    part_a, part_b = jnp.stack(by_y[:2]), jnp.stack(by_y[2:])
+    by_y = [scaled] + [shift(scaled, "y", k) for k in (1, 2, 3)]
+    part_a = jnp.stack([rows[:part] for rows in by_y])
+    part_b = jnp.stack([rows[part:] for rows in by_y])
     behind_a, far_a1, far_a2, ahead_a = ring(part_a, "x")
     behind_b, far_b1, far_b2, ahead_b = ring(part_b, "z")
     line_a = jnp.stack([part_a, behind_a, jnp.concatenate([far_a1, far_a2]), ahead_a])
     line_b = jnp.stack([part_b, behind_b, jnp.concatenate([far_b1, far_b2]), ahead_b])
-    behind_a, far_a1, far_a2, ahead_a = ring(line_a, "z")
-    behind_b, far_b1, far_b2, ahead_b = ring(line_b, "x")
-
     vocab_rows = head.shape[0]
     first_id = (lax.axis_index(AXES) * vocab_rows).reshape(1).astype(jnp.int32)
     x, z = lax.axis_index("x"), lax.axis_index("z")
-    order = [((x - i) % 4) * 4 + (z - j) % 4 for i in range(4) for j in range(4)]
     wanted = targets.reshape(n_node, 2, part, 1)
-    pieces = (line_a, behind_a, far_a1, far_a2, ahead_a, line_b, behind_b, far_b1, far_b2, ahead_b)
-    rows = n_node * part
-    own, other = pl.pallas_call(
-        half_head_kernel,
-        grid_spec=pltpu.PrefetchScalarGridSpec(
-            num_scalar_prefetch=1,
-            grid=(),
-            in_specs=[in_vmem] + [hbm] * 2 + [in_vmem] * len(pieces),
-            out_specs=[in_vmem] * 2,
-            scratch_shapes=[
-                pltpu.VMEM((2 * vocab_rows, 4 * width), BF),
-                pltpu.VMEM((rows, 4 * width), BF),
-                pltpu.SemaphoreType.DMA((2, 4)),
-            ],
-        ),
-        out_shape=(like(rows, vocab_rows + 128, dtype=F32),) * 2,
-        compiler_params=vmem(VMEM),
-        cost_estimate=pl.CostEstimate(
-            flops=16 * rows * width * vocab_rows, bytes_accessed=16 * width * vocab_rows, transcendentals=0
-        ),
-        name="half_head",
-    )(place, inverse, head, head_other, *pieces)
-    got = shift(other, "core", 1)
-    everyone, own = lax.optimization_barrier((everyone, own))
-    group = 8
-    whole_stats = pl.pallas_call(
-        functools.partial(whole_head_kernel, model),
-        grid_spec=pltpu.PrefetchScalarGridSpec(
-            num_scalar_prefetch=2,
-            grid=(n_node // group,),
-            in_specs=[
-                pl.BlockSpec((group, 8, part, width), lambda n, s, t: (n, 0, 0, 0)),
-                pl.BlockSpec((vocab_rows, model), lambda n, s, t: (0, 0)),
-                pl.BlockSpec((4, width), lambda n, s, t: (0, 0)),
-                pl.BlockSpec((4, width), lambda n, s, t: (0, 0)),
-                pl.BlockSpec((group * part, 1), lambda n, s, t: (n, 0)),
-            ],
-            out_specs=pl.BlockSpec((8, group * part), lambda n, s, t: (0, n)),
-            scratch_shapes=[pltpu.VMEM((group * part, model), BF)],
-        ),
-        out_shape=like(8, rows, dtype=F32),
-        compiler_params=vmem(VMEM),
-        name="whole_head",
-    )(
-        first_id,
-        place,
-        everyone.reshape(n_node, 8, part, width),
-        head,
-        inverse,
-        inverse_other,
-        wanted[:, 0].reshape(rows, 1),
-    )
-    stats = pl.pallas_call(
-        functools.partial(stats_kernel, model),
-        grid_spec=pltpu.PrefetchScalarGridSpec(
-            num_scalar_prefetch=2, grid=(), in_specs=[in_vmem] * 4, out_specs=in_vmem
-        ),
-        out_shape=like(3 * n_node, 128, dtype=F32),
-        compiler_params=vmem(VMEM),
-        name="stats",
-    )(first_id, jnp.stack(order).astype(jnp.int32), own, got, wanted[:, 1], whole_stats)
+
+    def node_at(back_x, back_z):
+        return ((x - back_x) % 4) * 4 + (z - back_z) % 4
+
+    def scored(pieces):
+        rows = sum(piece.shape[0] for piece in pieces) * part
+        own, other = pl.pallas_call(
+            head_kernel,
+            grid_spec=pltpu.PrefetchScalarGridSpec(
+                num_scalar_prefetch=1,
+                grid=(),
+                in_specs=[in_vmem] + [hbm] * (2 + len(pieces)),
+                out_specs=[in_vmem] * 2,
+                scratch_shapes=[
+                    pltpu.VMEM((2 * vocab_rows, 4 * width), BF),
+                    pltpu.VMEM((rows // part, part, 4 * width), BF),
+                    pltpu.SemaphoreType.DMA((2, 4)),
+                    pltpu.SemaphoreType.DMA((len(pieces), 4)),
+                ],
+            ),
+            out_shape=(like(rows, vocab_rows + 128, dtype=F32),) * 2,
+            compiler_params=vmem(VMEM),
+            cost_estimate=pl.CostEstimate(
+                flops=16 * rows * width * vocab_rows,
+                bytes_accessed=16 * width * vocab_rows,
+                transcendentals=0,
+            ),
+            name="head",
+        )(place, inverse, head, head_other, *pieces)
+        return own, other
+
+    def counted(own, got, order, stats):
+        return pl.pallas_call(
+            functools.partial(stats_kernel, model),
+            grid_spec=pltpu.PrefetchScalarGridSpec(
+                num_scalar_prefetch=2, grid=(), in_specs=[in_vmem] * 4, out_specs=in_vmem
+            ),
+            out_shape=like(3 * n_node, 128, dtype=F32),
+            compiler_params=vmem(VMEM),
+            cost_estimate=pl.CostEstimate(flops=1000, bytes_accessed=1000, transcendentals=0),
+            name="stats",
+        )(first_id, jnp.stack(order).astype(jnp.int32), own, got, wanted, stats)
+
+    behind_a, ahead_a = shift(line_a, "z", 1), shift(line_a, "z", -1)
+    behind_b, ahead_b = shift(line_b, "x", 1), shift(line_b, "x", -1)
+    scores = scored((line_a, line_b))
+    nearby = (behind_a, ahead_a, behind_b, ahead_b)
+    nearby, (own, other) = lax.optimization_barrier((nearby, scores))
+    behind_a, ahead_a, behind_b, ahead_b = nearby
+    far_a1, far_a2 = shift(behind_a[:2], "z", 1), shift(ahead_a[2:], "z", -1)
+    far_b1, far_b2 = shift(behind_b[:2], "x", 1), shift(ahead_b[2:], "x", -1)
+    order = [node_at(i, 0) for i in range(4)] + [node_at(0, i) for i in range(4)]
+    stats = jnp.zeros((3 * n_node, 128), F32)
+    stats = counted(own, shift(other, "core", 1), order, stats)
+    scores = scored((behind_a, ahead_a, behind_b, ahead_b))
+    far = (far_a1, far_a2, far_b1, far_b2)
+    far, (own, other), stats = lax.optimization_barrier((far, scores, stats))
+    order = [node_at(i, k) for k in (1, 3) for i in range(4)]
+    order = order + [node_at(k, i) for k in (1, 3) for i in range(4)]
+    stats = counted(own, shift(other, "core", 1), order, stats)
+    own, other = scored(far)
+    order = [node_at(i, 2) for i in range(4)] + [node_at(2, i) for i in range(4)]
+    stats = counted(own, shift(other, "core", 1), order, stats)
     for axis in ("core", "y", "z"):
         stats = pl.pallas_call(
             merge_kernel, out_shape=like(3 * n_node, 128, dtype=F32), name="merge"

time: 285 us -> 291 us (1.021); the launches traced: 283 us -> 286 us
  between operations: 14.7 us -> 1.47 us
  local copies, waits for them, and re-layouts: 17.7 us -> 26.6 us
  starting transfers between devices: 95.7 us -> 103 us
  waiting for transfers between devices: 89.6 us -> 86.6 us
    unnamed x64 -> x84, local copies, waits for them, and re-layouts: 14.1 us -> 20.4 us
    ppermute x52 -> x53, starting transfers between devices: 69.5 us -> 75.7 us  [shift(): lax.ppermute(value, axis, [(i, (i + step) % size) for i in range(size)])]
    slice x1 -> x4, local copies, waits for them, and re-layouts: 0.03 us -> 3.65 us  [the longest x2 1.83 us: shards(): far_b1, far_b2 = (shift(behind_b[:2], 'x', 1), shift(ahead_b[2:], 'x', -1))]
    pallas_call x3 -> x6, Pallas kernels: 28.8 us -> 30.7 us  [the longest x3 24 us: scored(): pl.pallas_call(head_kernel, grid_spec=pltpu.PrefetchScalarGridSpec(num_sc...]
    ppermute x52 -> x53, waiting for transfers between devices: 78.6 us -> 76.9 us  [shift(): lax.ppermute(value, axis, [(i, (i + step) % size) for i in range(size)])]
  transfers between devices with their start and end apart: 57 -> 57, of which waited for: 31 -> 31; matrix products, arithmetic and copies ran while one was open for 1% -> 2% of each run, Pallas kernels for 17% -> 21%
where the time goes in v5:
time: 291 us; the launch traced here: 286 us
  starting transfers between devices  103 us (35%)
  waiting for transfers between devices  86.6 us (30%)
  Pallas kernels  67.2 us (23%)
  local copies, waits for them, and re-layouts  26.6 us (9%)
    ppermute x53, waiting for transfers between devices, shift(): lax.ppermute(value, axis, [(i, (i + step) % size) for i in range(size)])  76.9 us
    ppermute x53, starting transfers between devices, shift(): lax.ppermute(value, axis, [(i, (i + step) % size) for i in range(size)])  75.7 us
    all_to_all x4, starting transfers between devices, over_nodes(): lax.all_to_all(cut, ('x', 'z'), split_axis=0, concat_axis=0, tiled=True)  27.8 us
    pallas_call x3, Pallas kernels, scored(): pl.pallas_call(head_kernel, grid_spec=pltpu.PrefetchScalarGridSpec(num_sc...  24 us
    unnamed x84, local copies, waits for them, and re-layouts  20.4 us
    pallas_call x1, Pallas kernels, shards(): pl.pallas_call(up_second_kernel, grid_spec=pltpu.PrefetchScalarGridSpec(n...  9.81 us
    all_to_all x4, waiting for transfers between devices, over_nodes(): lax.all_to_all(cut, ('x', 'z'), split_axis=0, concat_axis=0, tiled=True)  9.72 us
    pallas_call x1, Pallas kernels, shards(): pl.pallas_call(down_kernel, grid_spec=pltpu.PrefetchScalarGridSpec(num_sc...  9.5 us
  transfers between devices with their start and end apart: 57, of which 31 were waited for; matrix products, arithmetic and copies ran while one was open for 2% of the time, Pallas kernels for 21%

profile of v5, /device:TPU:0, one launch (start us, length us, event | category | flops | bytes accessed | tf_op | source)
XLA Modules:
  0.0 286.1 jit_solution(4702895306881854143)
XLA Ops:
  6.4 8.0 %all-to-all-start = ((bf16[16,40,512]{2,1,0:T(8,128)(2,1)}), bf16[16,40,512]{2,1,0:T(8,128)(2,1)S(1)}, u32[]{:S(2)}, u32[]{:S(2)}) async-start(bf16[16,40,512]{2,1,0:T(8,128)(2,1)} %bitcast.4), calls=%async_computation | async-start | bytes 1310720 | tf_op jit(solution)/shard_map/all_to_all | solution.py:418
  27.5 6.9 %all-to-all-start.1 = ((bf16[16,40,1536]{2,1,0:T(8,128)(2,1)}), bf16[16,40,1536]{2,1,0:T(8,128)(2,1)S(1)}, u32[]{:S(2)}, u32[]{:S(2)}) async-start(bf16[16,40,1536]{2,1,0:T(8,128)(2,1)} %bitcast.69), calls=%async_computation.1 | async-start | bytes 3932160 | tf_op jit(solution)/shard_map/all_to_all | solution.py:418
  37.9 12.8 %collective-permute-done.3.a1 = bf16[640,512]{1,0:T(8,128)(2,1)S(1)} collective-permute-done((bf16[640,512]{1,0:T(8,128)(2,1)S(1)}, bf16[640,512]{1,0:T(8,128)(2,1)S(1)}, u32[]{:S(2)}, u32[]{:S(2)}) %collective-permute-start.3) | collective-permute-done | bytes 655392 | tf_op jit(solution)/shard_map/ppermute | solution.py:19
  57.5 6.1 %up_first.1.before_ref = f32[640,1024]{1,0:T(8,128)S(1)} custom-call(s32[2]{0:T(128)S(1)} %pad_add_fusion.place_ref, bf16[640,512]{1,0:T(8,128)(2,1)S(1)} %bitcast.67, bf16[640,512]{1,0:T(8,128)(2,1)S(1)} %collective-permute-done.3.a1, bf16[640,512]{1,0:T(8,128)(2,1)S(1)} %copy-done.6, bf16[7168,256]{1,0:T(8,128)(2,1)} %bitcast.73, ...), custom_call_target="tpu_custom_call" | custom-call | flops 2013265920 | bytes 3145728 | tf_op jit(solution)/shard_map/up_first/pallas_call | solution.py:468
  65.2 9.8 %up_second.1 = (f32[640,1024]{1,0:T(8,128)}, bf16[640,1024]{1,0:T(8,128)(2,1)S(1)}) custom-call(s32[2]{0:T(128)S(1)} %pad_add_fusion.place_ref, f32[640,1024]{1,0:T(8,128)} %copy-done, bf16[640,1536]{1,0:T(8,128)(2,1)S(1)} %bitcast.64, bf16[320,512]{1,0:T(8,128)(2,1)} %collective-permute-done.7.a2_top, bf16[320,512]{1,0:T(8,128)(2,1)} %collective-permute-done.8.a2_low, ...), custom_call_target="tpu_custom_call" | custom-call | tf_op jit(solution)/shard_map/up_second/pallas_call | solution.py:484
  79.2 9.5 %down.1 = (bf16[640,512]{1,0:T(8,128)(2,1)}, bf16[320,512]{1,0:T(8,128)(2,1)}, bf16[320,512]{1,0:T(8,128)(2,1)}, bf16[320,512]{1,0:T(8,128)(2,1)}, bf16[320,512]...) custom-call(s32[2]{0:T(128)} %copy-done.25, ...), custom_call_target="tpu_custom_call" | custom-call | tf_op jit(solution)/shard_map/down/pallas_call | solution.py:502
  88.7 7.0 %all-to-all-start.3 = ((bf16[16,40,1536]{2,1,0:T(8,128)(2,1)}), bf16[16,40,1536]{2,1,0:T(8,128)(2,1)S(1)}, u32[]{:S(2)}, u32[]{:S(2)}) async-start(bf16[16,40,1536]{2,1,0:T(8,128)(2,1)} %bitcast.80), calls=%async_computation.3 | async-start | bytes 3932160 | tf_op jit(solution)/shard_map/all_to_all | solution.py:418
  101.6 5.2 %collective-permute-done.11.got1 = bf16[320,512]{1,0:T(8,128)(2,1)S(1)} collective-permute-done((bf16[320,512]{1,0:T(8,128)(2,1)}, bf16[320,512]{1,0:T(8,128)(2,1)S(1)}, u32[]{:S(2)}, u32[]{:S(2)}) %collective-permute-start.11) | collective-permute-done | bytes 327712 | tf_op jit(solution)/shard_map/ppermute | solution.py:19
  106.7 3.6 %collective-permute-done.12.got3 = bf16[320,512]{1,0:T(8,128)(2,1)S(1)} collective-permute-done((bf16[320,512]{1,0:T(8,128)(2,1)}, bf16[320,512]{1,0:T(8,128)(2,1)S(1)}, u32[]{:S(2)}, u32[]{:S(2)}) %collective-permute-start.12) | collective-permute-done | bytes 327712 | tf_op jit(solution)/shard_map/ppermute | solution.py:19
  113.8 3.6 %collective-permute-done.15.right_top = bf16[320,512]{1,0:T(8,128)(2,1)S(1)} collective-permute-done((bf16[320,512]{1,0:T(8,128)(2,1)}, bf16[320,512]{1,0:T(8,128)(2,1)S(1)}, u32[]{:S(2)}, u32[]{:S(2)}) %collective-permute-start.15) | collective-permute-done | bytes 327712 | tf_op jit(solution)/shard_map/ppermute | solution.py:19
  119.6 3.4 %collective-permute-done.16.right_low = bf16[320,512]{1,0:T(8,128)(2,1)S(1)} collective-permute-done((bf16[320,512]{1,0:T(8,128)(2,1)S(1)}, bf16[320,512]{1,0:T(8,128)(2,1)S(1)}, u32[]{:S(2)}, u32[]{:S(2)}) %collective-permute-start.16) | collective-permute-done | bytes 327712 | tf_op jit(solution)/shard_map/ppermute | solution.py:19
  125.1 5.9 %all-to-all-start.2 = ((bf16[16,40,512]{2,1,0:T(8,128)(2,1)}), bf16[16,40,512]{2,1,0:T(8,128)(2,1)S(1)}, u32[]{:S(2)}, u32[]{:S(2)}) async-start(bf16[16,40,512]{2,1,0:T(8,128)(2,1)} %bitcast.11), calls=%async_computation.2 | async-start | bytes 1310720 | tf_op jit(solution)/shard_map/all_to_all | solution.py:418
  134.0 8.4 %all-to-all-done.2 = bf16[16,40,512]{2,1,0:T(8,128)(2,1)S(1)} async-done(((bf16[16,40,512]{2,1,0:T(8,128)(2,1)}), bf16[16,40,512]{2,1,0:T(8,128)(2,1)S(1)}, u32[]{:S(2)}, u32[]{:S(2)}) %all-to-all-start.2) | async-done | bytes 655392 | tf_op jit(solution)/shard_map/all_to_all | solution.py:418
  146.8 5.2 %collective-permute-done.21 = bf16[96,896]{1,0:T(8,128)(2,1)S(1)} collective-permute-done((bf16[96,896]{1,0:T(8,128)(2,1)S(1)}, bf16[96,896]{1,0:T(8,128)(2,1)S(1)}, u32[]{:S(2)}, u32[]{:S(2)}) %collective-permute-start.21) | collective-permute-done | bytes 172064 | tf_op jit(solution)/shard_map/ppermute | solution.py:19
  159.7 3.3 %collective-permute-done.30 = bf16[4,48,896]{2,1,0:T(8,128)(2,1)S(1)} collective-permute-done((bf16[4,48,896]{2,1,0:T(8,128)(2,1)S(1)}, bf16[4,48,896]{2,1,0:T(8,128)(2,1)S(1)}, u32[]{:S(2)}, u32[]{:S(2)}) %collective-permute-start.30) | collective-permute-done | bytes 344096 | tf_op jit(solution)/shard_map/ppermute | solution.py:19
  163.1 3.4 %collective-permute-start.33 = (bf16[2,48,896]{2,1,0:T(8,128)(2,1)S(1)}, bf16[2,48,896]{2,1,0:T(8,128)(2,1)S(1)}, u32[]{:S(2)}, u32[]{:S(2)}) collective-permute-start(bf16[2,48,896]{2,1,0:T(8,128)(2,1)S(1)} %slice.83), channel_id=1, source_target_pairs={{0,24},{8,0},{16,8},{24,16},{1,25},{9,1},{17,9},{25,17},{2,26},{10... | collective-permute-start | bytes 516104 | tf_op jit(solution)/shard_map/ppermute | solution.py:19
  166.8 3.3 %collective-permute-start.27 = (bf16[2,48,896]{2,1,0:T(8,128)(2,1)S(1)}, bf16[2,48,896]{2,1,0:T(8,128)(2,1)S(1)}, u32[]{:S(2)}, u32[]{:S(2)}) collective-permute-start(bf16[2,48,896]{2,1,0:T(8,128)(2,1)S(1)} %slice.78), channel_id=1, source_target_pairs={{0,96},{32,0},{64,32},{96,64},{1,97},{33,1},{65,33},{97,65},{2,98}... | collective-permute-start | bytes 516104 | tf_op jit(solution)/shard_map/ppermute | solution.py:19
  178.8 6.2 %head.3 = (f32[384,640]{1,0:T(8,128)S(1)}, f32[384,640]{1,0:T(8,128)}) custom-call(s32[2]{0:T(128)S(1)} %copy-done.26, f32[4,896]{1,0:T(4,128)S(1)} %get-tuple-element.74.inverse_ref, bf16[512,7168]{1,0:T(8,128)(2,1)} %w0.5, bf16[512,7168]{1,0:T(8,128)(2,1)} %collective-permute-done.20.w1, bf16[4,4,48,896]{3,2,1,0:T(8,128)(2,1)S(1)} %pad_maximum_fusion.refs_0_, ...), custom_call_target="tpu_custom_call" | custom-call | flops 2818572288 | bytes 7340032 | tf_op jit(solution)/shard_map/head/pallas_call | solution.py:563
  185.0 13.9 %collective-permute-done.34.refs_2_ = bf16[4,4,48,896]{3,2,1,0:T(8,128)(2,1)S(1)} collective-permute-done((bf16[4,4,48,896]{3,2,1,0:T(8,128)(2,1)S(1)}, bf16[4,4,48,896]{3,2,1,0:T(8,128)(2,1)S(1)}, u32[]{:S(2)}, u32[]{:S(2)}) %collective-permute-start.34) | collective-permute-done | bytes 1376288 | tf_op jit(solution)/shard_map/ppermute | solution.py:19
  202.4 10.1 %collective-permute-start.36 = (bf16[2,4,48,896]{3,2,1,0:T(8,128)(2,1)}, bf16[2,4,48,896]{3,2,1,0:T(8,128)(2,1)S(1)}, u32[]{:S(2)}, u32[]{:S(2)}) collective-permute-start(bf16[2,4,48,896]{3,2,1,0:T(8,128)(2,1)} %slice.68), channel_id=1, source_target_pairs={{0,8},{8,16},{16,24},{24,0},{1,9},{9,17},{17,25},{25,1},{2,10},{10... | collective-permute-start | bytes 2064392 | tf_op jit(solution)/shard_map/ppermute | solution.py:19
  227.8 11.0 %head.4 = (f32[768,640]{1,0:T(8,128)}, f32[768,640]{1,0:T(8,128)}) custom-call(s32[2]{0:T(128)S(1)} %copy-done.26, f32[4,896]{1,0:T(4,128)S(1)} %get-tuple-element.74.inverse_ref, bf16[512,7168]{1,0:T(8,128)(2,1)} %w0.5, bf16[512,7168]{1,0:T(8,128)(2,1)} %collective-permute-done.20.w1, bf16[4,4,48,896]{3,2,1,0:T(8,128)(2,1)S(1)} %copy-done.19, ...), custom_call_target="tpu_custom_call" | custom-call | flops 5637144576 | bytes 7340032 | tf_op jit(solution)/shard_map/head/pallas_call | solution.py:563
  240.1 6.9 %head.5 = (f32[384,640]{1,0:T(8,128)S(1)}, f32[384,640]{1,0:T(8,128)}) custom-call(s32[2]{0:T(128)S(1)} %copy-done.26, f32[4,896]{1,0:T(4,128)S(1)} %get-tuple-element.74.inverse_ref, bf16[512,7168]{1,0:T(8,128)(2,1)} %w0.5, bf16[512,7168]{1,0:T(8,128)(2,1)} %collective-permute-done.20.w1, bf16[2,4,48,896]{3,2,1,0:T(8,128)(2,1)S(1)} %collective-permute-done.36.refs_0_, ...), custom_call_target="tpu_custom_call" | custom-call | flops 2818572288 | bytes 7340032 | tf_op jit(solution)/shard_map/head/pallas_call | solution.py:563
  257.6 3.5 %collective-permute-start.45 = (f32[48,128]{1,0:T(8,128)}, f32[48,128]{1,0:T(8,128)S(1)}, u32[]{:S(2)}, u32[]{:S(2)}) collective-permute-start(f32[48,128]{1,0:T(8,128)} %merge.3.refs_0_), channel_id=1, source_target_pairs={{0,4},{2,6},{4,0},{6,2},{1,5},{3,7},{5,1},{7,3},{8,12},{10,14},{12... | collective-permute-start | bytes 73736 | tf_op jit(solution)/shard_map/ppermute | solution.py:19
  267.2 3.3 %collective-permute-start.48 = (f32[48,128]{1,0:T(8,128)}, f32[48,128]{1,0:T(8,128)S(1)}, u32[]{:S(2)}, u32[]{:S(2)}) collective-permute-start(f32[48,128]{1,0:T(8,128)} %merge.4.refs_0_), channel_id=1, source_target_pairs={{0,16},{8,24},{16,0},{24,8},{1,17},{9,25},{17,1},{25,9},{2,18},{10... | collective-permute-start | bytes 73736 | tf_op jit(solution)/shard_map/ppermute | solution.py:19
  (221 shorter events, 124.3 us)
Async XLA Ops:
  0.6 52.8 %collective-permute-start.5 = (bf16[7168,256]{1,0:T(8,128)(2,1)}, bf16[7168,256]{1,0:T(8,128)(2,1)}, u32[]{:S(2)}, u32[]{:S(2)}) collective-permute-start(bf16[7168,256]{1,0:T(8,128)(2,1)} %bitcast.72), channel_id=1, source_target_pairs={{0,1},{1,0},{2,3},{3,2},{4,5},{5,4},{6,7},{7,6},{8,9},{9,8},{10,11... | collective-permute-start | bytes 11010056 | tf_op jit(solution)/shard_map/ppermute | solution.py:19
  0.7 55.6 %collective-permute-start.6 = (bf16[7168,256]{1,0:T(8,128)(2,1)}, bf16[7168,256]{1,0:T(8,128)(2,1)}, u32[]{:S(2)}, u32[]{:S(2)}) collective-permute-start(bf16[7168,256]{1,0:T(8,128)(2,1)} %bitcast.75), channel_id=1, source_target_pairs={{0,1},{1,0},{2,3},{3,2},{4,5},{5,4},{6,7},{7,6},{8,9},{9,8},{10,11... | collective-permute-start | bytes 11010056 | tf_op jit(solution)/shard_map/ppermute | solution.py:19
  6.4 21.1 %all-to-all-start = ((bf16[16,40,512]{2,1,0:T(8,128)(2,1)}), bf16[16,40,512]{2,1,0:T(8,128)(2,1)S(1)}, u32[]{:S(2)}, u32[]{:S(2)}) async-start(bf16[16,40,512]{2,1,0:T(8,128)(2,1)} %bitcast.4), calls=%async_computation | async-start | bytes 1310720 | tf_op jit(solution)/shard_map/all_to_all | solution.py:418
  14.4 60.7 %collective-permute-start.10 = (bf16[256,7168]{1,0:T(8,128)(2,1)}, bf16[256,7168]{1,0:T(8,128)(2,1)}, u32[]{:S(2)}, u32[]{:S(2)}) collective-permute-start(bf16[256,7168]{1,0:T(8,128)(2,1)} %bitcast.78), channel_id=1, source_target_pairs={{0,1},{1,0},{2,3},{3,2},{4,5},{5,4},{6,7},{7,6},{8,9},{9,8},{10,11... | collective-permute-start | bytes 11010056 | tf_op jit(solution)/shard_map/ppermute | solution.py:19
  27.5 37.6 %all-to-all-start.1 = ((bf16[16,40,1536]{2,1,0:T(8,128)(2,1)}), bf16[16,40,1536]{2,1,0:T(8,128)(2,1)S(1)}, u32[]{:S(2)}, u32[]{:S(2)}) async-start(bf16[16,40,1536]{2,1,0:T(8,128)(2,1)} %bitcast.69), calls=%async_computation.1 | async-start | bytes 3932160 | tf_op jit(solution)/shard_map/all_to_all | solution.py:418
  34.4 16.3 %collective-permute-start.3 = (bf16[640,512]{1,0:T(8,128)(2,1)S(1)}, bf16[640,512]{1,0:T(8,128)(2,1)S(1)}, u32[]{:S(2)}, u32[]{:S(2)}) collective-permute-start(bf16[640,512]{1,0:T(8,128)(2,1)S(1)} %bitcast.65), channel_id=1, source_target_pairs={{0,2},{2,4},{4,6},{6,0},{1,3},{3,5},{5,7},{7,1},{8,10},{10,12},{12... | collective-permute-start | bytes 1966088 | tf_op jit(solution)/shard_map/ppermute | solution.py:19
  34.9 16.6 %collective-permute-start.4 = (bf16[640,512]{1,0:T(8,128)(2,1)S(1)}, bf16[640,512]{1,0:T(8,128)(2,1)S(1)}, u32[]{:S(2)}, u32[]{:S(2)}) collective-permute-start(bf16[640,512]{1,0:T(8,128)(2,1)S(1)} %bitcast.66), channel_id=1, source_target_pairs={{0,6},{2,0},{4,2},{6,4},{1,7},{3,1},{5,3},{7,5},{8,14},{10,8},{12,... | collective-permute-start | bytes 1966088 | tf_op jit(solution)/shard_map/ppermute | solution.py:19
  50.7 128.1 %collective-permute-start.20 = (bf16[512,7168]{1,0:T(8,128)(2,1)}, bf16[512,7168]{1,0:T(8,128)(2,1)}, u32[]{:S(2)}, u32[]{:S(2)}) collective-permute-start(bf16[512,7168]{1,0:T(8,128)(2,1)} %w0.5), channel_id=1, source_target_pairs={{0,1},{1,0},{2,3},{3,2},{4,5},{5,4},{6,7},{7,6},{8,9},{9,8},{10,11... | collective-permute-start | bytes 22020104 | tf_op jit(solution)/shard_map/ppermute | solution.py:19
  51.5 13.6 %collective-permute-start.7 = (bf16[320,512]{1,0:T(8,128)(2,1)}, bf16[320,512]{1,0:T(8,128)(2,1)}, u32[]{:S(2)}, u32[]{:S(2)}) collective-permute-start(bf16[320,512]{1,0:T(8,128)(2,1)} %slice.72), channel_id=1, source_target_pairs={{0,2},{2,4},{4,6},{6,0},{1,3},{3,5},{5,7},{7,1},{8,10},{10,12},{12... | collective-permute-start | bytes 983048 | tf_op jit(solution)/shard_map/ppermute | solution.py:19
  88.7 36.4 %all-to-all-start.3 = ((bf16[16,40,1536]{2,1,0:T(8,128)(2,1)}), bf16[16,40,1536]{2,1,0:T(8,128)(2,1)S(1)}, u32[]{:S(2)}, u32[]{:S(2)}) async-start(bf16[16,40,1536]{2,1,0:T(8,128)(2,1)} %bitcast.80), calls=%async_computation.3 | async-start | bytes 3932160 | tf_op jit(solution)/shard_map/all_to_all | solution.py:418
  98.3 12.1 %collective-permute-start.12 = (bf16[320,512]{1,0:T(8,128)(2,1)}, bf16[320,512]{1,0:T(8,128)(2,1)S(1)}, u32[]{:S(2)}, u32[]{:S(2)}) collective-permute-start(bf16[320,512]{1,0:T(8,128)(2,1)} %get-tuple-element.63), channel_id=1, source_target_pairs={{0,2},{2,4},{4,6},{6,0},{1,3},{3,5},{5,7},{7,1},{8,10},{10,12},{12... | collective-permute-start | bytes 983048 | tf_op jit(solution)/shard_map/ppermute | solution.py:19
  98.3 15.4 %collective-permute-start.14 = (bf16[320,512]{1,0:T(8,128)(2,1)}, bf16[320,512]{1,0:T(8,128)(2,1)S(1)}, u32[]{:S(2)}, u32[]{:S(2)}) collective-permute-start(bf16[320,512]{1,0:T(8,128)(2,1)} %get-tuple-element.65), channel_id=1, source_target_pairs={{0,6},{2,0},{4,2},{6,4},{1,7},{3,1},{5,3},{7,5},{8,14},{10,8},{12,... | collective-permute-start | bytes 983048 | tf_op jit(solution)/shard_map/ppermute | solution.py:19
  101.5 15.8 %collective-permute-start.15 = (bf16[320,512]{1,0:T(8,128)(2,1)}, bf16[320,512]{1,0:T(8,128)(2,1)S(1)}, u32[]{:S(2)}, u32[]{:S(2)}) collective-permute-start(bf16[320,512]{1,0:T(8,128)(2,1)} %get-tuple-element.66), channel_id=1, source_target_pairs={{0,2},{2,4},{4,6},{6,0},{1,3},{3,5},{5,7},{7,1},{8,10},{10,12},{12... | collective-permute-start | bytes 983048 | tf_op jit(solution)/shard_map/ppermute | solution.py:19
  110.6 12.4 %collective-permute-start.16 = (bf16[320,512]{1,0:T(8,128)(2,1)S(1)}, bf16[320,512]{1,0:T(8,128)(2,1)S(1)}, u32[]{:S(2)}, u32[]{:S(2)}) collective-permute-start(bf16[320,512]{1,0:T(8,128)(2,1)S(1)} %get-tuple-element.67), channel_id=1, source_target_pairs={{0,2},{2,4},{4,6},{6,0},{1,3},{3,5},{5,7},{7,1},{8,10},{10,12},{12... | collective-permute-start | bytes 983048 | tf_op jit(solution)/shard_map/ppermute | solution.py:19
  125.1 17.4 %all-to-all-start.2 = ((bf16[16,40,512]{2,1,0:T(8,128)(2,1)}), bf16[16,40,512]{2,1,0:T(8,128)(2,1)S(1)}, u32[]{:S(2)}, u32[]{:S(2)}) async-start(bf16[16,40,512]{2,1,0:T(8,128)(2,1)} %bitcast.11), calls=%async_computation.2 | async-start | bytes 1310720 | tf_op jit(solution)/shard_map/all_to_all | solution.py:418
  170.3 28.6 %collective-permute-start.34 = (bf16[4,4,48,896]{3,2,1,0:T(8,128)(2,1)S(1)}, bf16[4,4,48,896]{3,2,1,0:T(8,128)(2,1)S(1)}, u32[]{:S(2)}, u32[]{:S(2)}) collective-permute-start(bf16[4,4,48,896]{3,2,1,0:T(8,128)(2,1)S(1)} %pad_maximum_fusion.1.refs_1_), channel_id=1, source_target_pairs={{0,32},{32,64},{64,96},{96,0},{1,33},{33,65},{65,97},{97,1},{2,34}... | collective-permute-start | bytes 4128776 | tf_op jit(solution)/shard_map/ppermute | solution.py:19
  170.4 28.5 %collective-permute-start.35 = (bf16[4,4,48,896]{3,2,1,0:T(8,128)(2,1)S(1)}, bf16[4,4,48,896]{3,2,1,0:T(8,128)(2,1)S(1)}, u32[]{:S(2)}, u32[]{:S(2)}) collective-permute-start(bf16[4,4,48,896]{3,2,1,0:T(8,128)(2,1)S(1)} %pad_maximum_fusion.1.refs_1_), channel_id=1, source_target_pairs={{0,96},{32,0},{64,32},{96,64},{1,97},{33,1},{65,33},{97,65},{2,98}... | collective-permute-start | bytes 4128776 | tf_op jit(solution)/shard_map/ppermute | solution.py:19
  175.5 24.9 %collective-permute-start.28 = (bf16[4,4,48,896]{3,2,1,0:T(8,128)(2,1)S(1)}, bf16[4,4,48,896]{3,2,1,0:T(8,128)(2,1)S(1)}, u32[]{:S(2)}, u32[]{:S(2)}) collective-permute-start(bf16[4,4,48,896]{3,2,1,0:T(8,128)(2,1)S(1)} %pad_maximum_fusion.refs_0_), channel_id=1, source_target_pairs={{0,8},{8,16},{16,24},{24,0},{1,9},{9,17},{17,25},{25,1},{2,10},{10... | collective-permute-start | bytes 4128776 | tf_op jit(solution)/shard_map/ppermute | solution.py:19
  175.6 24.8 %collective-permute-start.29 = (bf16[4,4,48,896]{3,2,1,0:T(8,128)(2,1)S(1)}, bf16[4,4,48,896]{3,2,1,0:T(8,128)(2,1)S(1)}, u32[]{:S(2)}, u32[]{:S(2)}) collective-permute-start(bf16[4,4,48,896]{3,2,1,0:T(8,128)(2,1)S(1)} %pad_maximum_fusion.refs_0_), channel_id=1, source_target_pairs={{0,24},{8,0},{16,8},{24,16},{1,25},{9,1},{17,9},{25,17},{2,26},{10... | collective-permute-start | bytes 4128776 | tf_op jit(solution)/shard_map/ppermute | solution.py:19
  200.4 38.4 %collective-permute-start.40 = (f32[384,640]{1,0:T(8,128)}, f32[384,640]{1,0:T(8,128)S(1)}, u32[]{:S(2)}, u32[]{:S(2)}) collective-permute-start(f32[384,640]{1,0:T(8,128)} %get-tuple-element.85), channel_id=1, source_target_pairs={{0,1},{1,0},{2,3},{3,2},{4,5},{5,4},{6,7},{7,6},{8,9},{9,8},{10,11... | collective-permute-start | bytes 2949128 | tf_op jit(solution)/shard_map/ppermute | solution.py:19
  202.4 37.6 %collective-permute-start.36 = (bf16[2,4,48,896]{3,2,1,0:T(8,128)(2,1)}, bf16[2,4,48,896]{3,2,1,0:T(8,128)(2,1)S(1)}, u32[]{:S(2)}, u32[]{:S(2)}) collective-permute-start(bf16[2,4,48,896]{3,2,1,0:T(8,128)(2,1)} %slice.68), channel_id=1, source_target_pairs={{0,8},{8,16},{16,24},{24,0},{1,9},{9,17},{17,25},{25,1},{2,10},{10... | collective-permute-start | bytes 2064392 | tf_op jit(solution)/shard_map/ppermute | solution.py:19
  214.6 25.5 %collective-permute-start.37 = (bf16[2,4,48,896]{3,2,1,0:T(8,128)(2,1)}, bf16[2,4,48,896]{3,2,1,0:T(8,128)(2,1)}, u32[]{:S(2)}, u32[]{:S(2)}) collective-permute-start(bf16[2,4,48,896]{3,2,1,0:T(8,128)(2,1)} %slice.69), channel_id=1, source_target_pairs={{0,24},{8,0},{16,8},{24,16},{1,25},{9,1},{17,9},{25,17},{2,26},{10... | collective-permute-start | bytes 2064392 | tf_op jit(solution)/shard_map/ppermute | solution.py:19
  217.6 22.4 %collective-permute-start.38 = (bf16[2,4,48,896]{3,2,1,0:T(8,128)(2,1)}, bf16[2,4,48,896]{3,2,1,0:T(8,128)(2,1)}, u32[]{:S(2)}, u32[]{:S(2)}) collective-permute-start(bf16[2,4,48,896]{3,2,1,0:T(8,128)(2,1)} %slice.70), channel_id=1, source_target_pairs={{0,32},{32,64},{64,96},{96,0},{1,33},{33,65},{65,97},{97,1},{2,34}... | collective-permute-start | bytes 2064392 | tf_op jit(solution)/shard_map/ppermute | solution.py:19
  218.5 21.5 %collective-permute-start.39 = (bf16[2,4,48,896]{3,2,1,0:T(8,128)(2,1)}, bf16[2,4,48,896]{3,2,1,0:T(8,128)(2,1)}, u32[]{:S(2)}, u32[]{:S(2)}) collective-permute-start(bf16[2,4,48,896]{3,2,1,0:T(8,128)(2,1)} %slice.71), channel_id=1, source_target_pairs={{0,96},{32,0},{64,32},{96,64},{1,97},{33,1},{65,33},{97,65},{2,98}... | collective-permute-start | bytes 2064392 | tf_op jit(solution)/shard_map/ppermute | solution.py:19
  (75 other events, 449.6 us)

commit v6 on v5

--- a/solution.py
+++ b/solution.py
@@ -129,7 +129,7 @@
 
 
 def up_second_kernel(
-    place_ref, before_ref, b_ref, a2_top, a2_low, w0, w1, w2, w3, sum_ref, out_ref, w_ref, sems
+    place_ref, before_ref, b_ref, a2_top, a2_low, w0, w1, w2, w3, sum_ref, out_ref, w_ref, a2_ref, sems
 ):
     step = pl.program_id(0)
     hidden = w0.shape[1]
@@ -147,27 +147,26 @@
         for copy in copies:
             copy.wait()
 
-    def total(a2):
-        @pl.loop(0, 4)
-        def _(j):
-            cols = pl.ds(pl.multiple_of(j * hidden, hidden), hidden)
-            part = dot(b_ref[...], w_ref[FIRST:, cols]) + dot(a2[...], w_ref[:FIRST, cols])
-            part = part + before_ref[:, cols]
-            sum_ref[:, cols] = part
-            out_ref[:, cols] = part.astype(BF)
-
     @pl.when(step == 0)
     def _():
-        total(a2_top)
+        a2_ref[...] = a2_top[...]
 
     @pl.when(step == 1)
     def _():
-        total(a2_low)
+        a2_ref[...] = a2_low[...]
+
+    @pl.loop(0, 4)
+    def _(j):
+        cols = pl.ds(pl.multiple_of(j * hidden, hidden), hidden)
+        part = dot(b_ref[...], w_ref[FIRST:, cols]) + dot(a2_ref[...], w_ref[:FIRST, cols])
+        part = part + before_ref[:, cols]
+        sum_ref[:, cols] = part
+        out_ref[:, cols] = part.astype(BF)
 
 
 def down_kernel(
     place_ref, sum_ref, got_ref, w0, w1, a0, a1_top, a1_low, a2_top, a2_low, a3_top, a3_low, b_ref,
-    w_ref, act_ref, sems
+    w_ref, act_ref, done_ref, sems
 ):
     step = pl.program_id(0)
     hidden = w0.shape[0]
@@ -198,7 +197,7 @@
 
     @pl.when(step == 0)
     def _():
-        for copy in copies():
+        for copy in copies()[0::2] + copies()[1::2]:
             copy.start()
 
     for j in range(2):
@@ -211,24 +210,32 @@
 
     @pl.when(step == 0)
     def _():
-        for copy in copies():
+        for copy in copies()[0::2]:
             copy.wait()
 
-    def out(start, size):
-        return dot(act_ref[...], w_ref[:, start : start + size]).astype(BF)
-
-    a0[...] = out(0, FIRST)
-    b_ref[...] = out(4 * FIRST, 4 * second)
+    @pl.loop(0, 4)
+    def _(k):
+        cols = pl.ds(pl.multiple_of(k * FIRST, FIRST), FIRST)
+        done_ref[k] = dot(act_ref[...], w_ref[:, cols]).astype(BF)
 
     @pl.when(step == 0)
     def _():
+        for copy in copies()[1::2]:
+            copy.wait()
+
+    b_ref[...] = dot(act_ref[...], w_ref[:, 4 * FIRST :]).astype(BF)
+
+    a0[...] = done_ref[0]
+
+    @pl.when(step == 0)
+    def _():
         for k, ref in ((1, a1_top), (2, a2_top), (3, a3_top)):
-            ref[...] = out(k * FIRST, FIRST)
+            ref[...] = done_ref[k]
 
     @pl.when(step == 1)
     def _():
         for k, ref in ((1, a1_low), (2, a2_low), (3, a3_low)):
-            ref[...] = out(k * FIRST, FIRST)
+            ref[...] = done_ref[k]
 
 
 def add_kernel(a1, got1, a3, got3, out1, out3):
@@ -316,13 +323,15 @@
         for copy in copies[4 * j : 4 * j + 4]:
             copy.wait()
 
-        @pl.loop(0, blocks // 8)
+        @pl.loop(0, blocks // 8 * (vocab // 256))
         def _(i, j=j, ref=ref):
-            at = pl.ds(pl.multiple_of(i * 8 * tokens, 8 * tokens), 8 * tokens)
-            rows = rows_ref[pl.ds(i * 8, 8)].reshape(8 * tokens, 4 * width)
-            ref[at, :vocab] = lax.dot_general(
+            group, part = i // (vocab // 256), i % (vocab // 256)
+            at = pl.ds(pl.multiple_of(group * 8 * tokens, 8 * tokens), 8 * tokens)
+            rows = rows_ref[pl.ds(group * 8, 8)].reshape(8 * tokens, 4 * width)
+            cols = pl.ds(pl.multiple_of(part * 256, 256), 256)
+            ref[at, cols] = lax.dot_general(
                 rows,
-                w_ref[j * vocab : (j + 1) * vocab, :],
+                w_ref[pl.ds(pl.multiple_of(j * vocab + part * 256, 256), 256), :],
                 (((1,), (1,)), ((), ())),
                 preferred_element_type=F32,
             )
@@ -490,6 +499,7 @@
             out_specs=[rows_of(4 * hid)] * 2,
             scratch_shapes=[
                 pltpu.VMEM((FIRST + 4 * second, 4 * hid), BF),
+                pltpu.VMEM((half, FIRST), BF),
                 pltpu.SemaphoreType.DMA((2, 4, 4)),
             ],
         ),
@@ -509,6 +519,7 @@
             scratch_shapes=[
                 pltpu.VMEM((2 * hid, 4 * width), BF),
                 pltpu.VMEM((half, 2 * hid), BF),
+                pltpu.VMEM((4, half, FIRST), BF),
                 pltpu.SemaphoreType.DMA((2, 8)),
             ],
         ),
@@ -558,7 +569,7 @@
     def node_at(back_x, back_z):
         return ((x - back_x) % 4) * 4 + (z - back_z) % 4
 
-    def scored(pieces):
+    def scored(pieces, mib):
         rows = sum(piece.shape[0] for piece in pieces) * part
         own, other = pl.pallas_call(
             head_kernel,
@@ -575,7 +586,7 @@
                 ],
             ),
             out_shape=(like(rows, vocab_rows + 128, dtype=F32),) * 2,
-            compiler_params=vmem(VMEM),
+            compiler_params=vmem(mib),
             cost_estimate=pl.CostEstimate(
                 flops=16 * rows * width * vocab_rows,
                 bytes_accessed=16 * width * vocab_rows,
@@ -599,7 +610,7 @@
 
     behind_a, ahead_a = shift(line_a, "z", 1), shift(line_a, "z", -1)
     behind_b, ahead_b = shift(line_b, "x", 1), shift(line_b, "x", -1)
-    scores = scored((line_a, line_b))
+    scores = scored((line_a, line_b), 60)
     nearby = (behind_a, ahead_a, behind_b, ahead_b)
     nearby, (own, other) = lax.optimization_barrier((nearby, scores))
     behind_a, ahead_a, behind_b, ahead_b = nearby
@@ -608,13 +619,13 @@
     order = [node_at(i, 0) for i in range(4)] + [node_at(0, i) for i in range(4)]
     stats = jnp.zeros((3 * n_node, 128), F32)
     stats = counted(own, shift(other, "core", 1), order, stats)
-    scores = scored((behind_a, ahead_a, behind_b, ahead_b))
+    scores = scored((behind_a, ahead_a, behind_b, ahead_b), 60)
     far = (far_a1, far_a2, far_b1, far_b2)
     far, (own, other), stats = lax.optimization_barrier((far, scores, stats))
     order = [node_at(i, k) for k in (1, 3) for i in range(4)]
     order = order + [node_at(k, i) for k in (1, 3) for i in range(4)]
     stats = counted(own, shift(other, "core", 1), order, stats)
-    own, other = scored(far)
+    own, other = scored(far, VMEM)
     order = [node_at(i, 2) for i in range(4)] + [node_at(2, i) for i in range(4)]
     stats = counted(own, shift(other, "core", 1), order, stats)
     for axis in ("core", "y", "z"):

time: 291 us -> 280 us (0.962); the launches traced: 286 us -> 279 us
  starting transfers between devices: 103 us -> 95.4 us
  Pallas kernels: 67.2 us -> 74.6 us
  local copies, waits for them, and re-layouts: 26.6 us -> 23.2 us
  waiting for transfers between devices: 86.6 us -> 83.3 us
    ppermute x53, starting transfers between devices: 75.7 us -> 67.3 us  [shift(): lax.ppermute(value, axis, [(i, (i + step) % size) for i in range(size)])]
    unnamed x84 -> x82, local copies, waits for them, and re-layouts: 20.4 us -> 13.6 us
    pallas_call x3, Pallas kernels: 24 us -> 30.7 us  [scored(): pl.pallas_call(head_kernel, grid_spec=pltpu.PrefetchScalarGridSpec(num_sc...]
    ppermute x53, waiting for transfers between devices: 76.9 us -> 73.9 us  [shift(): lax.ppermute(value, axis, [(i, (i + step) % size) for i in range(size)])]
  transfers between devices with their start and end apart: 57 -> 57, of which waited for: 31 -> 30; matrix products, arithmetic and copies ran while one was open for 2% -> 4% of each run, Pallas kernels for 21% -> 24%
where the time goes in v6:
time: 280 us; the launch traced here: 279 us
  starting transfers between devices  95.4 us (34%)
  waiting for transfers between devices  83.3 us (30%)
  Pallas kernels  74.6 us (27%)
  local copies, waits for them, and re-layouts  23.2 us (8%)
    ppermute x53, waiting for transfers between devices, shift(): lax.ppermute(value, axis, [(i, (i + step) % size) for i in range(size)])  73.9 us
    ppermute x53, starting transfers between devices, shift(): lax.ppermute(value, axis, [(i, (i + step) % size) for i in range(size)])  67.3 us
    pallas_call x3, Pallas kernels, scored(): pl.pallas_call(head_kernel, grid_spec=pltpu.PrefetchScalarGridSpec(num_sc...  30.7 us
    all_to_all x4, starting transfers between devices, over_nodes(): lax.all_to_all(cut, ('x', 'z'), split_axis=0, concat_axis=0, tiled=True)  28 us
    unnamed x82, local copies, waits for them, and re-layouts  13.6 us
    pallas_call x1, Pallas kernels, shards(): pl.pallas_call(down_kernel, grid_spec=pltpu.PrefetchScalarGridSpec(num_sc...  10.2 us
    pallas_call x1, Pallas kernels, shards(): pl.pallas_call(up_second_kernel, grid_spec=pltpu.PrefetchScalarGridSpec(n...  9.84 us
    all_to_all x4, waiting for transfers between devices, over_nodes(): lax.all_to_all(cut, ('x', 'z'), split_axis=0, concat_axis=0, tiled=True)  9.45 us
  transfers between devices with their start and end apart: 57, of which 30 were waited for; matrix products, arithmetic and copies ran while one was open for 4% of the time, Pallas kernels for 24%

profile of v6, /device:TPU:0, one launch (start us, length us, event | category | flops | bytes accessed | tf_op | source)
XLA Modules:
  0.0 278.6 jit_solution(3219570192363353543)
XLA Ops:
  6.4 8.0 %all-to-all-start = ((bf16[16,40,512]{2,1,0:T(8,128)(2,1)}), bf16[16,40,512]{2,1,0:T(8,128)(2,1)S(1)}, u32[]{:S(2)}, u32[]{:S(2)}) async-start(bf16[16,40,512]{2,1,0:T(8,128)(2,1)} %bitcast.4), calls=%async_computation | async-start | bytes 1310720 | tf_op jit(solution)/shard_map/all_to_all | solution.py:427
  27.8 7.1 %all-to-all-start.1 = ((bf16[16,40,1536]{2,1,0:T(8,128)(2,1)}), bf16[16,40,1536]{2,1,0:T(8,128)(2,1)S(1)}, u32[]{:S(2)}, u32[]{:S(2)}) async-start(bf16[16,40,1536]{2,1,0:T(8,128)(2,1)} %bitcast.69), calls=%async_computation.1 | async-start | bytes 3932160 | tf_op jit(solution)/shard_map/all_to_all | solution.py:427
  38.5 12.8 %collective-permute-done.3.a1 = bf16[640,512]{1,0:T(8,128)(2,1)S(1)} collective-permute-done((bf16[640,512]{1,0:T(8,128)(2,1)S(1)}, bf16[640,512]{1,0:T(8,128)(2,1)S(1)}, u32[]{:S(2)}, u32[]{:S(2)}) %collective-permute-start.3) | collective-permute-done | bytes 655392 | tf_op jit(solution)/shard_map/ppermute | solution.py:19
  58.1 6.1 %up_first.1.before_ref = f32[640,1024]{1,0:T(8,128)S(1)} custom-call(s32[2]{0:T(128)S(1)} %pad_add_fusion.place_ref, bf16[640,512]{1,0:T(8,128)(2,1)S(1)} %bitcast.67, bf16[640,512]{1,0:T(8,128)(2,1)S(1)} %collective-permute-done.3.a1, bf16[640,512]{1,0:T(8,128)(2,1)S(1)} %copy-done.6, bf16[7168,256]{1,0:T(8,128)(2,1)} %bitcast.73, ...), custom_call_target="tpu_custom_call" | custom-call | flops 2013265920 | bytes 3145728 | tf_op jit(solution)/shard_map/up_first/pallas_call | solution.py:477
  65.8 9.8 %up_second.1 = (f32[640,1024]{1,0:T(8,128)}, bf16[640,1024]{1,0:T(8,128)(2,1)S(1)}) custom-call(s32[2]{0:T(128)S(1)} %pad_add_fusion.place_ref, f32[640,1024]{1,0:T(8,128)} %copy-done, bf16[640,1536]{1,0:T(8,128)(2,1)S(1)} %bitcast.64, bf16[320,512]{1,0:T(8,128)(2,1)} %collective-permute-done.7.a2_top, bf16[320,512]{1,0:T(8,128)(2,1)} %collective-permute-done.8.a2_low, ...), custom_call_target="tpu_custom_call" | custom-call | tf_op jit(solution)/shard_map/up_second/pallas_call | solution.py:493
  79.8 10.2 %down.1 = (bf16[640,512]{1,0:T(8,128)(2,1)}, bf16[320,512]{1,0:T(8,128)(2,1)}, bf16[320,512]{1,0:T(8,128)(2,1)}, bf16[320,512]{1,0:T(8,128)(2,1)}, bf16[320,512]...) custom-call(s32[2]{0:T(128)} %copy-done.20, ...), custom_call_target="tpu_custom_call" | custom-call | tf_op jit(solution)/shard_map/down/pallas_call | solution.py:512
  90.0 7.0 %all-to-all-start.3 = ((bf16[16,40,1536]{2,1,0:T(8,128)(2,1)}), bf16[16,40,1536]{2,1,0:T(8,128)(2,1)S(1)}, u32[]{:S(2)}, u32[]{:S(2)}) async-start(bf16[16,40,1536]{2,1,0:T(8,128)(2,1)} %bitcast.80), calls=%async_computation.3 | async-start | bytes 3932160 | tf_op jit(solution)/shard_map/all_to_all | solution.py:427
  99.6 3.2 %collective-permute-start.14 = (bf16[320,512]{1,0:T(8,128)(2,1)}, bf16[320,512]{1,0:T(8,128)(2,1)S(1)}, u32[]{:S(2)}, u32[]{:S(2)}) collective-permute-start(bf16[320,512]{1,0:T(8,128)(2,1)} %get-tuple-element.65), channel_id=1, source_target_pairs={{0,6},{2,0},{4,2},{6,4},{1,7},{3,1},{5,3},{7,5},{8,14},{10,8},{12,... | collective-permute-start | bytes 983048 | tf_op jit(solution)/shard_map/ppermute | solution.py:19
  102.9 5.2 %collective-permute-done.11.got1 = bf16[320,512]{1,0:T(8,128)(2,1)S(1)} collective-permute-done((bf16[320,512]{1,0:T(8,128)(2,1)}, bf16[320,512]{1,0:T(8,128)(2,1)S(1)}, u32[]{:S(2)}, u32[]{:S(2)}) %collective-permute-start.11) | collective-permute-done | bytes 327712 | tf_op jit(solution)/shard_map/ppermute | solution.py:19
  108.1 3.6 %collective-permute-done.12.got3 = bf16[320,512]{1,0:T(8,128)(2,1)S(1)} collective-permute-done((bf16[320,512]{1,0:T(8,128)(2,1)}, bf16[320,512]{1,0:T(8,128)(2,1)S(1)}, u32[]{:S(2)}, u32[]{:S(2)}) %collective-permute-start.12) | collective-permute-done | bytes 327712 | tf_op jit(solution)/shard_map/ppermute | solution.py:19
  115.1 3.6 %collective-permute-done.15.right_top = bf16[320,512]{1,0:T(8,128)(2,1)S(1)} collective-permute-done((bf16[320,512]{1,0:T(8,128)(2,1)}, bf16[320,512]{1,0:T(8,128)(2,1)S(1)}, u32[]{:S(2)}, u32[]{:S(2)}) %collective-permute-start.15) | collective-permute-done | bytes 327712 | tf_op jit(solution)/shard_map/ppermute | solution.py:19
  120.9 3.4 %collective-permute-done.16.right_low = bf16[320,512]{1,0:T(8,128)(2,1)S(1)} collective-permute-done((bf16[320,512]{1,0:T(8,128)(2,1)S(1)}, bf16[320,512]{1,0:T(8,128)(2,1)S(1)}, u32[]{:S(2)}, u32[]{:S(2)}) %collective-permute-start.16) | collective-permute-done | bytes 327712 | tf_op jit(solution)/shard_map/ppermute | solution.py:19
  126.4 5.9 %all-to-all-start.2 = ((bf16[16,40,512]{2,1,0:T(8,128)(2,1)}), bf16[16,40,512]{2,1,0:T(8,128)(2,1)S(1)}, u32[]{:S(2)}, u32[]{:S(2)}) async-start(bf16[16,40,512]{2,1,0:T(8,128)(2,1)} %bitcast.11), calls=%async_computation.2 | async-start | bytes 1310720 | tf_op jit(solution)/shard_map/all_to_all | solution.py:427
  135.3 8.4 %all-to-all-done.2 = bf16[16,40,512]{2,1,0:T(8,128)(2,1)S(1)} async-done(((bf16[16,40,512]{2,1,0:T(8,128)(2,1)}), bf16[16,40,512]{2,1,0:T(8,128)(2,1)S(1)}, u32[]{:S(2)}, u32[]{:S(2)}) %all-to-all-start.2) | async-done | bytes 655392 | tf_op jit(solution)/shard_map/all_to_all | solution.py:427
  148.1 5.2 %collective-permute-done.21 = bf16[96,896]{1,0:T(8,128)(2,1)S(1)} collective-permute-done((bf16[96,896]{1,0:T(8,128)(2,1)S(1)}, bf16[96,896]{1,0:T(8,128)(2,1)S(1)}, u32[]{:S(2)}, u32[]{:S(2)}) %collective-permute-start.21) | collective-permute-done | bytes 172064 | tf_op jit(solution)/shard_map/ppermute | solution.py:19
  161.0 3.3 %collective-permute-done.30 = bf16[4,48,896]{2,1,0:T(8,128)(2,1)S(1)} collective-permute-done((bf16[4,48,896]{2,1,0:T(8,128)(2,1)S(1)}, bf16[4,48,896]{2,1,0:T(8,128)(2,1)S(1)}, u32[]{:S(2)}, u32[]{:S(2)}) %collective-permute-start.30) | collective-permute-done | bytes 344096 | tf_op jit(solution)/shard_map/ppermute | solution.py:19
  164.4 3.4 %collective-permute-start.33 = (bf16[2,48,896]{2,1,0:T(8,128)(2,1)S(1)}, bf16[2,48,896]{2,1,0:T(8,128)(2,1)S(1)}, u32[]{:S(2)}, u32[]{:S(2)}) collective-permute-start(bf16[2,48,896]{2,1,0:T(8,128)(2,1)S(1)} %slice.83), channel_id=1, source_target_pairs={{0,24},{8,0},{16,8},{24,16},{1,25},{9,1},{17,9},{25,17},{2,26},{10... | collective-permute-start | bytes 516104 | tf_op jit(solution)/shard_map/ppermute | solution.py:19
  168.1 3.3 %collective-permute-start.27 = (bf16[2,48,896]{2,1,0:T(8,128)(2,1)S(1)}, bf16[2,48,896]{2,1,0:T(8,128)(2,1)S(1)}, u32[]{:S(2)}, u32[]{:S(2)}) collective-permute-start(bf16[2,48,896]{2,1,0:T(8,128)(2,1)S(1)} %slice.78), channel_id=1, source_target_pairs={{0,96},{32,0},{64,32},{96,64},{1,97},{33,1},{65,33},{97,65},{2,98}... | collective-permute-start | bytes 516104 | tf_op jit(solution)/shard_map/ppermute | solution.py:19
  180.1 9.0 %head.3 = (f32[384,640]{1,0:T(8,128)}, f32[384,640]{1,0:T(8,128)}) custom-call(s32[2]{0:T(128)} %copy-done.20, f32[4,896]{1,0:T(4,128)} %copy-done.18, bf16[512,7168]{1,0:T(8,128)(2,1)} %w0.5, bf16[512,7168]{1,0:T(8,128)(2,1)} %collective-permute-done.20.w1, bf16[4,4,48,896]{3,2,1,0:T(8,128)(2,1)} %copy-done.25, bf16[4,4,48,896]{3,2,1,0:T(8,128)(2,1)} %copy-done.24), custom_call_target="tpu_custom_call" | custom-call | flops 2818572288 | bytes 7340032 | tf_op jit(solution)/shard_map/head/pallas_call | solution.py:574
  189.1 11.1 %collective-permute-done.34.refs_2_ = bf16[4,4,48,896]{3,2,1,0:T(8,128)(2,1)S(1)} collective-permute-done((bf16[4,4,48,896]{3,2,1,0:T(8,128)(2,1)S(1)}, bf16[4,4,48,896]{3,2,1,0:T(8,128)(2,1)S(1)}, u32[]{:S(2)}, u32[]{:S(2)}) %collective-permute-start.34) | collective-permute-done | bytes 1376288 | tf_op jit(solution)/shard_map/ppermute | solution.py:19
  216.3 14.3 %head.4 = (f32[768,640]{1,0:T(8,128)}, f32[768,640]{1,0:T(8,128)}) custom-call(s32[2]{0:T(128)} %copy-done.20, f32[4,896]{1,0:T(4,128)} %copy-done.18, bf16[512,7168]{1,0:T(8,128)(2,1)} %w0.5, bf16[512,7168]{1,0:T(8,128)(2,1)} %collective-permute-done.20.w1, bf16[4,4,48,896]{3,2,1,0:T(8,128)(2,1)} %collective-permute-done.28.refs_0_, ...), custom_call_target="tpu_custom_call" | custom-call | flops 5637144576 | bytes 7340032 | tf_op jit(solution)/shard_map/head/pallas_call | solution.py:574
  232.0 7.4 %head.5 = (f32[384,640]{1,0:T(8,128)S(1)}, f32[384,640]{1,0:T(8,128)}) custom-call(s32[2]{0:T(128)S(1)} %copy-done.21, f32[4,896]{1,0:T(4,128)S(1)} %copy-done.19, bf16[512,7168]{1,0:T(8,128)(2,1)} %w0.5, bf16[512,7168]{1,0:T(8,128)(2,1)} %collective-permute-done.20.w1, bf16[2,4,48,896]{3,2,1,0:T(8,128)(2,1)S(1)} %collective-permute-done.36.refs_0_, ...), custom_call_target="tpu_custom_call" | custom-call | flops 2818572288 | bytes 7340032 | tf_op jit(solution)/shard_map/head/pallas_call | solution.py:574
  250.0 3.5 %collective-permute-start.45 = (f32[48,128]{1,0:T(8,128)}, f32[48,128]{1,0:T(8,128)S(1)}, u32[]{:S(2)}, u32[]{:S(2)}) collective-permute-start(f32[48,128]{1,0:T(8,128)} %merge.3.refs_0_), channel_id=1, source_target_pairs={{0,4},{2,6},{4,0},{6,2},{1,5},{3,7},{5,1},{7,3},{8,12},{10,14},{12... | collective-permute-start | bytes 73736 | tf_op jit(solution)/shard_map/ppermute | solution.py:19
  269.1 3.3 %collective-permute-start.51 = (f32[48,128]{1,0:T(8,128)}, f32[48,128]{1,0:T(8,128)S(1)}, u32[]{:S(2)}, u32[]{:S(2)}) collective-permute-start(f32[48,128]{1,0:T(8,128)} %merge.5.refs_0_), channel_id=1, source_target_pairs={{0,64},{32,96},{64,0},{96,32},{1,65},{33,97},{65,1},{97,33},{2,66}... | collective-permute-start | bytes 73736 | tf_op jit(solution)/shard_map/ppermute | solution.py:19
  (219 shorter events, 119.0 us)
Async XLA Ops:
  0.6 53.4 %collective-permute-start.5 = (bf16[7168,256]{1,0:T(8,128)(2,1)}, bf16[7168,256]{1,0:T(8,128)(2,1)}, u32[]{:S(2)}, u32[]{:S(2)}) collective-permute-start(bf16[7168,256]{1,0:T(8,128)(2,1)} %bitcast.72), channel_id=1, source_target_pairs={{0,1},{1,0},{2,3},{3,2},{4,5},{5,4},{6,7},{7,6},{8,9},{9,8},{10,11... | collective-permute-start | bytes 11010056 | tf_op jit(solution)/shard_map/ppermute | solution.py:19
  0.7 56.2 %collective-permute-start.6 = (bf16[7168,256]{1,0:T(8,128)(2,1)}, bf16[7168,256]{1,0:T(8,128)(2,1)}, u32[]{:S(2)}, u32[]{:S(2)}) collective-permute-start(bf16[7168,256]{1,0:T(8,128)(2,1)} %bitcast.75), channel_id=1, source_target_pairs={{0,1},{1,0},{2,3},{3,2},{4,5},{5,4},{6,7},{7,6},{8,9},{9,8},{10,11... | collective-permute-start | bytes 11010056 | tf_op jit(solution)/shard_map/ppermute | solution.py:19
  6.4 21.4 %all-to-all-start = ((bf16[16,40,512]{2,1,0:T(8,128)(2,1)}), bf16[16,40,512]{2,1,0:T(8,128)(2,1)S(1)}, u32[]{:S(2)}, u32[]{:S(2)}) async-start(bf16[16,40,512]{2,1,0:T(8,128)(2,1)} %bitcast.4), calls=%async_computation | async-start | bytes 1310720 | tf_op jit(solution)/shard_map/all_to_all | solution.py:427
  14.4 61.3 %collective-permute-start.10 = (bf16[256,7168]{1,0:T(8,128)(2,1)}, bf16[256,7168]{1,0:T(8,128)(2,1)}, u32[]{:S(2)}, u32[]{:S(2)}) collective-permute-start(bf16[256,7168]{1,0:T(8,128)(2,1)} %bitcast.78), channel_id=1, source_target_pairs={{0,1},{1,0},{2,3},{3,2},{4,5},{5,4},{6,7},{7,6},{8,9},{9,8},{10,11... | collective-permute-start | bytes 11010056 | tf_op jit(solution)/shard_map/ppermute | solution.py:19
  27.8 37.9 %all-to-all-start.1 = ((bf16[16,40,1536]{2,1,0:T(8,128)(2,1)}), bf16[16,40,1536]{2,1,0:T(8,128)(2,1)S(1)}, u32[]{:S(2)}, u32[]{:S(2)}) async-start(bf16[16,40,1536]{2,1,0:T(8,128)(2,1)} %bitcast.69), calls=%async_computation.1 | async-start | bytes 3932160 | tf_op jit(solution)/shard_map/all_to_all | solution.py:427
  35.0 16.3 %collective-permute-start.3 = (bf16[640,512]{1,0:T(8,128)(2,1)S(1)}, bf16[640,512]{1,0:T(8,128)(2,1)S(1)}, u32[]{:S(2)}, u32[]{:S(2)}) collective-permute-start(bf16[640,512]{1,0:T(8,128)(2,1)S(1)} %bitcast.65), channel_id=1, source_target_pairs={{0,2},{2,4},{4,6},{6,0},{1,3},{3,5},{5,7},{7,1},{8,10},{10,12},{12... | collective-permute-start | bytes 1966088 | tf_op jit(solution)/shard_map/ppermute | solution.py:19
  35.5 16.6 %collective-permute-start.4 = (bf16[640,512]{1,0:T(8,128)(2,1)S(1)}, bf16[640,512]{1,0:T(8,128)(2,1)S(1)}, u32[]{:S(2)}, u32[]{:S(2)}) collective-permute-start(bf16[640,512]{1,0:T(8,128)(2,1)S(1)} %bitcast.66), channel_id=1, source_target_pairs={{0,6},{2,0},{4,2},{6,4},{1,7},{3,1},{5,3},{7,5},{8,14},{10,8},{12,... | collective-permute-start | bytes 1966088 | tf_op jit(solution)/shard_map/ppermute | solution.py:19
  51.3 128.8 %collective-permute-start.20 = (bf16[512,7168]{1,0:T(8,128)(2,1)}, bf16[512,7168]{1,0:T(8,128)(2,1)}, u32[]{:S(2)}, u32[]{:S(2)}) collective-permute-start(bf16[512,7168]{1,0:T(8,128)(2,1)} %w0.5), channel_id=1, source_target_pairs={{0,1},{1,0},{2,3},{3,2},{4,5},{5,4},{6,7},{7,6},{8,9},{9,8},{10,11... | collective-permute-start | bytes 22020104 | tf_op jit(solution)/shard_map/ppermute | solution.py:19
  52.1 13.6 %collective-permute-start.7 = (bf16[320,512]{1,0:T(8,128)(2,1)}, bf16[320,512]{1,0:T(8,128)(2,1)}, u32[]{:S(2)}, u32[]{:S(2)}) collective-permute-start(bf16[320,512]{1,0:T(8,128)(2,1)} %slice.72), channel_id=1, source_target_pairs={{0,2},{2,4},{4,6},{6,0},{1,3},{3,5},{5,7},{7,1},{8,10},{10,12},{12... | collective-permute-start | bytes 983048 | tf_op jit(solution)/shard_map/ppermute | solution.py:19
  90.0 36.4 %all-to-all-start.3 = ((bf16[16,40,1536]{2,1,0:T(8,128)(2,1)}), bf16[16,40,1536]{2,1,0:T(8,128)(2,1)S(1)}, u32[]{:S(2)}, u32[]{:S(2)}) async-start(bf16[16,40,1536]{2,1,0:T(8,128)(2,1)} %bitcast.80), calls=%async_computation.3 | async-start | bytes 3932160 | tf_op jit(solution)/shard_map/all_to_all | solution.py:427
  99.6 12.1 %collective-permute-start.12 = (bf16[320,512]{1,0:T(8,128)(2,1)}, bf16[320,512]{1,0:T(8,128)(2,1)S(1)}, u32[]{:S(2)}, u32[]{:S(2)}) collective-permute-start(bf16[320,512]{1,0:T(8,128)(2,1)} %get-tuple-element.63), channel_id=1, source_target_pairs={{0,2},{2,4},{4,6},{6,0},{1,3},{3,5},{5,7},{7,1},{8,10},{10,12},{12... | collective-permute-start | bytes 983048 | tf_op jit(solution)/shard_map/ppermute | solution.py:19
  99.6 15.5 %collective-permute-start.14 = (bf16[320,512]{1,0:T(8,128)(2,1)}, bf16[320,512]{1,0:T(8,128)(2,1)S(1)}, u32[]{:S(2)}, u32[]{:S(2)}) collective-permute-start(bf16[320,512]{1,0:T(8,128)(2,1)} %get-tuple-element.65), channel_id=1, source_target_pairs={{0,6},{2,0},{4,2},{6,4},{1,7},{3,1},{5,3},{7,5},{8,14},{10,8},{12,... | collective-permute-start | bytes 983048 | tf_op jit(solution)/shard_map/ppermute | solution.py:19
  102.9 15.8 %collective-permute-start.15 = (bf16[320,512]{1,0:T(8,128)(2,1)}, bf16[320,512]{1,0:T(8,128)(2,1)S(1)}, u32[]{:S(2)}, u32[]{:S(2)}) collective-permute-start(bf16[320,512]{1,0:T(8,128)(2,1)} %get-tuple-element.66), channel_id=1, source_target_pairs={{0,2},{2,4},{4,6},{6,0},{1,3},{3,5},{5,7},{7,1},{8,10},{10,12},{12... | collective-permute-start | bytes 983048 | tf_op jit(solution)/shard_map/ppermute | solution.py:19
  111.9 12.4 %collective-permute-start.16 = (bf16[320,512]{1,0:T(8,128)(2,1)S(1)}, bf16[320,512]{1,0:T(8,128)(2,1)S(1)}, u32[]{:S(2)}, u32[]{:S(2)}) collective-permute-start(bf16[320,512]{1,0:T(8,128)(2,1)S(1)} %get-tuple-element.67), channel_id=1, source_target_pairs={{0,2},{2,4},{4,6},{6,0},{1,3},{3,5},{5,7},{7,1},{8,10},{10,12},{12... | collective-permute-start | bytes 983048 | tf_op jit(solution)/shard_map/ppermute | solution.py:19
  126.4 17.3 %all-to-all-start.2 = ((bf16[16,40,512]{2,1,0:T(8,128)(2,1)}), bf16[16,40,512]{2,1,0:T(8,128)(2,1)S(1)}, u32[]{:S(2)}, u32[]{:S(2)}) async-start(bf16[16,40,512]{2,1,0:T(8,128)(2,1)} %bitcast.11), calls=%async_computation.2 | async-start | bytes 1310720 | tf_op jit(solution)/shard_map/all_to_all | solution.py:427
  171.6 28.6 %collective-permute-start.34 = (bf16[4,4,48,896]{3,2,1,0:T(8,128)(2,1)S(1)}, bf16[4,4,48,896]{3,2,1,0:T(8,128)(2,1)S(1)}, u32[]{:S(2)}, u32[]{:S(2)}) collective-permute-start(bf16[4,4,48,896]{3,2,1,0:T(8,128)(2,1)S(1)} %pad_maximum_fusion.1.refs_1_), channel_id=1, source_target_pairs={{0,32},{32,64},{64,96},{96,0},{1,33},{33,65},{65,97},{97,1},{2,34}... | collective-permute-start | bytes 4128776 | tf_op jit(solution)/shard_map/ppermute | solution.py:19
  171.7 28.5 %collective-permute-start.35 = (bf16[4,4,48,896]{3,2,1,0:T(8,128)(2,1)S(1)}, bf16[4,4,48,896]{3,2,1,0:T(8,128)(2,1)}, u32[]{:S(2)}, u32[]{:S(2)}) collective-permute-start(bf16[4,4,48,896]{3,2,1,0:T(8,128)(2,1)S(1)} %pad_maximum_fusion.1.refs_1_), channel_id=1, source_target_pairs={{0,96},{32,0},{64,32},{96,64},{1,97},{33,1},{65,33},{97,65},{2,98}... | collective-permute-start | bytes 4128776 | tf_op jit(solution)/shard_map/ppermute | solution.py:19
  176.8 25.0 %collective-permute-start.28 = (bf16[4,4,48,896]{3,2,1,0:T(8,128)(2,1)S(1)}, bf16[4,4,48,896]{3,2,1,0:T(8,128)(2,1)}, u32[]{:S(2)}, u32[]{:S(2)}) collective-permute-start(bf16[4,4,48,896]{3,2,1,0:T(8,128)(2,1)S(1)} %pad_maximum_fusion.refs_0_), channel_id=1, source_target_pairs={{0,8},{8,16},{16,24},{24,0},{1,9},{9,17},{17,25},{25,1},{2,10},{10... | collective-permute-start | bytes 4128776 | tf_op jit(solution)/shard_map/ppermute | solution.py:19
  176.9 24.9 %collective-permute-start.29 = (bf16[4,4,48,896]{3,2,1,0:T(8,128)(2,1)S(1)}, bf16[4,4,48,896]{3,2,1,0:T(8,128)(2,1)}, u32[]{:S(2)}, u32[]{:S(2)}) collective-permute-start(bf16[4,4,48,896]{3,2,1,0:T(8,128)(2,1)S(1)} %pad_maximum_fusion.refs_0_), channel_id=1, source_target_pairs={{0,24},{8,0},{16,8},{24,16},{1,25},{9,1},{17,9},{25,17},{2,26},{10... | collective-permute-start | bytes 4128776 | tf_op jit(solution)/shard_map/ppermute | solution.py:19
  201.8 28.8 %collective-permute-start.40 = (f32[384,640]{1,0:T(8,128)}, f32[384,640]{1,0:T(8,128)S(1)}, u32[]{:S(2)}, u32[]{:S(2)}) collective-permute-start(f32[384,640]{1,0:T(8,128)} %get-tuple-element.85), channel_id=1, source_target_pairs={{0,1},{1,0},{2,3},{3,2},{4,5},{5,4},{6,7},{7,6},{8,9},{9,8},{10,11... | collective-permute-start | bytes 2949128 | tf_op jit(solution)/shard_map/ppermute | solution.py:19
  204.1 27.8 %collective-permute-start.36 = (bf16[2,4,48,896]{3,2,1,0:T(8,128)(2,1)}, bf16[2,4,48,896]{3,2,1,0:T(8,128)(2,1)S(1)}, u32[]{:S(2)}, u32[]{:S(2)}) collective-permute-start(bf16[2,4,48,896]{3,2,1,0:T(8,128)(2,1)} %slice.68), channel_id=1, source_target_pairs={{0,8},{8,16},{16,24},{24,0},{1,9},{9,17},{17,25},{25,1},{2,10},{10... | collective-permute-start | bytes 2064392 | tf_op jit(solution)/shard_map/ppermute | solution.py:19
  207.1 24.7 %collective-permute-start.37 = (bf16[2,4,48,896]{3,2,1,0:T(8,128)(2,1)}, bf16[2,4,48,896]{3,2,1,0:T(8,128)(2,1)}, u32[]{:S(2)}, u32[]{:S(2)}) collective-permute-start(bf16[2,4,48,896]{3,2,1,0:T(8,128)(2,1)} %slice.69), channel_id=1, source_target_pairs={{0,24},{8,0},{16,8},{24,16},{1,25},{9,1},{17,9},{25,17},{2,26},{10... | collective-permute-start | bytes 2064392 | tf_op jit(solution)/shard_map/ppermute | solution.py:19
  210.2 21.6 %collective-permute-start.38 = (bf16[2,4,48,896]{3,2,1,0:T(8,128)(2,1)}, bf16[2,4,48,896]{3,2,1,0:T(8,128)(2,1)}, u32[]{:S(2)}, u32[]{:S(2)}) collective-permute-start(bf16[2,4,48,896]{3,2,1,0:T(8,128)(2,1)} %slice.70), channel_id=1, source_target_pairs={{0,32},{32,64},{64,96},{96,0},{1,33},{33,65},{65,97},{97,1},{2,34}... | collective-permute-start | bytes 2064392 | tf_op jit(solution)/shard_map/ppermute | solution.py:19
  212.3 19.6 %collective-permute-start.39 = (bf16[2,4,48,896]{3,2,1,0:T(8,128)(2,1)}, bf16[2,4,48,896]{3,2,1,0:T(8,128)(2,1)}, u32[]{:S(2)}, u32[]{:S(2)}) collective-permute-start(bf16[2,4,48,896]{3,2,1,0:T(8,128)(2,1)} %slice.71), channel_id=1, source_target_pairs={{0,96},{32,0},{64,32},{96,64},{1,97},{33,1},{65,33},{97,65},{2,98}... | collective-permute-start | bytes 2064392 | tf_op jit(solution)/shard_map/ppermute | solution.py:19
  (74 other events, 439.7 us)

commit v7 on v6

--- a/solution.py
+++ b/solution.py
@@ -559,8 +559,9 @@
     part_b = jnp.stack([rows[part:] for rows in by_y])
     behind_a, far_a1, far_a2, ahead_a = ring(part_a, "x")
     behind_b, far_b1, far_b2, ahead_b = ring(part_b, "z")
-    line_a = jnp.stack([part_a, behind_a, jnp.concatenate([far_a1, far_a2]), ahead_a])
-    line_b = jnp.stack([part_b, behind_b, jnp.concatenate([far_b1, far_b2]), ahead_b])
+    lines_a = (jnp.stack([part_a, behind_a]), jnp.stack([jnp.concatenate([far_a1, far_a2]), ahead_a]))
+    lines_b = (jnp.stack([part_b, behind_b]), jnp.stack([jnp.concatenate([far_b1, far_b2]), ahead_b]))
+
     vocab_rows = head.shape[0]
     first_id = (lax.axis_index(AXES) * vocab_rows).reshape(1).astype(jnp.int32)
     x, z = lax.axis_index("x"), lax.axis_index("z")
@@ -608,18 +609,20 @@
             name="stats",
         )(first_id, jnp.stack(order).astype(jnp.int32), own, got, wanted, stats)
 
-    behind_a, ahead_a = shift(line_a, "z", 1), shift(line_a, "z", -1)
-    behind_b, ahead_b = shift(line_b, "x", 1), shift(line_b, "x", -1)
-    scores = scored((line_a, line_b), 60)
-    nearby = (behind_a, ahead_a, behind_b, ahead_b)
-    nearby, (own, other) = lax.optimization_barrier((nearby, scores))
-    behind_a, ahead_a, behind_b, ahead_b = nearby
-    far_a1, far_a2 = shift(behind_a[:2], "z", 1), shift(ahead_a[2:], "z", -1)
-    far_b1, far_b2 = shift(behind_b[:2], "x", 1), shift(ahead_b[2:], "x", -1)
+    onward_a = (shift(lines_a[0], "z", 1), shift(lines_a[1], "z", -1))
+    onward_b = (shift(lines_b[0], "x", 1), shift(lines_b[1], "x", -1))
+    rest_a = (shift(lines_a[1], "z", 1), shift(lines_a[0], "z", -1))
+    rest_b = (shift(lines_b[1], "x", 1), shift(lines_b[0], "x", -1))
+    scores = scored(lines_a + lines_b, 60)
+    (onward_a, onward_b), (own, other) = lax.optimization_barrier(((onward_a, onward_b), scores))
+    far_a1, far_a2 = shift(onward_a[0], "z", 1), shift(onward_a[1], "z", -1)
+    far_b1, far_b2 = shift(onward_b[0], "x", 1), shift(onward_b[1], "x", -1)
     order = [node_at(i, 0) for i in range(4)] + [node_at(0, i) for i in range(4)]
     stats = jnp.zeros((3 * n_node, 128), F32)
     stats = counted(own, shift(other, "core", 1), order, stats)
-    scores = scored((behind_a, ahead_a, behind_b, ahead_b), 60)
+    scores = scored(
+        (onward_a[0], rest_a[0], rest_a[1], onward_a[1], onward_b[0], rest_b[0], rest_b[1], onward_b[1]), 60
+    )
     far = (far_a1, far_a2, far_b1, far_b2)
     far, (own, other), stats = lax.optimization_barrier((far, scores, stats))
     order = [node_at(i, k) for k in (1, 3) for i in range(4)]

time: 280 us -> 276 us (0.986)
  starting transfers between devices: 95.4 us -> 90.4 us
  waiting for transfers between devices: 83.3 us -> 86.4 us
    slice x4 -> x0, local copies, waits for them, and re-layouts: 7.15 us -> none  [the longest x2 4.15 us: shards(): far_a1, far_a2 = (shift(behind_a[:2], 'z', 1), shift(ahead_a[2:], 'z', -1))]
    ppermute x53 -> x57, starting transfers between devices: 67.3 us -> 62.5 us  [shift(): lax.ppermute(value, axis, [(i, (i + step) % size) for i in range(size)])]
    unnamed x82 -> x88, local copies, waits for them, and re-layouts: 13.6 us -> 17.3 us
    ppermute x53 -> x57, waiting for transfers between devices: 73.9 us -> 76.8 us  [shift(): lax.ppermute(value, axis, [(i, (i + step) % size) for i in range(size)])]
  transfers between devices with their start and end apart: 57 -> 61, of which waited for: 30 -> 30; matrix products, arithmetic and copies ran while one was open for 4% -> 2% of each run, Pallas kernels for 24% -> 24%
where the time goes in v7:
time: 276 us; the launch traced here: 275 us
  starting transfers between devices  90.4 us (33%)
  waiting for transfers between devices  86.4 us (31%)
  Pallas kernels  75.2 us (27%)
  local copies, waits for them, and re-layouts  20.5 us (7%)
    ppermute x57, waiting for transfers between devices, shift(): lax.ppermute(value, axis, [(i, (i + step) % size) for i in range(size)])  76.8 us
    ppermute x57, starting transfers between devices, shift(): lax.ppermute(value, axis, [(i, (i + step) % size) for i in range(size)])  62.5 us
    pallas_call x3, Pallas kernels, scored(): pl.pallas_call(head_kernel, grid_spec=pltpu.PrefetchScalarGridSpec(num_sc...  31.3 us
    all_to_all x4, starting transfers between devices, over_nodes(): lax.all_to_all(cut, ('x', 'z'), split_axis=0, concat_axis=0, tiled=True)  27.9 us
    unnamed x88, local copies, waits for them, and re-layouts  17.3 us
    pallas_call x1, Pallas kernels, shards(): pl.pallas_call(down_kernel, grid_spec=pltpu.PrefetchScalarGridSpec(num_sc...  10.2 us
    pallas_call x1, Pallas kernels, shards(): pl.pallas_call(up_second_kernel, grid_spec=pltpu.PrefetchScalarGridSpec(n...  9.85 us
    all_to_all x4, waiting for transfers between devices, over_nodes(): lax.all_to_all(cut, ('x', 'z'), split_axis=0, concat_axis=0, tiled=True)  9.58 us
  transfers between devices with their start and end apart: 61, of which 30 were waited for; matrix products, arithmetic and copies ran while one was open for 2% of the time, Pallas kernels for 24%

profile of v7, /device:TPU:0, one launch (start us, length us, event | category | flops | bytes accessed | tf_op | source)
XLA Modules:
  0.0 275.2 jit_solution(12682739014844450715)
XLA Ops:
  5.7 8.0 %all-to-all-start = ((bf16[16,40,512]{2,1,0:T(8,128)(2,1)}), bf16[16,40,512]{2,1,0:T(8,128)(2,1)S(1)}, u32[]{:S(2)}, u32[]{:S(2)}) async-start(bf16[16,40,512]{2,1,0:T(8,128)(2,1)} %bitcast.4), calls=%async_computation | async-start | bytes 1310720 | tf_op jit(solution)/shard_map/all_to_all | solution.py:427
  28.7 7.1 %all-to-all-start.1 = ((bf16[16,40,1536]{2,1,0:T(8,128)(2,1)}), bf16[16,40,1536]{2,1,0:T(8,128)(2,1)S(1)}, u32[]{:S(2)}, u32[]{:S(2)}) async-start(bf16[16,40,1536]{2,1,0:T(8,128)(2,1)} %bitcast.69), calls=%async_computation.1 | async-start | bytes 3932160 | tf_op jit(solution)/shard_map/all_to_all | solution.py:427
  39.4 12.8 %collective-permute-done.3.a1 = bf16[640,512]{1,0:T(8,128)(2,1)S(1)} collective-permute-done((bf16[640,512]{1,0:T(8,128)(2,1)S(1)}, bf16[640,512]{1,0:T(8,128)(2,1)S(1)}, u32[]{:S(2)}, u32[]{:S(2)}) %collective-permute-start.3) | collective-permute-done | bytes 655392 | tf_op jit(solution)/shard_map/ppermute | solution.py:19
  58.9 6.1 %up_first.1.before_ref = f32[640,1024]{1,0:T(8,128)S(1)} custom-call(s32[2]{0:T(128)S(1)} %pad_add_fusion.place_ref, bf16[640,512]{1,0:T(8,128)(2,1)S(1)} %bitcast.67, bf16[640,512]{1,0:T(8,128)(2,1)S(1)} %collective-permute-done.3.a1, bf16[640,512]{1,0:T(8,128)(2,1)S(1)} %copy-done.7, bf16[7168,256]{1,0:T(8,128)(2,1)} %bitcast.73, ...), custom_call_target="tpu_custom_call" | custom-call | flops 2013265920 | bytes 3145728 | tf_op jit(solution)/shard_map/up_first/pallas_call | solution.py:477
  66.6 9.9 %up_second.1 = (f32[640,1024]{1,0:T(8,128)}, bf16[640,1024]{1,0:T(8,128)(2,1)S(1)}) custom-call(s32[2]{0:T(128)S(1)} %pad_add_fusion.place_ref, f32[640,1024]{1,0:T(8,128)} %copy-done, bf16[640,1536]{1,0:T(8,128)(2,1)S(1)} %bitcast.64, bf16[320,512]{1,0:T(8,128)(2,1)} %collective-permute-done.7.a2_top, bf16[320,512]{1,0:T(8,128)(2,1)} %collective-permute-done.8.a2_low, ...), custom_call_target="tpu_custom_call" | custom-call | tf_op jit(solution)/shard_map/up_second/pallas_call | solution.py:493
  80.6 10.2 %down.1 = (bf16[640,512]{1,0:T(8,128)(2,1)}, bf16[320,512]{1,0:T(8,128)(2,1)}, bf16[320,512]{1,0:T(8,128)(2,1)}, bf16[320,512]{1,0:T(8,128)(2,1)}, bf16[320,512]...) custom-call(s32[2]{0:T(128)} %copy-done.19, ...), custom_call_target="tpu_custom_call" | custom-call | tf_op jit(solution)/shard_map/down/pallas_call | solution.py:512
  90.9 7.0 %all-to-all-start.3 = ((bf16[16,40,1536]{2,1,0:T(8,128)(2,1)}), bf16[16,40,1536]{2,1,0:T(8,128)(2,1)S(1)}, u32[]{:S(2)}, u32[]{:S(2)}) async-start(bf16[16,40,1536]{2,1,0:T(8,128)(2,1)} %bitcast.80), calls=%async_computation.3 | async-start | bytes 3932160 | tf_op jit(solution)/shard_map/all_to_all | solution.py:427
  103.8 4.9 %collective-permute-done.11.got1 = bf16[320,512]{1,0:T(8,128)(2,1)S(1)} collective-permute-done((bf16[320,512]{1,0:T(8,128)(2,1)S(1)}, bf16[320,512]{1,0:T(8,128)(2,1)S(1)}, u32[]{:S(2)}, u32[]{:S(2)}) %collective-permute-start.11) | collective-permute-done | bytes 327712 | tf_op jit(solution)/shard_map/ppermute | solution.py:19
  108.7 3.7 %collective-permute-done.12.got3 = bf16[320,512]{1,0:T(8,128)(2,1)S(1)} collective-permute-done((bf16[320,512]{1,0:T(8,128)(2,1)S(1)}, bf16[320,512]{1,0:T(8,128)(2,1)S(1)}, u32[]{:S(2)}, u32[]{:S(2)}) %collective-permute-start.12) | collective-permute-done | bytes 327712 | tf_op jit(solution)/shard_map/ppermute | solution.py:19
  121.6 3.4 %collective-permute-done.16.right_low = bf16[320,512]{1,0:T(8,128)(2,1)S(1)} collective-permute-done((bf16[320,512]{1,0:T(8,128)(2,1)S(1)}, bf16[320,512]{1,0:T(8,128)(2,1)S(1)}, u32[]{:S(2)}, u32[]{:S(2)}) %collective-permute-start.16) | collective-permute-done | bytes 327712 | tf_op jit(solution)/shard_map/ppermute | solution.py:19
  127.3 5.7 %all-to-all-start.2 = ((bf16[16,40,512]{2,1,0:T(8,128)(2,1)}), bf16[16,40,512]{2,1,0:T(8,128)(2,1)S(1)}, u32[]{:S(2)}, u32[]{:S(2)}) async-start(bf16[16,40,512]{2,1,0:T(8,128)(2,1)} %bitcast.11), calls=%async_computation.2 | async-start | bytes 1310720 | tf_op jit(solution)/shard_map/all_to_all | solution.py:427
  136.0 8.4 %all-to-all-done.2 = bf16[16,40,512]{2,1,0:T(8,128)(2,1)S(1)} async-done(((bf16[16,40,512]{2,1,0:T(8,128)(2,1)}), bf16[16,40,512]{2,1,0:T(8,128)(2,1)S(1)}, u32[]{:S(2)}, u32[]{:S(2)}) %all-to-all-start.2) | async-done | bytes 655392 | tf_op jit(solution)/shard_map/all_to_all | solution.py:427
  148.7 5.2 %collective-permute-done.21 = bf16[96,896]{1,0:T(8,128)(2,1)S(1)} collective-permute-done((bf16[96,896]{1,0:T(8,128)(2,1)S(1)}, bf16[96,896]{1,0:T(8,128)(2,1)S(1)}, u32[]{:S(2)}, u32[]{:S(2)}) %collective-permute-start.21) | collective-permute-done | bytes 172064 | tf_op jit(solution)/shard_map/ppermute | solution.py:19
  161.6 3.3 %collective-permute-done.30 = bf16[4,48,896]{2,1,0:T(8,128)(2,1)S(1)} collective-permute-done((bf16[4,48,896]{2,1,0:T(8,128)(2,1)S(1)}, bf16[4,48,896]{2,1,0:T(8,128)(2,1)S(1)}, u32[]{:S(2)}, u32[]{:S(2)}) %collective-permute-start.30) | collective-permute-done | bytes 344096 | tf_op jit(solution)/shard_map/ppermute | solution.py:19
  165.0 3.4 %collective-permute-start.34 = (bf16[2,48,896]{2,1,0:T(8,128)(2,1)S(1)}, bf16[2,48,896]{2,1,0:T(8,128)(2,1)S(1)}, u32[]{:S(2)}, u32[]{:S(2)}) collective-permute-start(bf16[2,48,896]{2,1,0:T(8,128)(2,1)S(1)} %slice.67), channel_id=1, source_target_pairs={{0,24},{8,0},{16,8},{24,16},{1,25},{9,1},{17,9},{25,17},{2,26},{10... | collective-permute-start | bytes 516104 | tf_op jit(solution)/shard_map/ppermute | solution.py:19
  168.7 3.3 %collective-permute-start.28 = (bf16[2,48,896]{2,1,0:T(8,128)(2,1)S(1)}, bf16[2,48,896]{2,1,0:T(8,128)(2,1)S(1)}, u32[]{:S(2)}, u32[]{:S(2)}) collective-permute-start(bf16[2,48,896]{2,1,0:T(8,128)(2,1)S(1)} %slice.62), channel_id=1, source_target_pairs={{0,96},{32,0},{64,32},{96,64},{1,97},{33,1},{65,33},{97,65},{2,98}... | collective-permute-start | bytes 516104 | tf_op jit(solution)/shard_map/ppermute | solution.py:19
  173.8 3.4 %collective-permute-done.26 = bf16[2,48,896]{2,1,0:T(8,128)(2,1)S(1)} collective-permute-done((bf16[2,48,896]{2,1,0:T(8,128)(2,1)S(1)}, bf16[2,48,896]{2,1,0:T(8,128)(2,1)S(1)}, u32[]{:S(2)}, u32[]{:S(2)}) %collective-permute-start.26) | collective-permute-done | bytes 172064 | tf_op jit(solution)/shard_map/ppermute | solution.py:19
  181.6 7.1 %collective-permute-done.31.refs_4_ = bf16[2,4,48,896]{3,2,1,0:T(8,128)(2,1)S(1)} collective-permute-done((bf16[2,4,48,896]{3,2,1,0:T(8,128)(2,1)S(1)}, bf16[2,4,48,896]{3,2,1,0:T(8,128)(2,1)S(1)}, u32[]{:S(2)}, u32[]{:S(2)}) %collective-permute-start.31) | collective-permute-done | bytes 688160 | tf_op jit(solution)/shard_map/ppermute | solution.py:19
  189.2 6.0 %collective-permute-done.35.refs_7_ = bf16[2,4,48,896]{3,2,1,0:T(8,128)(2,1)S(1)} collective-permute-done((bf16[2,4,48,896]{3,2,1,0:T(8,128)(2,1)S(1)}, bf16[2,4,48,896]{3,2,1,0:T(8,128)(2,1)S(1)}, u32[]{:S(2)}, u32[]{:S(2)}) %collective-permute-start.35) | collective-permute-done | bytes 688160 | tf_op jit(solution)/shard_map/ppermute | solution.py:19
  196.1 9.3 %head.3 = (f32[384,640]{1,0:T(8,128)}, f32[384,640]{1,0:T(8,128)}) custom-call(s32[2]{0:T(128)} %copy-done.19, f32[4,896]{1,0:T(4,128)} %copy-done.17, bf16[512,7168]{1,0:T(8,128)(2,1)} %w0.5, bf16[512,7168]{1,0:T(8,128)(2,1)} %collective-permute-done.20.w1, bf16[2,4,48,896]{3,2,1,0:T(8,128)(2,1)} %copy-done.23, ...), custom_call_target="tpu_custom_call" | custom-call | flops 2818572288 | bytes 7340032 | tf_op jit(solution)/shard_map/head/pallas_call | solution.py:575
  213.4 14.6 %head.4 = (f32[768,640]{1,0:T(8,128)}, f32[768,640]{1,0:T(8,128)}) custom-call(s32[2]{0:T(128)} %copy-done.19, f32[4,896]{1,0:T(4,128)} %copy-done.17, bf16[512,7168]{1,0:T(8,128)(2,1)} %w0.5, bf16[512,7168]{1,0:T(8,128)(2,1)} %collective-permute-done.20.w1, bf16[2,4,48,896]{3,2,1,0:T(8,128)(2,1)} %copy-done.39, ...), custom_call_target="tpu_custom_call" | custom-call | flops 5637144576 | bytes 7340032 | tf_op jit(solution)/shard_map/head/pallas_call | solution.py:575
  229.5 7.4 %head.5 = (f32[384,640]{1,0:T(8,128)S(1)}, f32[384,640]{1,0:T(8,128)}) custom-call(s32[2]{0:T(128)S(1)} %copy-done.20, f32[4,896]{1,0:T(4,128)S(1)} %copy-done.18, bf16[512,7168]{1,0:T(8,128)(2,1)} %w0.5, bf16[512,7168]{1,0:T(8,128)(2,1)} %collective-permute-done.20.w1, bf16[2,4,48,896]{3,2,1,0:T(8,128)(2,1)S(1)} %collective-permute-done.36.refs_0_, ...), custom_call_target="tpu_custom_call" | custom-call | flops 2818572288 | bytes 7340032 | tf_op jit(solution)/shard_map/head/pallas_call | solution.py:575
  247.2 3.7 %collective-permute-start.49 = (f32[48,128]{1,0:T(8,128)}, f32[48,128]{1,0:T(8,128)S(1)}, u32[]{:S(2)}, u32[]{:S(2)}) collective-permute-start(f32[48,128]{1,0:T(8,128)} %merge.3.refs_0_), channel_id=1, source_target_pairs={{0,4},{2,6},{4,0},{6,2},{1,5},{3,7},{5,1},{7,3},{8,12},{10,14},{12... | collective-permute-start | bytes 73736 | tf_op jit(solution)/shard_map/ppermute | solution.py:19
  265.8 3.3 %collective-permute-start.55 = (f32[48,128]{1,0:T(8,128)}, f32[48,128]{1,0:T(8,128)S(1)}, u32[]{:S(2)}, u32[]{:S(2)}) collective-permute-start(f32[48,128]{1,0:T(8,128)} %merge.5.refs_0_), channel_id=1, source_target_pairs={{0,64},{32,96},{64,0},{96,32},{1,65},{33,97},{65,1},{97,33},{2,66}... | collective-permute-start | bytes 73736 | tf_op jit(solution)/shard_map/ppermute | solution.py:19
  (231 shorter events, 116.8 us)
Async XLA Ops:
  0.6 54.2 %collective-permute-start.5 = (bf16[7168,256]{1,0:T(8,128)(2,1)}, bf16[7168,256]{1,0:T(8,128)(2,1)}, u32[]{:S(2)}, u32[]{:S(2)}) collective-permute-start(bf16[7168,256]{1,0:T(8,128)(2,1)} %bitcast.72), channel_id=1, source_target_pairs={{0,1},{1,0},{2,3},{3,2},{4,5},{5,4},{6,7},{7,6},{8,9},{9,8},{10,11... | collective-permute-start | bytes 11010056 | tf_op jit(solution)/shard_map/ppermute | solution.py:19
  0.7 57.1 %collective-permute-start.6 = (bf16[7168,256]{1,0:T(8,128)(2,1)}, bf16[7168,256]{1,0:T(8,128)(2,1)}, u32[]{:S(2)}, u32[]{:S(2)}) collective-permute-start(bf16[7168,256]{1,0:T(8,128)(2,1)} %bitcast.75), channel_id=1, source_target_pairs={{0,1},{1,0},{2,3},{3,2},{4,5},{5,4},{6,7},{7,6},{8,9},{9,8},{10,11... | collective-permute-start | bytes 11010056 | tf_op jit(solution)/shard_map/ppermute | solution.py:19
  5.7 23.0 %all-to-all-start = ((bf16[16,40,512]{2,1,0:T(8,128)(2,1)}), bf16[16,40,512]{2,1,0:T(8,128)(2,1)S(1)}, u32[]{:S(2)}, u32[]{:S(2)}) async-start(bf16[16,40,512]{2,1,0:T(8,128)(2,1)} %bitcast.4), calls=%async_computation | async-start | bytes 1310720 | tf_op jit(solution)/shard_map/all_to_all | solution.py:427
  13.7 62.9 %collective-permute-start.10 = (bf16[256,7168]{1,0:T(8,128)(2,1)}, bf16[256,7168]{1,0:T(8,128)(2,1)}, u32[]{:S(2)}, u32[]{:S(2)}) collective-permute-start(bf16[256,7168]{1,0:T(8,128)(2,1)} %bitcast.78), channel_id=1, source_target_pairs={{0,1},{1,0},{2,3},{3,2},{4,5},{5,4},{6,7},{7,6},{8,9},{9,8},{10,11... | collective-permute-start | bytes 11010056 | tf_op jit(solution)/shard_map/ppermute | solution.py:19
  28.7 37.8 %all-to-all-start.1 = ((bf16[16,40,1536]{2,1,0:T(8,128)(2,1)}), bf16[16,40,1536]{2,1,0:T(8,128)(2,1)S(1)}, u32[]{:S(2)}, u32[]{:S(2)}) async-start(bf16[16,40,1536]{2,1,0:T(8,128)(2,1)} %bitcast.69), calls=%async_computation.1 | async-start | bytes 3932160 | tf_op jit(solution)/shard_map/all_to_all | solution.py:427
  35.9 16.3 %collective-permute-start.3 = (bf16[640,512]{1,0:T(8,128)(2,1)S(1)}, bf16[640,512]{1,0:T(8,128)(2,1)S(1)}, u32[]{:S(2)}, u32[]{:S(2)}) collective-permute-start(bf16[640,512]{1,0:T(8,128)(2,1)S(1)} %bitcast.65), channel_id=1, source_target_pairs={{0,2},{2,4},{4,6},{6,0},{1,3},{3,5},{5,7},{7,1},{8,10},{10,12},{12... | collective-permute-start | bytes 1966088 | tf_op jit(solution)/shard_map/ppermute | solution.py:19
  36.4 16.5 %collective-permute-start.4 = (bf16[640,512]{1,0:T(8,128)(2,1)S(1)}, bf16[640,512]{1,0:T(8,128)(2,1)S(1)}, u32[]{:S(2)}, u32[]{:S(2)}) collective-permute-start(bf16[640,512]{1,0:T(8,128)(2,1)S(1)} %bitcast.66), channel_id=1, source_target_pairs={{0,6},{2,0},{4,2},{6,4},{1,7},{3,1},{5,3},{7,5},{8,14},{10,8},{12,... | collective-permute-start | bytes 1966088 | tf_op jit(solution)/shard_map/ppermute | solution.py:19
  52.2 129.0 %collective-permute-start.20 = (bf16[512,7168]{1,0:T(8,128)(2,1)}, bf16[512,7168]{1,0:T(8,128)(2,1)}, u32[]{:S(2)}, u32[]{:S(2)}) collective-permute-start(bf16[512,7168]{1,0:T(8,128)(2,1)} %w0.5), channel_id=1, source_target_pairs={{0,1},{1,0},{2,3},{3,2},{4,5},{5,4},{6,7},{7,6},{8,9},{9,8},{10,11... | collective-permute-start | bytes 22020104 | tf_op jit(solution)/shard_map/ppermute | solution.py:19
  90.9 36.4 %all-to-all-start.3 = ((bf16[16,40,1536]{2,1,0:T(8,128)(2,1)}), bf16[16,40,1536]{2,1,0:T(8,128)(2,1)S(1)}, u32[]{:S(2)}, u32[]{:S(2)}) async-start(bf16[16,40,1536]{2,1,0:T(8,128)(2,1)} %bitcast.80), calls=%async_computation.3 | async-start | bytes 3932160 | tf_op jit(solution)/shard_map/all_to_all | solution.py:427
  100.5 16.0 %collective-permute-start.14 = (bf16[320,512]{1,0:T(8,128)(2,1)}, bf16[320,512]{1,0:T(8,128)(2,1)S(1)}, u32[]{:S(2)}, u32[]{:S(2)}) collective-permute-start(bf16[320,512]{1,0:T(8,128)(2,1)} %get-tuple-element.65), channel_id=1, source_target_pairs={{0,6},{2,0},{4,2},{6,4},{1,7},{3,1},{5,3},{7,5},{8,14},{10,8},{12,... | collective-permute-start | bytes 983048 | tf_op jit(solution)/shard_map/ppermute | solution.py:19
  103.8 15.6 %collective-permute-start.15 = (bf16[320,512]{1,0:T(8,128)(2,1)}, bf16[320,512]{1,0:T(8,128)(2,1)S(1)}, u32[]{:S(2)}, u32[]{:S(2)}) collective-permute-start(bf16[320,512]{1,0:T(8,128)(2,1)} %get-tuple-element.66), channel_id=1, source_target_pairs={{0,2},{2,4},{4,6},{6,0},{1,3},{3,5},{5,7},{7,1},{8,10},{10,12},{12... | collective-permute-start | bytes 983048 | tf_op jit(solution)/shard_map/ppermute | solution.py:19
  127.3 17.1 %all-to-all-start.2 = ((bf16[16,40,512]{2,1,0:T(8,128)(2,1)}), bf16[16,40,512]{2,1,0:T(8,128)(2,1)S(1)}, u32[]{:S(2)}, u32[]{:S(2)}) async-start(bf16[16,40,512]{2,1,0:T(8,128)(2,1)} %bitcast.11), calls=%async_computation.2 | async-start | bytes 1310720 | tf_op jit(solution)/shard_map/all_to_all | solution.py:427
  173.5 15.3 %collective-permute-start.31 = (bf16[2,4,48,896]{3,2,1,0:T(8,128)(2,1)S(1)}, bf16[2,4,48,896]{3,2,1,0:T(8,128)(2,1)S(1)}, u32[]{:S(2)}, u32[]{:S(2)}) collective-permute-start(bf16[2,4,48,896]{3,2,1,0:T(8,128)(2,1)S(1)} %pad_maximum_fusion.2.refs_2_), channel_id=1, source_target_pairs={{0,32},{32,64},{64,96},{96,0},{1,33},{33,65},{65,97},{97,1},{2,34}... | collective-permute-start | bytes 2064392 | tf_op jit(solution)/shard_map/ppermute | solution.py:19
  173.6 15.1 %collective-permute-start.25 = (bf16[2,4,48,896]{3,2,1,0:T(8,128)(2,1)S(1)}, bf16[2,4,48,896]{3,2,1,0:T(8,128)(2,1)S(1)}, u32[]{:S(2)}, u32[]{:S(2)}) collective-permute-start(bf16[2,4,48,896]{3,2,1,0:T(8,128)(2,1)S(1)} %pad_maximum_fusion.refs_0_), channel_id=1, source_target_pairs={{0,8},{8,16},{16,24},{24,0},{1,9},{9,17},{17,25},{25,1},{2,10},{10... | collective-permute-start | bytes 2064392 | tf_op jit(solution)/shard_map/ppermute | solution.py:19
  177.2 18.1 %collective-permute-start.35 = (bf16[2,4,48,896]{3,2,1,0:T(8,128)(2,1)S(1)}, bf16[2,4,48,896]{3,2,1,0:T(8,128)(2,1)S(1)}, u32[]{:S(2)}, u32[]{:S(2)}) collective-permute-start(bf16[2,4,48,896]{3,2,1,0:T(8,128)(2,1)S(1)} %pad_maximum_fusion.3.refs_3_), channel_id=1, source_target_pairs={{0,96},{32,0},{64,32},{96,64},{1,97},{33,1},{65,33},{97,65},{2,98}... | collective-permute-start | bytes 2064392 | tf_op jit(solution)/shard_map/ppermute | solution.py:19
  178.2 27.2 %collective-permute-start.29 = (bf16[2,4,48,896]{3,2,1,0:T(8,128)(2,1)}, bf16[2,4,48,896]{3,2,1,0:T(8,128)(2,1)S(1)}, u32[]{:S(2)}, u32[]{:S(2)}) collective-permute-start(bf16[2,4,48,896]{3,2,1,0:T(8,128)(2,1)} %pad_maximum_fusion.1.refs_1_), channel_id=1, source_target_pairs={{0,24},{8,0},{16,8},{24,16},{1,25},{9,1},{17,9},{25,17},{2,26},{10... | collective-permute-start | bytes 2064392 | tf_op jit(solution)/shard_map/ppermute | solution.py:19
  181.1 25.1 %collective-permute-start.43 = (bf16[2,4,48,896]{3,2,1,0:T(8,128)(2,1)S(1)}, bf16[2,4,48,896]{3,2,1,0:T(8,128)(2,1)}, u32[]{:S(2)}, u32[]{:S(2)}) collective-permute-start(bf16[2,4,48,896]{3,2,1,0:T(8,128)(2,1)S(1)} %pad_maximum_fusion.2.refs_2_), channel_id=1, source_target_pairs={{0,96},{32,0},{64,32},{96,64},{1,97},{33,1},{65,33},{97,65},{2,98}... | collective-permute-start | bytes 2064392 | tf_op jit(solution)/shard_map/ppermute | solution.py:19
  188.7 17.5 %collective-permute-start.41 = (bf16[2,4,48,896]{3,2,1,0:T(8,128)(2,1)S(1)}, bf16[2,4,48,896]{3,2,1,0:T(8,128)(2,1)}, u32[]{:S(2)}, u32[]{:S(2)}) collective-permute-start(bf16[2,4,48,896]{3,2,1,0:T(8,128)(2,1)S(1)} %pad_maximum_fusion.refs_0_), channel_id=1, source_target_pairs={{0,24},{8,0},{16,8},{24,16},{1,25},{9,1},{17,9},{25,17},{2,26},{10... | collective-permute-start | bytes 2064392 | tf_op jit(solution)/shard_map/ppermute | solution.py:19
  188.7 20.7 %collective-permute-start.42 = (bf16[2,4,48,896]{3,2,1,0:T(8,128)(2,1)S(1)}, bf16[2,4,48,896]{3,2,1,0:T(8,128)(2,1)}, u32[]{:S(2)}, u32[]{:S(2)}) collective-permute-start(bf16[2,4,48,896]{3,2,1,0:T(8,128)(2,1)S(1)} %pad_maximum_fusion.3.refs_3_), channel_id=1, source_target_pairs={{0,32},{32,64},{64,96},{96,0},{1,33},{33,65},{65,97},{97,1},{2,34}... | collective-permute-start | bytes 2064392 | tf_op jit(solution)/shard_map/ppermute | solution.py:19
  206.2 21.9 %collective-permute-start.44 = (f32[384,640]{1,0:T(8,128)}, f32[384,640]{1,0:T(8,128)S(1)}, u32[]{:S(2)}, u32[]{:S(2)}) collective-permute-start(f32[384,640]{1,0:T(8,128)} %get-tuple-element.85), channel_id=1, source_target_pairs={{0,1},{1,0},{2,3},{3,2},{4,5},{5,4},{6,7},{7,6},{8,9},{9,8},{10,11... | collective-permute-start | bytes 2949128 | tf_op jit(solution)/shard_map/ppermute | solution.py:19
  206.2 23.1 %collective-permute-start.36 = (bf16[2,4,48,896]{3,2,1,0:T(8,128)(2,1)}, bf16[2,4,48,896]{3,2,1,0:T(8,128)(2,1)S(1)}, u32[]{:S(2)}, u32[]{:S(2)}) collective-permute-start(bf16[2,4,48,896]{3,2,1,0:T(8,128)(2,1)} %copy-done.39), channel_id=1, source_target_pairs={{0,8},{8,16},{16,24},{24,0},{1,9},{9,17},{17,25},{25,1},{2,10},{10... | collective-permute-start | bytes 2064392 | tf_op jit(solution)/shard_map/ppermute | solution.py:19
  206.3 23.1 %collective-permute-start.37 = (bf16[2,4,48,896]{3,2,1,0:T(8,128)(2,1)}, bf16[2,4,48,896]{3,2,1,0:T(8,128)(2,1)}, u32[]{:S(2)}, u32[]{:S(2)}) collective-permute-start(bf16[2,4,48,896]{3,2,1,0:T(8,128)(2,1)} %copy-done.41), channel_id=1, source_target_pairs={{0,24},{8,0},{16,8},{24,16},{1,25},{9,1},{17,9},{25,17},{2,26},{10... | collective-permute-start | bytes 2064392 | tf_op jit(solution)/shard_map/ppermute | solution.py:19
  209.5 19.8 %collective-permute-start.38 = (bf16[2,4,48,896]{3,2,1,0:T(8,128)(2,1)}, bf16[2,4,48,896]{3,2,1,0:T(8,128)(2,1)}, u32[]{:S(2)}, u32[]{:S(2)}) collective-permute-start(bf16[2,4,48,896]{3,2,1,0:T(8,128)(2,1)} %copy-done.38), channel_id=1, source_target_pairs={{0,32},{32,64},{64,96},{96,0},{1,33},{33,65},{65,97},{97,1},{2,34}... | collective-permute-start | bytes 2064392 | tf_op jit(solution)/shard_map/ppermute | solution.py:19
  209.5 19.8 %collective-permute-start.39 = (bf16[2,4,48,896]{3,2,1,0:T(8,128)(2,1)}, bf16[2,4,48,896]{3,2,1,0:T(8,128)(2,1)}, u32[]{:S(2)}, u32[]{:S(2)}) collective-permute-start(bf16[2,4,48,896]{3,2,1,0:T(8,128)(2,1)} %copy-done.40), channel_id=1, source_target_pairs={{0,96},{32,0},{64,32},{96,64},{1,97},{33,1},{65,33},{97,65},{2,98}... | collective-permute-start | bytes 2064392 | tf_op jit(solution)/shard_map/ppermute | solution.py:19
  (81 other events, 529.9 us)

commit v8 on v7

--- a/solution.py
+++ b/solution.py
@@ -613,7 +613,7 @@
     onward_b = (shift(lines_b[0], "x", 1), shift(lines_b[1], "x", -1))
     rest_a = (shift(lines_a[1], "z", 1), shift(lines_a[0], "z", -1))
     rest_b = (shift(lines_b[1], "x", 1), shift(lines_b[0], "x", -1))
-    scores = scored(lines_a + lines_b, 60)
+    scores = scored(lines_a + lines_b, VMEM)
     (onward_a, onward_b), (own, other) = lax.optimization_barrier(((onward_a, onward_b), scores))
     far_a1, far_a2 = shift(onward_a[0], "z", 1), shift(onward_a[1], "z", -1)
     far_b1, far_b2 = shift(onward_b[0], "x", 1), shift(onward_b[1], "x", -1)

time: 276 us -> 274 us (level)
  waiting for transfers between devices: 86.4 us -> 89.3 us
    ppermute x57, waiting for transfers between devices: 76.8 us -> 79.9 us  [shift(): lax.ppermute(value, axis, [(i, (i + step) % size) for i in range(size)])]
    unnamed x88 -> x80, local copies, waits for them, and re-layouts: 17.3 us -> 15.9 us
  transfers between devices with their start and end apart: 61 -> 61, of which waited for: 30 -> 33; matrix products, arithmetic and copies ran while one was open for 2% -> 1% of each run, Pallas kernels for 24% -> 24%
where the time goes in v8:
time: 274 us; the launch traced here: 272 us
  starting transfers between devices  89.6 us (33%)
  waiting for transfers between devices  89.3 us (33%)
  Pallas kernels  72.6 us (26%)
  local copies, waits for them, and re-layouts  19.1 us (7%)
    ppermute x57, waiting for transfers between devices, shift(): lax.ppermute(value, axis, [(i, (i + step) % size) for i in range(size)])  79.9 us
    ppermute x57, starting transfers between devices, shift(): lax.ppermute(value, axis, [(i, (i + step) % size) for i in range(size)])  61.7 us
    pallas_call x3, Pallas kernels, scored(): pl.pallas_call(head_kernel, grid_spec=pltpu.PrefetchScalarGridSpec(num_sc...  28.6 us
    all_to_all x4, starting transfers between devices, over_nodes(): lax.all_to_all(cut, ('x', 'z'), split_axis=0, concat_axis=0, tiled=True)  27.9 us
    unnamed x80, local copies, waits for them, and re-layouts  15.9 us
    pallas_call x1, Pallas kernels, shards(): pl.pallas_call(down_kernel, grid_spec=pltpu.PrefetchScalarGridSpec(num_sc...  10.2 us
    pallas_call x1, Pallas kernels, shards(): pl.pallas_call(up_second_kernel, grid_spec=pltpu.PrefetchScalarGridSpec(n...  9.87 us
    all_to_all x4, waiting for transfers between devices, over_nodes(): lax.all_to_all(cut, ('x', 'z'), split_axis=0, concat_axis=0, tiled=True)  9.4 us
  transfers between devices with their start and end apart: 61, of which 33 were waited for; matrix products, arithmetic and copies ran while one was open for 1% of the time, Pallas kernels for 24%

profile of v8, /device:TPU:0, one launch (start us, length us, event | category | flops | bytes accessed | tf_op | source)
XLA Modules:
  0.0 272.4 jit_solution(14840278074392728035)
XLA Ops:
  5.7 8.0 %all-to-all-start = ((bf16[16,40,512]{2,1,0:T(8,128)(2,1)}), bf16[16,40,512]{2,1,0:T(8,128)(2,1)S(1)}, u32[]{:S(2)}, u32[]{:S(2)}) async-start(bf16[16,40,512]{2,1,0:T(8,128)(2,1)} %bitcast.4), calls=%async_computation | async-start | bytes 1310720 | tf_op jit(solution)/shard_map/all_to_all | solution.py:427
  28.1 7.1 %all-to-all-start.1 = ((bf16[16,40,1536]{2,1,0:T(8,128)(2,1)}), bf16[16,40,1536]{2,1,0:T(8,128)(2,1)S(1)}, u32[]{:S(2)}, u32[]{:S(2)}) async-start(bf16[16,40,1536]{2,1,0:T(8,128)(2,1)} %bitcast.69), calls=%async_computation.1 | async-start | bytes 3932160 | tf_op jit(solution)/shard_map/all_to_all | solution.py:427
  38.8 12.8 %collective-permute-done.3.a1 = bf16[640,512]{1,0:T(8,128)(2,1)S(1)} collective-permute-done((bf16[640,512]{1,0:T(8,128)(2,1)S(1)}, bf16[640,512]{1,0:T(8,128)(2,1)S(1)}, u32[]{:S(2)}, u32[]{:S(2)}) %collective-permute-start.3) | collective-permute-done | bytes 655392 | tf_op jit(solution)/shard_map/ppermute | solution.py:19
  58.3 6.1 %up_first.1.before_ref = f32[640,1024]{1,0:T(8,128)S(1)} custom-call(s32[2]{0:T(128)S(1)} %pad_add_fusion.place_ref, bf16[640,512]{1,0:T(8,128)(2,1)S(1)} %bitcast.67, bf16[640,512]{1,0:T(8,128)(2,1)S(1)} %collective-permute-done.3.a1, bf16[640,512]{1,0:T(8,128)(2,1)S(1)} %copy-done.7, bf16[7168,256]{1,0:T(8,128)(2,1)} %bitcast.73, ...), custom_call_target="tpu_custom_call" | custom-call | flops 2013265920 | bytes 3145728 | tf_op jit(solution)/shard_map/up_first/pallas_call | solution.py:477
  66.0 9.9 %up_second.1 = (f32[640,1024]{1,0:T(8,128)}, bf16[640,1024]{1,0:T(8,128)(2,1)S(1)}) custom-call(s32[2]{0:T(128)S(1)} %pad_add_fusion.place_ref, f32[640,1024]{1,0:T(8,128)} %copy-done, bf16[640,1536]{1,0:T(8,128)(2,1)S(1)} %bitcast.64, bf16[320,512]{1,0:T(8,128)(2,1)} %collective-permute-done.7.a2_top, bf16[320,512]{1,0:T(8,128)(2,1)} %collective-permute-done.8.a2_low, ...), custom_call_target="tpu_custom_call" | custom-call | tf_op jit(solution)/shard_map/up_second/pallas_call | solution.py:493
  80.1 10.2 %down.1 = (bf16[640,512]{1,0:T(8,128)(2,1)}, bf16[320,512]{1,0:T(8,128)(2,1)}, bf16[320,512]{1,0:T(8,128)(2,1)}, bf16[320,512]{1,0:T(8,128)(2,1)}, bf16[320,512]...) custom-call(s32[2]{0:T(128)} %copy-done.18, ...), custom_call_target="tpu_custom_call" | custom-call | tf_op jit(solution)/shard_map/down/pallas_call | solution.py:512
  90.3 7.0 %all-to-all-start.3 = ((bf16[16,40,1536]{2,1,0:T(8,128)(2,1)}), bf16[16,40,1536]{2,1,0:T(8,128)(2,1)S(1)}, u32[]{:S(2)}, u32[]{:S(2)}) async-start(bf16[16,40,1536]{2,1,0:T(8,128)(2,1)} %bitcast.80), calls=%async_computation.3 | async-start | bytes 3932160 | tf_op jit(solution)/shard_map/all_to_all | solution.py:427
  103.2 5.2 %collective-permute-done.11.got1 = bf16[320,512]{1,0:T(8,128)(2,1)S(1)} collective-permute-done((bf16[320,512]{1,0:T(8,128)(2,1)}, bf16[320,512]{1,0:T(8,128)(2,1)S(1)}, u32[]{:S(2)}, u32[]{:S(2)}) %collective-permute-start.11) | collective-permute-done | bytes 327712 | tf_op jit(solution)/shard_map/ppermute | solution.py:19
  108.4 3.6 %collective-permute-done.12.got3 = bf16[320,512]{1,0:T(8,128)(2,1)S(1)} collective-permute-done((bf16[320,512]{1,0:T(8,128)(2,1)}, bf16[320,512]{1,0:T(8,128)(2,1)S(1)}, u32[]{:S(2)}, u32[]{:S(2)}) %collective-permute-start.12) | collective-permute-done | bytes 327712 | tf_op jit(solution)/shard_map/ppermute | solution.py:19
  121.2 3.3 %collective-permute-done.16.right_low = bf16[320,512]{1,0:T(8,128)(2,1)S(1)} collective-permute-done((bf16[320,512]{1,0:T(8,128)(2,1)S(1)}, bf16[320,512]{1,0:T(8,128)(2,1)S(1)}, u32[]{:S(2)}, u32[]{:S(2)}) %collective-permute-start.16) | collective-permute-done | bytes 327712 | tf_op jit(solution)/shard_map/ppermute | solution.py:19
  126.7 5.8 %all-to-all-start.2 = ((bf16[16,40,512]{2,1,0:T(8,128)(2,1)}), bf16[16,40,512]{2,1,0:T(8,128)(2,1)S(1)}, u32[]{:S(2)}, u32[]{:S(2)}) async-start(bf16[16,40,512]{2,1,0:T(8,128)(2,1)} %bitcast.11), calls=%async_computation.2 | async-start | bytes 1310720 | tf_op jit(solution)/shard_map/all_to_all | solution.py:427
  135.6 8.3 %all-to-all-done.2 = bf16[16,40,512]{2,1,0:T(8,128)(2,1)S(1)} async-done(((bf16[16,40,512]{2,1,0:T(8,128)(2,1)}), bf16[16,40,512]{2,1,0:T(8,128)(2,1)S(1)}, u32[]{:S(2)}, u32[]{:S(2)}) %all-to-all-start.2) | async-done | bytes 655392 | tf_op jit(solution)/shard_map/all_to_all | solution.py:427
  148.2 5.2 %collective-permute-done.21 = bf16[96,896]{1,0:T(8,128)(2,1)S(1)} collective-permute-done((bf16[96,896]{1,0:T(8,128)(2,1)S(1)}, bf16[96,896]{1,0:T(8,128)(2,1)S(1)}, u32[]{:S(2)}, u32[]{:S(2)}) %collective-permute-start.21) | collective-permute-done | bytes 172064 | tf_op jit(solution)/shard_map/ppermute | solution.py:19
  161.1 3.3 %collective-permute-done.30 = bf16[4,48,896]{2,1,0:T(8,128)(2,1)S(1)} collective-permute-done((bf16[4,48,896]{2,1,0:T(8,128)(2,1)S(1)}, bf16[4,48,896]{2,1,0:T(8,128)(2,1)S(1)}, u32[]{:S(2)}, u32[]{:S(2)}) %collective-permute-start.30) | collective-permute-done | bytes 344096 | tf_op jit(solution)/shard_map/ppermute | solution.py:19
  164.6 3.4 %collective-permute-start.34 = (bf16[2,48,896]{2,1,0:T(8,128)(2,1)S(1)}, bf16[2,48,896]{2,1,0:T(8,128)(2,1)S(1)}, u32[]{:S(2)}, u32[]{:S(2)}) collective-permute-start(bf16[2,48,896]{2,1,0:T(8,128)(2,1)S(1)} %slice.67), channel_id=1, source_target_pairs={{0,24},{8,0},{16,8},{24,16},{1,25},{9,1},{17,9},{25,17},{2,26},{10... | collective-permute-start | bytes 516104 | tf_op jit(solution)/shard_map/ppermute | solution.py:19
  168.2 3.3 %collective-permute-start.28 = (bf16[2,48,896]{2,1,0:T(8,128)(2,1)S(1)}, bf16[2,48,896]{2,1,0:T(8,128)(2,1)S(1)}, u32[]{:S(2)}, u32[]{:S(2)}) collective-permute-start(bf16[2,48,896]{2,1,0:T(8,128)(2,1)S(1)} %slice.62), channel_id=1, source_target_pairs={{0,96},{32,0},{64,32},{96,64},{1,97},{33,1},{65,33},{97,65},{2,98}... | collective-permute-start | bytes 516104 | tf_op jit(solution)/shard_map/ppermute | solution.py:19
  173.3 3.4 %collective-permute-done.26 = bf16[2,48,896]{2,1,0:T(8,128)(2,1)S(1)} collective-permute-done((bf16[2,48,896]{2,1,0:T(8,128)(2,1)S(1)}, bf16[2,48,896]{2,1,0:T(8,128)(2,1)S(1)}, u32[]{:S(2)}, u32[]{:S(2)}) %collective-permute-start.26) | collective-permute-done | bytes 172064 | tf_op jit(solution)/shard_map/ppermute | solution.py:19
  180.3 7.9 %collective-permute-done.31.refs_4_ = bf16[2,4,48,896]{3,2,1,0:T(8,128)(2,1)} collective-permute-done((bf16[2,4,48,896]{3,2,1,0:T(8,128)(2,1)S(1)}, bf16[2,4,48,896]{3,2,1,0:T(8,128)(2,1)}, u32[]{:S(2)}, u32[]{:S(2)}) %collective-permute-start.31) | collective-permute-done | bytes 688160 | tf_op jit(solution)/shard_map/ppermute | solution.py:19
  189.0 5.9 %collective-permute-done.35.refs_7_ = bf16[2,4,48,896]{3,2,1,0:T(8,128)(2,1)} collective-permute-done((bf16[2,4,48,896]{3,2,1,0:T(8,128)(2,1)S(1)}, bf16[2,4,48,896]{3,2,1,0:T(8,128)(2,1)}, u32[]{:S(2)}, u32[]{:S(2)}) %collective-permute-start.35) | collective-permute-done | bytes 688160 | tf_op jit(solution)/shard_map/ppermute | solution.py:19
  194.9 6.8 %head.3 = (f32[384,640]{1,0:T(8,128)S(1)}, f32[384,640]{1,0:T(8,128)}) custom-call(s32[2]{0:T(128)S(1)} %copy-done.19, f32[4,896]{1,0:T(4,128)S(1)} %get-tuple-element.74.inverse_ref, bf16[512,7168]{1,0:T(8,128)(2,1)} %w0.5, bf16[512,7168]{1,0:T(8,128)(2,1)} %collective-permute-done.20.w1, bf16[2,4,48,896]{3,2,1,0:T(8,128)(2,1)S(1)} %pad_maximum_fusion.refs_0_, ...), custom_call_target="tpu_custom_call" | custom-call | flops 2818572288 | bytes 7340032 | tf_op jit(solution)/shard_map/head/pallas_call | solution.py:575
  210.4 14.5 %head.4 = (f32[768,640]{1,0:T(8,128)}, f32[768,640]{1,0:T(8,128)}) custom-call(s32[2]{0:T(128)} %copy-done.18, f32[4,896]{1,0:T(4,128)} %copy-done.16, bf16[512,7168]{1,0:T(8,128)(2,1)} %w0.5, bf16[512,7168]{1,0:T(8,128)(2,1)} %collective-permute-done.20.w1, bf16[2,4,48,896]{3,2,1,0:T(8,128)(2,1)} %collective-permute-done.25.refs_0_, ...), custom_call_target="tpu_custom_call" | custom-call | flops 5637144576 | bytes 7340032 | tf_op jit(solution)/shard_map/head/pallas_call | solution.py:575
  226.3 7.3 %head.5 = (f32[384,640]{1,0:T(8,128)S(1)}, f32[384,640]{1,0:T(8,128)}) custom-call(s32[2]{0:T(128)S(1)} %copy-done.20, f32[4,896]{1,0:T(4,128)S(1)} %copy-done.17, bf16[512,7168]{1,0:T(8,128)(2,1)} %w0.5, bf16[512,7168]{1,0:T(8,128)(2,1)} %collective-permute-done.20.w1, bf16[2,4,48,896]{3,2,1,0:T(8,128)(2,1)S(1)} %collective-permute-done.36.refs_0_, ...), custom_call_target="tpu_custom_call" | custom-call | flops 2818572288 | bytes 7340032 | tf_op jit(solution)/shard_map/head/pallas_call | solution.py:575
  244.1 3.8 %collective-permute-start.49 = (f32[48,128]{1,0:T(8,128)}, f32[48,128]{1,0:T(8,128)S(1)}, u32[]{:S(2)}, u32[]{:S(2)}) collective-permute-start(f32[48,128]{1,0:T(8,128)} %merge.3.refs_0_), channel_id=1, source_target_pairs={{0,4},{2,6},{4,0},{6,2},{1,5},{3,7},{5,1},{7,3},{8,12},{10,14},{12... | collective-permute-start | bytes 73736 | tf_op jit(solution)/shard_map/ppermute | solution.py:19
  262.9 3.4 %collective-permute-start.55 = (f32[48,128]{1,0:T(8,128)}, f32[48,128]{1,0:T(8,128)S(1)}, u32[]{:S(2)}, u32[]{:S(2)}) collective-permute-start(f32[48,128]{1,0:T(8,128)} %merge.5.refs_0_), channel_id=1, source_target_pairs={{0,64},{32,96},{64,0},{96,32},{1,65},{33,97},{65,1},{97,33},{2,66}... | collective-permute-start | bytes 73736 | tf_op jit(solution)/shard_map/ppermute | solution.py:19
  (223 shorter events, 115.6 us)
Async XLA Ops:
  0.6 53.6 %collective-permute-start.5 = (bf16[7168,256]{1,0:T(8,128)(2,1)}, bf16[7168,256]{1,0:T(8,128)(2,1)}, u32[]{:S(2)}, u32[]{:S(2)}) collective-permute-start(bf16[7168,256]{1,0:T(8,128)(2,1)} %bitcast.72), channel_id=1, source_target_pairs={{0,1},{1,0},{2,3},{3,2},{4,5},{5,4},{6,7},{7,6},{8,9},{9,8},{10,11... | collective-permute-start | bytes 11010056 | tf_op jit(solution)/shard_map/ppermute | solution.py:19
  0.7 56.5 %collective-permute-start.6 = (bf16[7168,256]{1,0:T(8,128)(2,1)}, bf16[7168,256]{1,0:T(8,128)(2,1)}, u32[]{:S(2)}, u32[]{:S(2)}) collective-permute-start(bf16[7168,256]{1,0:T(8,128)(2,1)} %bitcast.75), channel_id=1, source_target_pairs={{0,1},{1,0},{2,3},{3,2},{4,5},{5,4},{6,7},{7,6},{8,9},{9,8},{10,11... | collective-permute-start | bytes 11010056 | tf_op jit(solution)/shard_map/ppermute | solution.py:19
  5.7 22.4 %all-to-all-start = ((bf16[16,40,512]{2,1,0:T(8,128)(2,1)}), bf16[16,40,512]{2,1,0:T(8,128)(2,1)S(1)}, u32[]{:S(2)}, u32[]{:S(2)}) async-start(bf16[16,40,512]{2,1,0:T(8,128)(2,1)} %bitcast.4), calls=%async_computation | async-start | bytes 1310720 | tf_op jit(solution)/shard_map/all_to_all | solution.py:427
  13.7 62.3 %collective-permute-start.10 = (bf16[256,7168]{1,0:T(8,128)(2,1)}, bf16[256,7168]{1,0:T(8,128)(2,1)}, u32[]{:S(2)}, u32[]{:S(2)}) collective-permute-start(bf16[256,7168]{1,0:T(8,128)(2,1)} %bitcast.78), channel_id=1, source_target_pairs={{0,1},{1,0},{2,3},{3,2},{4,5},{5,4},{6,7},{7,6},{8,9},{9,8},{10,11... | collective-permute-start | bytes 11010056 | tf_op jit(solution)/shard_map/ppermute | solution.py:19
  28.1 37.9 %all-to-all-start.1 = ((bf16[16,40,1536]{2,1,0:T(8,128)(2,1)}), bf16[16,40,1536]{2,1,0:T(8,128)(2,1)S(1)}, u32[]{:S(2)}, u32[]{:S(2)}) async-start(bf16[16,40,1536]{2,1,0:T(8,128)(2,1)} %bitcast.69), calls=%async_computation.1 | async-start | bytes 3932160 | tf_op jit(solution)/shard_map/all_to_all | solution.py:427
  35.3 16.3 %collective-permute-start.3 = (bf16[640,512]{1,0:T(8,128)(2,1)S(1)}, bf16[640,512]{1,0:T(8,128)(2,1)S(1)}, u32[]{:S(2)}, u32[]{:S(2)}) collective-permute-start(bf16[640,512]{1,0:T(8,128)(2,1)S(1)} %bitcast.65), channel_id=1, source_target_pairs={{0,2},{2,4},{4,6},{6,0},{1,3},{3,5},{5,7},{7,1},{8,10},{10,12},{12... | collective-permute-start | bytes 1966088 | tf_op jit(solution)/shard_map/ppermute | solution.py:19
  35.8 16.5 %collective-permute-start.4 = (bf16[640,512]{1,0:T(8,128)(2,1)S(1)}, bf16[640,512]{1,0:T(8,128)(2,1)S(1)}, u32[]{:S(2)}, u32[]{:S(2)}) collective-permute-start(bf16[640,512]{1,0:T(8,128)(2,1)S(1)} %bitcast.66), channel_id=1, source_target_pairs={{0,6},{2,0},{4,2},{6,4},{1,7},{3,1},{5,3},{7,5},{8,14},{10,8},{12,... | collective-permute-start | bytes 1966088 | tf_op jit(solution)/shard_map/ppermute | solution.py:19
  51.6 128.3 %collective-permute-start.20 = (bf16[512,7168]{1,0:T(8,128)(2,1)}, bf16[512,7168]{1,0:T(8,128)(2,1)}, u32[]{:S(2)}, u32[]{:S(2)}) collective-permute-start(bf16[512,7168]{1,0:T(8,128)(2,1)} %w0.5), channel_id=1, source_target_pairs={{0,1},{1,0},{2,3},{3,2},{4,5},{5,4},{6,7},{7,6},{8,9},{9,8},{10,11... | collective-permute-start | bytes 22020104 | tf_op jit(solution)/shard_map/ppermute | solution.py:19
  90.3 36.4 %all-to-all-start.3 = ((bf16[16,40,1536]{2,1,0:T(8,128)(2,1)}), bf16[16,40,1536]{2,1,0:T(8,128)(2,1)S(1)}, u32[]{:S(2)}, u32[]{:S(2)}) async-start(bf16[16,40,1536]{2,1,0:T(8,128)(2,1)} %bitcast.80), calls=%async_computation.3 | async-start | bytes 3932160 | tf_op jit(solution)/shard_map/all_to_all | solution.py:427
  99.9 16.3 %collective-permute-start.14 = (bf16[320,512]{1,0:T(8,128)(2,1)}, bf16[320,512]{1,0:T(8,128)(2,1)S(1)}, u32[]{:S(2)}, u32[]{:S(2)}) collective-permute-start(bf16[320,512]{1,0:T(8,128)(2,1)} %get-tuple-element.65), channel_id=1, source_target_pairs={{0,6},{2,0},{4,2},{6,4},{1,7},{3,1},{5,3},{7,5},{8,14},{10,8},{12,... | collective-permute-start | bytes 983048 | tf_op jit(solution)/shard_map/ppermute | solution.py:19
  103.2 15.8 %collective-permute-start.15 = (bf16[320,512]{1,0:T(8,128)(2,1)S(1)}, bf16[320,512]{1,0:T(8,128)(2,1)S(1)}, u32[]{:S(2)}, u32[]{:S(2)}) collective-permute-start(bf16[320,512]{1,0:T(8,128)(2,1)S(1)} %copy-done.39), channel_id=1, source_target_pairs={{0,2},{2,4},{4,6},{6,0},{1,3},{3,5},{5,7},{7,1},{8,10},{10,12},{12... | collective-permute-start | bytes 983048 | tf_op jit(solution)/shard_map/ppermute | solution.py:19
  126.7 17.2 %all-to-all-start.2 = ((bf16[16,40,512]{2,1,0:T(8,128)(2,1)}), bf16[16,40,512]{2,1,0:T(8,128)(2,1)S(1)}, u32[]{:S(2)}, u32[]{:S(2)}) async-start(bf16[16,40,512]{2,1,0:T(8,128)(2,1)} %bitcast.11), calls=%async_computation.2 | async-start | bytes 1310720 | tf_op jit(solution)/shard_map/all_to_all | solution.py:427
  173.0 15.3 %collective-permute-start.31 = (bf16[2,4,48,896]{3,2,1,0:T(8,128)(2,1)S(1)}, bf16[2,4,48,896]{3,2,1,0:T(8,128)(2,1)}, u32[]{:S(2)}, u32[]{:S(2)}) collective-permute-start(bf16[2,4,48,896]{3,2,1,0:T(8,128)(2,1)S(1)} %pad_maximum_fusion.2.refs_2_), channel_id=1, source_target_pairs={{0,32},{32,64},{64,96},{96,0},{1,33},{33,65},{65,97},{97,1},{2,34}... | collective-permute-start | bytes 2064392 | tf_op jit(solution)/shard_map/ppermute | solution.py:19
  173.1 15.1 %collective-permute-start.25 = (bf16[2,4,48,896]{3,2,1,0:T(8,128)(2,1)S(1)}, bf16[2,4,48,896]{3,2,1,0:T(8,128)(2,1)}, u32[]{:S(2)}, u32[]{:S(2)}) collective-permute-start(bf16[2,4,48,896]{3,2,1,0:T(8,128)(2,1)S(1)} %pad_maximum_fusion.refs_0_), channel_id=1, source_target_pairs={{0,8},{8,16},{16,24},{24,0},{1,9},{9,17},{17,25},{25,1},{2,10},{10... | collective-permute-start | bytes 2064392 | tf_op jit(solution)/shard_map/ppermute | solution.py:19
  176.7 18.2 %collective-permute-start.35 = (bf16[2,4,48,896]{3,2,1,0:T(8,128)(2,1)S(1)}, bf16[2,4,48,896]{3,2,1,0:T(8,128)(2,1)}, u32[]{:S(2)}, u32[]{:S(2)}) collective-permute-start(bf16[2,4,48,896]{3,2,1,0:T(8,128)(2,1)S(1)} %pad_maximum_fusion.3.refs_3_), channel_id=1, source_target_pairs={{0,96},{32,0},{64,32},{96,64},{1,97},{33,1},{65,33},{97,65},{2,98}... | collective-permute-start | bytes 2064392 | tf_op jit(solution)/shard_map/ppermute | solution.py:19
  176.8 24.9 %collective-permute-start.29 = (bf16[2,4,48,896]{3,2,1,0:T(8,128)(2,1)S(1)}, bf16[2,4,48,896]{3,2,1,0:T(8,128)(2,1)}, u32[]{:S(2)}, u32[]{:S(2)}) collective-permute-start(bf16[2,4,48,896]{3,2,1,0:T(8,128)(2,1)S(1)} %pad_maximum_fusion.1.refs_1_), channel_id=1, source_target_pairs={{0,24},{8,0},{16,8},{24,16},{1,25},{9,1},{17,9},{25,17},{2,26},{10... | collective-permute-start | bytes 2064392 | tf_op jit(solution)/shard_map/ppermute | solution.py:19
  179.9 22.3 %collective-permute-start.43 = (bf16[2,4,48,896]{3,2,1,0:T(8,128)(2,1)S(1)}, bf16[2,4,48,896]{3,2,1,0:T(8,128)(2,1)S(1)}, u32[]{:S(2)}, u32[]{:S(2)}) collective-permute-start(bf16[2,4,48,896]{3,2,1,0:T(8,128)(2,1)S(1)} %pad_maximum_fusion.2.refs_2_), channel_id=1, source_target_pairs={{0,96},{32,0},{64,32},{96,64},{1,97},{33,1},{65,33},{97,65},{2,98}... | collective-permute-start | bytes 2064392 | tf_op jit(solution)/shard_map/ppermute | solution.py:19
  188.2 14.3 %collective-permute-start.41 = (bf16[2,4,48,896]{3,2,1,0:T(8,128)(2,1)S(1)}, bf16[2,4,48,896]{3,2,1,0:T(8,128)(2,1)S(1)}, u32[]{:S(2)}, u32[]{:S(2)}) collective-permute-start(bf16[2,4,48,896]{3,2,1,0:T(8,128)(2,1)S(1)} %pad_maximum_fusion.refs_0_), channel_id=1, source_target_pairs={{0,24},{8,0},{16,8},{24,16},{1,25},{9,1},{17,9},{25,17},{2,26},{10... | collective-permute-start | bytes 2064392 | tf_op jit(solution)/shard_map/ppermute | solution.py:19
  188.3 17.2 %collective-permute-start.42 = (bf16[2,4,48,896]{3,2,1,0:T(8,128)(2,1)S(1)}, bf16[2,4,48,896]{3,2,1,0:T(8,128)(2,1)S(1)}, u32[]{:S(2)}, u32[]{:S(2)}) collective-permute-start(bf16[2,4,48,896]{3,2,1,0:T(8,128)(2,1)S(1)} %pad_maximum_fusion.3.refs_3_), channel_id=1, source_target_pairs={{0,32},{32,64},{64,96},{96,0},{1,33},{33,65},{65,97},{97,1},{2,34}... | collective-permute-start | bytes 2064392 | tf_op jit(solution)/shard_map/ppermute | solution.py:19
  201.7 23.3 %collective-permute-start.44 = (f32[384,640]{1,0:T(8,128)}, f32[384,640]{1,0:T(8,128)S(1)}, u32[]{:S(2)}, u32[]{:S(2)}) collective-permute-start(f32[384,640]{1,0:T(8,128)} %get-tuple-element.85), channel_id=1, source_target_pairs={{0,1},{1,0},{2,3},{3,2},{4,5},{5,4},{6,7},{7,6},{8,9},{9,8},{10,11... | collective-permute-start | bytes 2949128 | tf_op jit(solution)/shard_map/ppermute | solution.py:19
  202.1 24.0 %collective-permute-start.36 = (bf16[2,4,48,896]{3,2,1,0:T(8,128)(2,1)}, bf16[2,4,48,896]{3,2,1,0:T(8,128)(2,1)S(1)}, u32[]{:S(2)}, u32[]{:S(2)}) collective-permute-start(bf16[2,4,48,896]{3,2,1,0:T(8,128)(2,1)} %collective-permute-done.25.refs_0_), channel_id=1, source_target_pairs={{0,8},{8,16},{16,24},{24,0},{1,9},{9,17},{17,25},{25,1},{2,10},{10... | collective-permute-start | bytes 2064392 | tf_op jit(solution)/shard_map/ppermute | solution.py:19
  202.6 23.6 %collective-permute-start.37 = (bf16[2,4,48,896]{3,2,1,0:T(8,128)(2,1)}, bf16[2,4,48,896]{3,2,1,0:T(8,128)(2,1)}, u32[]{:S(2)}, u32[]{:S(2)}) collective-permute-start(bf16[2,4,48,896]{3,2,1,0:T(8,128)(2,1)} %collective-permute-done.29.refs_3_), channel_id=1, source_target_pairs={{0,24},{8,0},{16,8},{24,16},{1,25},{9,1},{17,9},{25,17},{2,26},{10... | collective-permute-start | bytes 2064392 | tf_op jit(solution)/shard_map/ppermute | solution.py:19
  205.4 20.8 %collective-permute-start.38 = (bf16[2,4,48,896]{3,2,1,0:T(8,128)(2,1)}, bf16[2,4,48,896]{3,2,1,0:T(8,128)(2,1)}, u32[]{:S(2)}, u32[]{:S(2)}) collective-permute-start(bf16[2,4,48,896]{3,2,1,0:T(8,128)(2,1)} %collective-permute-done.31.refs_4_), channel_id=1, source_target_pairs={{0,32},{32,64},{64,96},{96,0},{1,33},{33,65},{65,97},{97,1},{2,34}... | collective-permute-start | bytes 2064392 | tf_op jit(solution)/shard_map/ppermute | solution.py:19
  208.2 18.0 %collective-permute-start.39 = (bf16[2,4,48,896]{3,2,1,0:T(8,128)(2,1)}, bf16[2,4,48,896]{3,2,1,0:T(8,128)(2,1)}, u32[]{:S(2)}, u32[]{:S(2)}) collective-permute-start(bf16[2,4,48,896]{3,2,1,0:T(8,128)(2,1)} %collective-permute-done.35.refs_7_), channel_id=1, source_target_pairs={{0,96},{32,0},{64,32},{96,64},{1,97},{33,1},{65,33},{97,65},{2,98}... | collective-permute-start | bytes 2064392 | tf_op jit(solution)/shard_map/ppermute | solution.py:19
  (77 other events, 643.8 us)
